TPU v7x, 32 devices: a whole 2x2x4 slice. The times are simulated.
32 devices in a mesh: dp: 16 (over z, y, x), tensor: 2 (over core).
Axes of the slice: x: 2, y: 2, z: 4, core: 2. Of those that a mesh axis runs over, the one named last changes fastest.
Arguments:
- layer_input: bfloat16 [2048, 8192], P('dp', 'tensor'), may hold values from -6 to 6
- output_grad: bfloat16 [2048, 8192], P('dp', 'tensor'), may hold values from -0.06591797 to 0.06591797
- gate_pre: bfloat16 [2048, 28672], P('dp', 'tensor'), may hold values from -6 to 6
- up_pre: bfloat16 [2048, 28672], P('dp', 'tensor'), may hold values from -6 to 6
- hidden_grad: bfloat16 [2048, 28672], P('dp', 'tensor'), may hold values from -0.06591797 to 0.06591797
- tile_list: int32 [28, 3], P('tensor'), may hold values from 0 to 111, as said below
- tile_slots: int32 [28], P('tensor'), may hold values from 0 to 31, as said below
- first_codes: int32 [2, 32, 16384], P('tensor', 'dp'), may hold values from 0 to 255
- second_codes: int32 [2, 32, 16384], P('tensor', 'dp'), may hold values from 0 to 255
- first_absmax: float32 [2, 32, 8], P('tensor', 'dp'), may hold values from 0.05 to 0.5
- second_absmax: float32 [2, 32, 8], P('tensor', 'dp'), may hold values from 0.005 to 0.05
- signed_map: float32 [256], replicated, may hold values from -1 to 1
- unsigned_map: float32 [256], replicated, may hold values from 0.05 to 1
Outputs:
- update_tiles: bfloat16 [28, 128, 128], P('tensor')
- first_moment: float32 [2, 32, 16384], P('tensor', 'dp')
- second_moment: float32 [2, 32, 16384], P('tensor', 'dp')
Inputs may be any that keep to these rules, and one draw needn't show every extreme that they name: `tile_list`: within each group of 14 rows that belongs to one tensor index the triples are distinct; the first entry is below 64, the second below 112, the third is 0, 1 or 2. `tile_slots`: within each group of 14 entries the slots are distinct; a dp index owns slots s with s // 2 equal to it, so it holds at most 2 tiles of a group, and in every group some dp index holds exactly 2.
All inputs are finite; a program needn't handle non-finite values.
Results may differ from a plain program's by a relative error of at most 0.0085.
Values may be sent and summed in bfloat16 or wider, within the bound.
No kernel may reach another device: no remote copies, remote signals or barrier semaphores. Data moves between devices by JAX's collectives and lax.ppermute only.
A program may use at most 64 MiB of HBM per device.

v0:
```python
import jax
import jax.numpy as jnp
from jax import lax
from jax.sharding import PartitionSpec as P

CAP = 2
TB = 128
STEP = 10


BETA_FIRST = 0.9
BETA_SECOND = 0.99
EPSILON = 1e-08


def lookup(code_table, level_table):
    levels = jnp.arange(16, dtype=jnp.int32)
    high_part = jnp.right_shift(code_table, 4)
    low_part = jnp.bitwise_and(code_table, 15)
    low_onehot = (low_part[:, None, :] == levels[None, :, None]).astype(jnp.bfloat16)
    high_onehot = (high_part[:, None, :] == levels[None, :, None]).astype(jnp.float32)
    square = level_table.reshape(16, 16)
    first_part = square.astype(jnp.bfloat16)
    remain = square - first_part.astype(jnp.float32)
    second_part = remain.astype(jnp.bfloat16)
    third_part = (remain - second_part.astype(jnp.float32)).astype(jnp.bfloat16)
    total = jnp.zeros(code_table.shape, jnp.float32)
    for level_part in (third_part, second_part, first_part):
        by_high = jnp.einsum(
            "hl,cln->chn", level_part, low_onehot, preferred_element_type=jnp.float32
        )
        total = total + jnp.sum(by_high * high_onehot, axis=1)
    return total


def dequantize(code_table, level_table, scales):
    values = lookup(code_table, level_table)
    shaped = values.reshape(code_table.shape[0], scales.shape[1], -1) * scales[:, :, None]
    return shaped.reshape(code_table.shape)


def body(
    layer_input,
    output_grad,
    gate_pre,
    up_pre,
    hidden_grad,
    tile_list,
    tile_slots,
    first_codes,
    second_codes,
    first_absmax,
    second_absmax,
    signed_map,
    unsigned_map,
):
    whole_input, whole_grad = (
        lax.all_gather(layer_input, "tensor", axis=1, tiled=True),
        lax.all_gather(output_grad, "tensor", axis=1, tiled=True),
    )
    tokens_here = whole_input.shape[0]
    tile_count = tile_list.shape[0]
    gate_value = gate_pre.astype(jnp.float32)
    up_value = up_pre.astype(jnp.float32)
    grad_value = hidden_grad.astype(jnp.float32)
    sigmoid_gate = jax.nn.sigmoid(gate_value)
    silu_gate = gate_value * sigmoid_gate
    hidden = (silu_gate * up_value).astype(jnp.bfloat16)
    gate_grad = (
        grad_value * up_value * sigmoid_gate * (1.0 + gate_value * (1.0 - sigmoid_gate))
    ).astype(jnp.bfloat16)
    up_grad = (grad_value * silu_gate).astype(jnp.bfloat16)
    width_block = tile_list[:, 0]
    hidden_block = tile_list[:, 1]
    matrix_id = tile_list[:, 2][None, :, None]

    def blocks(source, block_index):
        return jnp.take(source.reshape(tokens_here, -1, TB), block_index, axis=1)

    left_side = jnp.where(
        matrix_id == 2, blocks(hidden, hidden_block), blocks(whole_input, width_block)
    )
    right_side = jnp.where(
        matrix_id == 0,
        blocks(gate_grad, hidden_block),
        jnp.where(matrix_id == 1, blocks(up_grad, hidden_block), blocks(whole_grad, width_block)),
    )
    partial_value = jnp.einsum(
        "tki,tkj->kij", left_side, right_side, preferred_element_type=jnp.float32
    )
    partial_value = partial_value.reshape(tile_count, -1)
    owner_count = lax.axis_size("dp")
    share = lax.psum_scatter(partial_value, "dp", scatter_dimension=1, tiled=True)
    every_slot = jnp.arange(owner_count * CAP, dtype=jnp.int32)
    all_match = (every_slot[:, None] == tile_slots[None, :]).astype(jnp.float32)
    by_slot = jnp.dot(all_match, share, precision=lax.Precision.HIGHEST)
    own_grad = lax.all_to_all(
        by_slot.astype(jnp.bfloat16), "dp", split_axis=0, concat_axis=1, tiled=True
    ).astype(by_slot.dtype)
    first_old = dequantize(first_codes[0], signed_map, first_absmax[0])
    second_old = dequantize(second_codes[0], unsigned_map, second_absmax[0])
    first_moment = BETA_FIRST * first_old + (1.0 - BETA_FIRST) * own_grad
    second_moment = BETA_SECOND * second_old + (1.0 - BETA_SECOND) * own_grad * own_grad
    first_hat = first_moment / (1.0 - BETA_FIRST**STEP)
    second_hat = second_moment / (1.0 - BETA_SECOND**STEP)
    slot_update = (first_hat / (jnp.sqrt(second_hat) + EPSILON)).astype(jnp.bfloat16)
    everyone = lax.all_gather(slot_update, "dp", axis=0, tiled=True)
    picked = jnp.take(everyone, tile_slots, axis=0)
    return (picked.reshape(tile_count, TB, TB), first_moment[None], second_moment[None])


def solution(mesh):
    in_specs = (
        P("dp", "tensor"),
        P("dp", "tensor"),
        P("dp", "tensor"),
        P("dp", "tensor"),
        P("dp", "tensor"),
        P("tensor", None),
        P("tensor"),
        P("tensor", "dp", None),
        P("tensor", "dp", None),
        P("tensor", "dp", None),
        P("tensor", "dp", None),
        P(),
        P(),
    )
    out_specs = (P("tensor", None, None), P("tensor", "dp", None), P("tensor", "dp", None))
    return jax.shard_map(body, mesh=mesh, in_specs=in_specs, out_specs=out_specs, check_vma=False)
```

profile of v0, /device:TPU:0, one launch (start us, length us, event | category | flops | bytes accessed | tf_op | source)
XLA Modules:
  0.0 240.2 jit_solution(1480161829235145956)
XLA Ops:
  7.2 2.3 copy.34
  9.6 1.3 copy.39
  11.0 6.0 %copy.31 = bf16[128,14336]{0,1:T(8,128)(2,1)} copy(bf16[128,14336]{1,0:T(8,128)(2,1)} %param.19) | data formatting | bytes 7340032 | tf_op args[2]
  17.1 6.2 %copy.32 = bf16[128,14336]{0,1:T(8,128)(2,1)} copy(bf16[128,14336]{1,0:T(8,128)(2,1)} %param.20) | data formatting | bytes 7340032 | tf_op args[3]
  23.3 6.1 %copy.36 = bf16[128,14336]{0,1:T(8,128)(2,1)} copy(bf16[128,14336]{1,0:T(8,128)(2,1)} %param.21) | data formatting | bytes 7340032 | tf_op args[4]
  29.5 10.1 %fusion.6 = (bf16[128,14336]{0,1:T(8,128)(2,1)}, bf16[128,14336]{0,1:T(8,128)(2,1)}, bf16[128,14336]{0,1:T(8,128)(2,1)}) fusion(bf16[128,14336]{0,1:T(8,128)(2,1)} %copy.32, bf16[128,14336]{0,1:T(8,128)(2,1)} %copy.31, bf16[128,14336]{0,1:T(8,128)(2,1)} %copy.36), kind=kLoop, calls=%fused_computation.24 | loop fusion | flops 33030144 | bytes 22020096 | tf_op jit(solution)/shard_map/convert_element_type | solution.py:68
  39.7 6.1 %copy.33 = bf16[128,112,128]{2,0,1:T(8,128)(2,1)} copy(bf16[128,112,128]{0,2,1:T(8,128)(2,1)} %bitcast.138) | data formatting | bytes 7340032 | tf_op jit(solution)/shard_map/reshape | solution.py:78
  45.8 6.1 %copy.37 = bf16[128,112,128]{2,0,1:T(8,128)(2,1)} copy(bf16[128,112,128]{0,2,1:T(8,128)(2,1)} %bitcast.137) | data formatting | bytes 7340032 | tf_op jit(solution)/shard_map/reshape | solution.py:78
  51.9 2.7 %gather_fusion.1 = bf16[14,128,128]{2,1,0:T(8,128)(2,1)S(1)} fusion(bf16[128,112,128]{2,0,1:T(8,128)(2,1)} %copy.33, s32[1024]{0:T(1024)S(1)} %get-tuple-element.24), kind=kCustom, calls=%fused_computation.clone | custom fusion | bytes 917560 | tf_op jit(solution)/shard_map/jit(_take)/gather | solution.py:78
  54.6 2.7 %gather_fusion.3 = bf16[14,128,128]{2,1,0:T(8,128)(2,1)S(1)} fusion(bf16[128,112,128]{2,0,1:T(8,128)(2,1)} %copy.37, s32[1024]{0:T(1024)S(1)} %get-tuple-element.24), kind=kCustom, calls=%fused_computation.2.clone | custom fusion | bytes 917560 | tf_op jit(solution)/shard_map/jit(_take)/gather | solution.py:78
  57.3 6.0 %copy.38 = bf16[128,112,128]{2,0,1:T(8,128)(2,1)} copy(bf16[128,112,128]{0,2,1:T(8,128)(2,1)} %bitcast.136) | data formatting | bytes 7340032 | tf_op jit(solution)/shard_map/reshape | solution.py:78
  63.3 2.7 %gather_fusion.4 = bf16[14,128,128]{2,1,0:T(8,128)(2,1)S(1)} fusion(bf16[128,112,128]{2,0,1:T(8,128)(2,1)} %copy.38, s32[1024]{0:T(1024)S(1)} %get-tuple-element.24), kind=kCustom, calls=%fused_computation.3.clone | custom fusion | bytes 917560 | tf_op jit(solution)/shard_map/jit(_take)/gather | solution.py:78
  66.2 1.5 fusion.16
  67.7 1.5 fusion.19
  69.3 3.2 %copy.35 = bf16[128,64,128]{2,0,1:T(8,128)(2,1)S(1)} copy(bf16[128,64,128]{0,2,1:T(8,128)(2,1)} %bitcast.142) | data formatting | bytes 4194304 | tf_op jit(solution)/shard_map/reshape | solution.py:78
  72.5 4.1 %copy.40 = bf16[128,64,128]{2,0,1:T(8,128)(2,1)} copy(bf16[128,64,128]{0,2,1:T(8,128)(2,1)} %bitcast.143) | data formatting | bytes 4194304 | tf_op jit(solution)/shard_map/reshape | solution.py:78
  76.6 1.4 gather_fusion.2
  78.0 2.2 gather_fusion.5
  80.2 1.5 fusion.28
  81.9 1.6 copy.44
  83.6 0.9 fusion.17
  84.5 0.9 fusion.15
  85.4 0.9 fusion.18
  86.5 77.7 %reduce-scatter.2.cloned.1.call-done = f32[14,1024]{1,0:T(8,128)} async-done(((f32[14,16384]{1,0:T(8,128)}), f32[14,1024]{1,0:T(8,128)}) %reduce-scatter.2.cloned.1.call-update) | async-done | bytes 57360 | tf_op jit(solution)/shard_map/reduce_scatter | solution.py:93
  164.2 1.0 convolution_convert_fusion
  165.9 3.6 %all-to-all-start = ((bf16[16,2,1024]{2,1,0:T(2,128)(2,1)}), bf16[16,2,1024]{2,1,0:T(2,128)(2,1)S(1)}, u32[]{:S(2)}, u32[]{:S(2)}) async-start(bf16[16,2,1024]{2,1,0:T(2,128)(2,1)} %all_to_all.10), calls=%async_computation.1 | async-start | bytes 131072 | tf_op jit(solution)/shard_map/all_to_all | solution.py:97
  169.8 0.9 fusion.20
  171.3 5.7 %all-to-all-done = bf16[16,2,1024]{2,1,0:T(2,128)(2,1)S(1)} async-done(((bf16[16,2,1024]{2,1,0:T(2,128)(2,1)}), bf16[16,2,1024]{2,1,0:T(2,128)(2,1)S(1)}, u32[]{:S(2)}, u32[]{:S(2)}) %all-to-all-start) | async-done | bytes 65568 | tf_op jit(solution)/shard_map/all_to_all | solution.py:97
  177.1 1.1 fusion.52
  178.2 1.0 fusion.47
  179.3 51.1 %all-gather.9.cloned.1.call-done = bf16[16,2,16384]{2,1,0:T(2,128)(2,1)} async-done(((bf16[1,2,16384]{2,1,0:T(2,128)(2,1)}), bf16[16,2,16384]{2,1,0:T(2,128)(2,1)}) %all-gather.9.cloned.1.call-update) | async-done | bytes 1048592 | tf_op jit(solution)/shard_map/all_gather | solution.py:107
  230.4 1.5 reshape.289
  (72 shorter events, 4.3 us)
Async XLA Ops:
  7.2 2.5 %copy-start = (bf16[128,4096]{1,0:T(8,128)(2,1)S(1)}, bf16[128,4096]{1,0:T(8,128)(2,1)}, u32[]{:S(2)}) copy-start(bf16[128,4096]{1,0:T(8,128)(2,1)} %param.18) | copy-start | bytes 3145732
  7.2 62.1 %all-gather.5.cloned.1.call-start = ((), (), s32[]{:S(2)}) async-start(), calls=%async_computation.2 | async-start | bytes 3145728 | tf_op jit(solution)/shard_map/all_gather | solution.py:58
  9.6 62.9 %all-gather.7.cloned.1.call-start = ((), (), s32[]{:S(2)}) async-start(), calls=%async_computation.3 | async-start | bytes 3145728 | tf_op jit(solution)/shard_map/all_gather | solution.py:59
  11.0 153.2 %reduce-scatter.2.cloned.1.call-start = ((), (), s32[]{:S(2)}) async-start(), calls=%async_computation.4 | async-start | bytes 1114112 | tf_op jit(solution)/shard_map/reduce_scatter | solution.py:93
  23.2 6.1 %copy-start.3 = (s32[1,2,16384]{2,1,0:T(2,128)S(1)}, s32[1,2,16384]{2,1,0:T(2,128)}, u32[]{:S(2)}) copy-start(s32[1,2,16384]{2,1,0:T(2,128)} %param.24) | copy-start | bytes 393220
  29.4 36.8 %copy-start.9 = (s32[2,16384]{1,0:T(2,128)}, s32[2,16384]{1,0:T(2,128)S(1)}, u32[]{:S(2)}) copy-start(s32[2,16384]{1,0:T(2,128)S(1)} %get-tuple-element.16) | copy-start | bytes 393220
  29.4 36.7 %copy-start.11 = (s32[2,16384]{1,0:T(2,128)}, s32[2,16384]{1,0:T(2,128)S(1)}, u32[]{:S(2)}) copy-start(s32[2,16384]{1,0:T(2,128)S(1)} %get-tuple-element.17) | copy-start | bytes 393220
  29.4 10.1 %copy-start.4 = (s32[1,2,16384]{2,1,0:T(2,128)S(1)}, s32[1,2,16384]{2,1,0:T(2,128)}, u32[]{:S(2)}) copy-start(s32[1,2,16384]{2,1,0:T(2,128)} %param.25) | copy-start | bytes 393220
  39.7 28.1 %copy-start.5 = (s32[2,16384]{1,0:T(2,128)}, s32[2,16384]{1,0:T(2,128)S(1)}, u32[]{:S(2)}) copy-start(s32[2,16384]{1,0:T(2,128)S(1)} %get-tuple-element.14) | copy-start | bytes 393220
  39.7 28.1 %copy-start.7 = (s32[2,16384]{1,0:T(2,128)}, s32[2,16384]{1,0:T(2,128)S(1)}, u32[]{:S(2)}) copy-start(s32[2,16384]{1,0:T(2,128)S(1)} %get-tuple-element.15) | copy-start | bytes 393220
  45.8 6.1 %copy-start.15 = (s32[14,3]{0,1:T(4,128)S(1)}, s32[14,3]{0,1:T(4,128)}, u32[]{:S(2)}) copy-start(s32[14,3]{0,1:T(4,128)} %param.22) | copy-start | bytes 508
  57.3 8.7 %copy-start.16 = (f32[256]{0:T(256)S(1)}, f32[256]{0:T(256)}, u32[]{:S(2)}) copy-start(f32[256]{0:T(256)} %param.28) | copy-start | bytes 3076
  57.3 8.8 %copy-start.17 = (f32[256]{0:T(256)S(1)}, f32[256]{0:T(256)}, u32[]{:S(2)}) copy-start(f32[256]{0:T(256)} %param.29) | copy-start | bytes 3076
  81.8 1.8 copy-start.10
  81.8 1.8 copy-start.12
  83.5 1.8 copy-start.6
  83.6 1.8 copy-start.8
  84.5 1.8 copy-start.18
  84.5 1.9 copy-start.13
  84.5 1.9 copy-start.14
  165.9 11.2 %copy-start.1 = (f32[2,16384]{1,0:T(2,128)S(1)}, f32[2,16384]{1,0:T(2,128)}, u32[]{:S(2)}) copy-start(f32[2,16384]{1,0:T(2,128)} %fusion.16) | copy-start | bytes 393220
  165.9 11.2 %copy-start.2 = (f32[2,16384]{1,0:T(2,128)S(1)}, f32[2,16384]{1,0:T(2,128)}, u32[]{:S(2)}) copy-start(f32[2,16384]{1,0:T(2,128)} %fusion.19) | copy-start | bytes 393220
  165.9 11.1 %all-to-all-start = ((bf16[16,2,1024]{2,1,0:T(2,128)(2,1)}), bf16[16,2,1024]{2,1,0:T(2,128)(2,1)S(1)}, u32[]{:S(2)}, u32[]{:S(2)}) async-start(bf16[16,2,1024]{2,1,0:T(2,128)(2,1)} %all_to_all.10), calls=%async_computation.1 | async-start | bytes 131072 | tf_op jit(solution)/shard_map/all_to_all | solution.py:97
  169.6 60.8 %all-gather.9.cloned.1.call-start = ((), (), s32[]{:S(2)}) async-start(), calls=%async_computation.5 | async-start | bytes 1114112 | tf_op jit(solution)/shard_map/all_gather | solution.py:107
Sparse Core Ops, SparseCore 0:
  9.7 13.2 all-gather.4
  24.6 11.7 all-gather.6
  83.6 80.5 reduce-scatter.1
  178.4 51.9 all-gather.8
where the time goes:
time: 242 us; the launch traced here: 240 us
  waiting for transfers between devices  135 us (56%)
  local copies, waits for them, and re-layouts  64.9 us (27%)
  between operations  14.2 us (6%)
  other arithmetic  13.4 us (6%)
  matrix products  9.2 us (4%)
  starting transfers between devices  3.98 us (2%)
    reduce_scatter x1, waiting for transfers between devices, body(): lax.psum_scatter(partial_value, 'dp', scatter_dimension=1, tiled=True)  77.7 us
    all_gather x1, waiting for transfers between devices, body(): everyone = lax.all_gather(slot_update, 'dp', axis=0, tiled=True)  51.1 us
    unnamed x51, local copies, waits for them, and re-layouts  25.6 us
    reshape x5, local copies, waits for them, and re-layouts, blocks(): return jnp.take(source.reshape(tokens_here, -1, TB), block_index, axis=1)  25.6 us
    gather x5, local copies, waits for them, and re-layouts, blocks(): return jnp.take(source.reshape(tokens_here, -1, TB), block_index, axis=1)  11.6 us
    convert_element_type x1, other arithmetic, body(): hidden = (silu_gate * up_value).astype(jnp.bfloat16)  10.1 us
    dot_general x6, matrix products, lookup(): jnp.einsum('hl,cln->chn', level_part, low_onehot, preferred_element_type=...  6.64 us
    all_to_all x1, waiting for transfers between devices, body(): lax.all_to_all(by_slot.astype(jnp.bfloat16), 'dp', split_axis=0, concat_a...  5.73 us
  transfers between devices with their start and end apart: 5, of which 3 were waited for; matrix products, arithmetic and copies ran while one was open for 28% of the time, Pallas kernels for 0%

commit v1 on v0

v1 whole, which is shorter than its diff:
```python
import jax
import jax.numpy as jnp
from jax import lax
from jax.experimental import pallas as pl
from jax.experimental.pallas import tpu as pltpu
from jax.sharding import PartitionSpec as P

CAP = 2
TB = 128
STEP = 10
INNER = 4
SHARE = TB // INNER
QUANT = 2048 // TB

BETA_FIRST = 0.9
BETA_SECOND = 0.99
EPSILON = 1e-08

VMEM = pl.BlockSpec(memory_space=pltpu.VMEM)
SMEM = pl.BlockSpec(memory_space=pltpu.SMEM)
ANY = pl.BlockSpec(memory_space=pl.ANY)
LIMIT = 48 * 1024 * 1024


def partner(array, axis, distance):
    count = lax.axis_size(axis)
    return lax.ppermute(array, axis, [(i, i ^ distance) for i in range(count)])


def states_kernel(first_codes, second_codes, first_scale, second_scale, first_map, second_map, first_old, second_old, message):
    copies = message.shape[0] // INNER
    tables = ((first_codes, first_scale, first_map, first_old), (second_codes, second_scale, second_map, second_old))
    for which, (codes, scale, levels, old) in enumerate(tables):
        low = jnp.broadcast_to(levels[0:1, :], (QUANT, TB))
        high = jnp.broadcast_to(levels[1:2, :], (QUANT, TB))
        for slot in range(CAP):
            for block in range(TB // QUANT):
                rows = pl.ds(block * QUANT, QUANT)
                code = codes[slot, rows, :]
                lane = jnp.bitwise_and(code, TB - 1)
                picked = jnp.where(
                    code >= TB,
                    jnp.take_along_axis(high, lane, axis=1),
                    jnp.take_along_axis(low, lane, axis=1),
                )
                value = picked * scale[slot, block]
                old[slot, rows, :] = value
                part, offset = divmod(block * QUANT, SHARE)
                sent = value.astype(jnp.bfloat16)
                for copy in range(copies):
                    message[copy * INNER + part, which * CAP + slot, pl.ds(offset, QUANT), :] = sent


def partial_kernel(pieces, *refs):
    tile_list, place = refs[0], refs[1]
    inputs = refs[2 : 2 + pieces]
    grads = refs[2 + pieces : 2 + 2 * pieces]
    gate_pre, up_pre, hidden_grad = refs[2 + 2 * pieces : 5 + 2 * pieces]
    outs = refs[5 + 2 * pieces : 5 + 2 * pieces + INNER]
    wide, gate, up, grad, part, sems = refs[5 + 2 * pieces + INNER :]
    tiles = wide.shape[0]
    per_piece = inputs[0].shape[1] // TB
    me, inner = place[0], place[1]

    def columns(block):
        return pl.ds(pl.multiple_of(block * TB, TB), TB)

    def begin(k, carry):
        width, hidden_block, matrix = tile_list[k, 0], tile_list[k, 1], tile_list[k, 2]
        for slot, (source, target) in enumerate(((gate_pre, gate), (up_pre, up), (hidden_grad, grad))):
            pltpu.make_async_copy(source.at[:, columns(hidden_block)], target.at[k], sems.at[k, slot]).start()
        distance = jnp.bitwise_xor(width // per_piece, me)
        local = lax.rem(width, per_piece)
        for piece in range(pieces):
            for down, source in ((False, inputs[piece]), (True, grads[piece])):

                @pl.when((distance == piece) & ((matrix == 2) == down))
                def _():
                    pltpu.make_async_copy(source.at[:, columns(local)], wide.at[k], sems.at[k, 3]).start()

        return carry

    lax.fori_loop(0, tiles, begin, 0)

    def work(k, carry):
        matrix = tile_list[k, 2]
        for slot, (source, target) in enumerate(((gate_pre, gate), (up_pre, up), (hidden_grad, grad), (inputs[0], wide))):
            pltpu.make_async_copy(source.at[:, pl.ds(0, TB)], target.at[k], sems.at[k, slot]).wait()
        gate_value = gate[k].astype(jnp.float32)
        up_value = up[k].astype(jnp.float32)
        grad_value = grad[k].astype(jnp.float32)
        sigmoid_gate = 1.0 / (1.0 + jnp.exp(-gate_value))
        silu_gate = gate_value * sigmoid_gate
        gate_side = grad_value * up_value * sigmoid_gate * (1.0 + gate_value * (1.0 - sigmoid_gate))
        hidden_side = jnp.where(
            matrix == 0, gate_side, jnp.where(matrix == 1, grad_value * silu_gate, silu_gate * up_value)
        ).astype(jnp.bfloat16)
        wide_side = wide[k]
        is_down = matrix == 2
        left = jnp.where(is_down, hidden_side, wide_side)
        right = jnp.where(is_down, wide_side, hidden_side)
        part[...] = lax.dot_general(left, right, (((0,), (0,)), ((), ())), preferred_element_type=jnp.float32)
        for distance in range(INNER):
            start = pl.multiple_of(jnp.bitwise_xor(inner, distance) * SHARE, SHARE)
            outs[distance][k] = part[pl.ds(start, SHARE), :].astype(outs[distance].dtype)
        return carry

    lax.fori_loop(0, tiles, work, 0)


def adam_kernel(outer, *refs):
    slots, place = refs[0], refs[1]
    sums = refs[2 : 2 + outer]
    states = refs[2 + outer]
    messages = refs[3 + outer : 3 + outer + INNER]
    total = refs[3 + outer + INNER]
    tiles = sums[0].shape[0]
    plane, inner = place[0], place[1]

    def step(k, carry):
        parts = [ref[k].astype(jnp.float32) for ref in sums]
        while len(parts) > 1:
            parts = [parts[i] + parts[i + 1] for i in range(0, len(parts), 2)]
        grad = parts[0]
        total[k] = grad
        owner, slot = slots[k] // CAP, lax.rem(slots[k], CAP)
        first_old = states[owner, slot].astype(jnp.float32)
        second_old = states[owner, CAP + slot].astype(jnp.float32)
        first = BETA_FIRST * first_old + (1.0 - BETA_FIRST) * grad
        second = BETA_SECOND * second_old + (1.0 - BETA_SECOND) * grad * grad
        first_hat = first / (1.0 - BETA_FIRST**STEP)
        second_hat = second / (1.0 - BETA_SECOND**STEP)
        update = (first_hat / (jnp.sqrt(second_hat) + EPSILON)).astype(jnp.bfloat16)
        for ref in messages:
            ref[k] = update
        return carry

    lax.fori_loop(0, tiles, step, 0)
    for distance in range(INNER):
        owner = plane * INNER + jnp.bitwise_xor(inner, distance)
        for slot in range(CAP):
            wanted = owner * CAP + slot

            def find(k, found):
                return jnp.where(slots[k] == wanted, k, found)

            found = lax.fori_loop(0, tiles, find, jnp.int32(-1))
            grad = total[jnp.maximum(found, 0)]
            grad = jnp.where(found >= 0, grad, jnp.zeros_like(grad))
            coarse = grad.astype(jnp.bfloat16)
            messages[distance][tiles + 2 * slot] = coarse
            messages[distance][tiles + 2 * slot + 1] = (grad - coarse.astype(jnp.float32)).astype(jnp.bfloat16)


def final_kernel(*refs):
    place = refs[0]
    messages = refs[1 : 1 + INNER]
    first_old, second_old, update_tiles, first_moment, second_moment = refs[1 + INNER :]
    tiles = update_tiles.shape[0]
    inner = place[1]
    for distance in range(INNER):
        rows = pl.ds(pl.multiple_of(jnp.bitwise_xor(inner, distance) * SHARE, SHARE), SHARE)
        update_tiles[:, rows, :] = messages[distance][pl.ds(0, tiles)]
        for slot in range(CAP):
            coarse = messages[distance][tiles + 2 * slot].astype(jnp.float32)
            grad = coarse + messages[distance][tiles + 2 * slot + 1].astype(jnp.float32)
            first_moment[slot, rows, :] = BETA_FIRST * first_old[slot, rows, :] + (1.0 - BETA_FIRST) * grad
            second_moment[slot, rows, :] = (
                BETA_SECOND * second_old[slot, rows, :] + (1.0 - BETA_SECOND) * grad * grad
            )


def body(
    layer_input,
    output_grad,
    gate_pre,
    up_pre,
    hidden_grad,
    tile_list,
    tile_slots,
    first_codes,
    second_codes,
    first_absmax,
    second_absmax,
    signed_map,
    unsigned_map,
):
    tiles = tile_list.shape[0]
    owners = lax.axis_size("dp")
    outer = owners // INNER
    pieces = lax.axis_size("tensor")
    dp_index = lax.axis_index("dp")
    params = pltpu.CompilerParams(vmem_limit_bytes=LIMIT)
    inner_place = jnp.stack([lax.axis_index("tensor"), lax.rem(dp_index, INNER)]).astype(jnp.int32)
    outer_place = jnp.stack([dp_index // INNER, lax.rem(dp_index, INNER)]).astype(jnp.int32)

    inputs = [layer_input] + [partner(layer_input, "tensor", r) for r in range(1, pieces)]
    grads = [output_grad] + [partner(output_grad, "tensor", r) for r in range(1, pieces)]

    shape = (CAP, TB, TB)
    first_old, second_old, state_message = pl.pallas_call(
        states_kernel,
        out_shape=(
            jax.ShapeDtypeStruct(shape, jnp.float32),
            jax.ShapeDtypeStruct(shape, jnp.float32),
            jax.ShapeDtypeStruct((owners, 2 * CAP, SHARE, TB), jnp.bfloat16),
        ),
        in_specs=[VMEM, VMEM, SMEM, SMEM, VMEM, VMEM],
        out_specs=(VMEM, VMEM, VMEM),
        compiler_params=params,
        name="states",
    )(
        first_codes.reshape(shape),
        second_codes.reshape(shape),
        first_absmax[0],
        second_absmax[0],
        signed_map.reshape(2, TB),
        unsigned_map.reshape(2, TB),
    )
    states = lax.all_to_all(state_message, "dp", 0, 0, tiled=True)

    share = (tiles, SHARE, TB)
    parts = pl.pallas_call(
        lambda *refs: partial_kernel(pieces, *refs),
        out_shape=(jax.ShapeDtypeStruct(share, jnp.float32),)
        + (jax.ShapeDtypeStruct(share, jnp.bfloat16),) * (INNER - 1),
        in_specs=[SMEM, SMEM] + [ANY] * (2 * pieces + 3),
        out_specs=(VMEM,) * INNER,
        scratch_shapes=[pltpu.VMEM((tiles, TB, TB), jnp.bfloat16)] * 4
        + [pltpu.VMEM((TB, TB), jnp.float32), pltpu.SemaphoreType.DMA((tiles, 4))],
        compiler_params=params,
        name="partials",
    )(tile_list, inner_place, *inputs, *grads, gate_pre, up_pre, hidden_grad)

    received = [partner(parts[r], "dp", r) for r in range(1, INNER)]
    summed = parts[0]
    for block in received:
        summed = summed + block.astype(jnp.float32)
    summed = summed.astype(jnp.bfloat16)
    sums = [summed] + [partner(summed, "dp", r * INNER) for r in range(1, outer)]

    message = (tiles + 2 * CAP, SHARE, TB)
    messages = pl.pallas_call(
        lambda *refs: adam_kernel(outer, *refs),
        out_shape=(jax.ShapeDtypeStruct(message, jnp.bfloat16),) * INNER,
        in_specs=[SMEM, SMEM] + [VMEM] * (outer + 1),
        out_specs=(VMEM,) * INNER,
        scratch_shapes=[pltpu.VMEM(share, jnp.float32)],
        compiler_params=params,
        name="adam",
    )(tile_slots, outer_place, *sums, states)
    messages = [messages[0]] + [partner(messages[r], "dp", r) for r in range(1, INNER)]

    update_tiles, first_moment, second_moment = pl.pallas_call(
        final_kernel,
        out_shape=(
            jax.ShapeDtypeStruct((tiles, TB, TB), jnp.bfloat16),
            jax.ShapeDtypeStruct(shape, jnp.float32),
            jax.ShapeDtypeStruct(shape, jnp.float32),
        ),
        in_specs=[SMEM] + [VMEM] * (INNER + 2),
        out_specs=(VMEM,) * 3,
        compiler_params=params,
        name="final",
    )(outer_place, *messages, first_old, second_old)
    return (
        update_tiles,
        first_moment.reshape(1, CAP, TB * TB),
        second_moment.reshape(1, CAP, TB * TB),
    )


def solution(mesh):
    in_specs = (
        P("dp", "tensor"),
        P("dp", "tensor"),
        P("dp", "tensor"),
        P("dp", "tensor"),
        P("dp", "tensor"),
        P("tensor", None),
        P("tensor"),
        P("tensor", "dp", None),
        P("tensor", "dp", None),
        P("tensor", "dp", None),
        P("tensor", "dp", None),
        P(),
        P(),
    )
    out_specs = (P("tensor", None, None), P("tensor", "dp", None), P("tensor", "dp", None))
    return jax.shard_map(body, mesh=mesh, in_specs=in_specs, out_specs=out_specs, check_vma=False)
```

time: 242 us -> 60.2 us (0.25)
  waiting for transfers between devices: 135 us -> 19.2 us
  local copies, waits for them, and re-layouts: 64.9 us -> 8.39 us
  starting transfers between devices: 3.98 us -> 20.5 us
  between operations: 14.2 us -> 0.7 us
  other arithmetic: 13.4 us -> 0.21 us
  Pallas kernels: 0 us -> 10.6 us
  matrix products: 9.2 us -> 0 us
    reduce_scatter x1 -> x0, waiting for transfers between devices: 77.7 us -> none  [body(): lax.psum_scatter(partial_value, 'dp', scatter_dimension=1, tiled=True)]
    all_gather x3 -> x0, waiting for transfers between devices: 51.1 us -> none  [the longest x1 51.1 us: body(): everyone = lax.all_gather(slot_update, 'dp', axis=0, tiled=True)]
    reshape x7 -> x3, local copies, waits for them, and re-layouts: 25.7 us -> 2.46 us  [the longest x1 0.98 us: body(): second_codes.reshape(shape)]
    unnamed x51 -> x15, local copies, waits for them, and re-layouts: 25.6 us -> 5.93 us
    ppermute x0 -> x11, waiting for transfers between devices: none -> 19.2 us  [partner(): return lax.ppermute(array, axis, [(i, i ^ distance) for i in range(count)])]
    gather x6 -> x0, local copies, waits for them, and re-layouts: 12.5 us -> none  [the longest x5 11.6 us: blocks(): return jnp.take(source.reshape(tokens_here, -1, TB), block_index, axis=1)]
    ppermute x0 -> x11, starting transfers between devices: none -> 12.2 us  [partner(): return lax.ppermute(array, axis, [(i, i ^ distance) for i in range(count)])]
    pallas_call x0 -> x4, Pallas kernels: none -> 10.6 us  [the longest x1 5.29 us: body(): pl.pallas_call(lambda *refs: partial_kernel(pieces, *refs), out_shape=(ja...]
  transfers between devices with their start and end apart: 5 -> 12, of which waited for: 3 -> 7; matrix products, arithmetic and copies ran while one was open for 28% -> 3% of each run, Pallas kernels for 0% -> 12%
where the time goes in v1:
time: 60.2 us; the launch traced here: 59.7 us
  starting transfers between devices  20.5 us (34%)
  waiting for transfers between devices  19.2 us (32%)
  Pallas kernels  10.6 us (18%)
  local copies, waits for them, and re-layouts  8.39 us (14%)
  between operations  0.7 us (1%)
    ppermute x11, waiting for transfers between devices, partner(): return lax.ppermute(array, axis, [(i, i ^ distance) for i in range(count)])  19.2 us
    ppermute x11, starting transfers between devices, partner(): return lax.ppermute(array, axis, [(i, i ^ distance) for i in range(count)])  12.2 us
    all_to_all x1, starting transfers between devices, body(): states = lax.all_to_all(state_message, 'dp', 0, 0, tiled=True)  8.29 us
    unnamed x15, local copies, waits for them, and re-layouts  5.93 us
    pallas_call x1, Pallas kernels, body(): pl.pallas_call(lambda *refs: partial_kernel(pieces, *refs), out_shape=(ja...  5.29 us
    pallas_call x1, Pallas kernels, body(): pl.pallas_call(lambda *refs: adam_kernel(outer, *refs), out_shape=(jax.Sh...  2.22 us
    pallas_call x1, Pallas kernels, body(): pl.pallas_call(states_kernel, out_shape=(jax.ShapeDtypeStruct(shape, jnp....  1.75 us
    pallas_call x1, Pallas kernels, body(): pl.pallas_call(final_kernel, out_shape=(jax.ShapeDtypeStruct((tiles, TB,...  1.37 us
  transfers between devices with their start and end apart: 12, of which 7 were waited for; matrix products, arithmetic and copies ran while one was open for 3% of the time, Pallas kernels for 12%

profile of v1, /device:TPU:0, one launch (start us, length us, event | category | flops | bytes accessed | tf_op | source)
XLA Modules:
  0.0 59.7 jit_solution(14257374444467075157)
XLA Ops:
  0.6 0.5 collective-permute-start
  1.2 1.0 %copy_bitcast_fusion = (s32[2,128,128]{2,1,0:T(8,128)S(1)}, s32[2,128,128]{2,1,0:T(8,128)S(1)}) fusion(s32[1,2,128,128]{3,1,2,0:T(2,128)} %bitcast.19, s32[1,2,128,128]{3,1,2,0:T(2,128)} %bitcast.20), kind=kLoop, calls=%fused_computation.1 | loop fusion | bytes 524288 | tf_op jit(solution)/shard_map/reshape | solution.py:214
  2.2 0.7 %copy-done.2 = f32[1,2,8]{2,1,0:T(2,128)S(1)} copy-done((f32[1,2,8]{2,1,0:T(2,128)S(1)}, f32[1,2,8]{2,1,0:T(2,128)}, u32[]{:S(2)}) %copy-start.2) | copy-done | bytes 88
  2.9 0.7 %copy-done.3 = f32[1,2,8]{2,1,0:T(2,128)S(1)} copy-done((f32[1,2,8]{2,1,0:T(2,128)S(1)}, f32[1,2,8]{2,1,0:T(2,128)}, u32[]{:S(2)}) %copy-start.3) | copy-done | bytes 88
  3.6 0.7 %copy-done.4 = f32[256]{0:T(256)S(1)} copy-done((f32[256]{0:T(256)S(1)}, f32[256]{0:T(256)}, u32[]{:S(2)}) %copy-start.4) | copy-done | bytes 1048
  4.3 0.7 %copy-done.5 = f32[256]{0:T(256)S(1)} copy-done((f32[256]{0:T(256)S(1)}, f32[256]{0:T(256)}, u32[]{:S(2)}) %copy-start.5) | copy-done | bytes 1048
  4.9 1.8 %states.1 = (f32[2,128,128]{2,1,0:T(8,128)S(1)}, f32[2,128,128]{2,1,0:T(8,128)S(1)}, bf16[16,4,32,128]{3,2,1,0:T(8,128)(2,1)}) custom-call(s32[2,128,128]{2,1,0:T(8,128)S(1)} %get-tuple-element.32.first_codes, s32[2,128,128]{2,1,0:T(8,128)S(1)} %get-tuple-element.31.second_codes, f32[2,8]{1,0:T(2,128)S(1)} %bitcast.15, f32[2,8]{1,0:T(2,128)S(1)} %bitcast.16, ...), custom_call_target="tpu_custom_call" | custom-call | tf_op jit(solution)/shard_map/states/pallas_call | solution.py:201
  6.7 8.3 %all-to-all-start = ((bf16[16,4,32,128]{3,2,1,0:T(8,128)(2,1)}), bf16[16,4,32,128]{3,2,1,0:T(8,128)(2,1)S(1)}, u32[]{:S(2)}, u32[]{:S(2)}) async-start(bf16[16,4,32,128]{3,2,1,0:T(8,128)(2,1)} %get-tuple-element.21), calls=%async_computation | async-start | bytes 1048576 | tf_op jit(solution)/shard_map/all_to_all | solution.py:220
  15.0 0.8 %copy.16.refs_0_ = s32[14,3]{1,0:T(8,128)S(1)} copy(s32[14,3]{0,1:T(4,128)} %param.18) | data formatting | bytes 336 | tf_op args[5]
  15.9 1.2 %copy-done = bf16[128,4096]{1,0:T(8,128)(2,1)S(1)} copy-done((bf16[128,4096]{1,0:T(8,128)(2,1)S(1)}, bf16[128,4096]{1,0:T(8,128)(2,1)}, u32[]{:S(2)}) %copy-start) | copy-done | bytes 1048600
  17.1 1.2 %copy-done.1 = bf16[128,4096]{1,0:T(8,128)(2,1)S(1)} copy-done((bf16[128,4096]{1,0:T(8,128)(2,1)S(1)}, bf16[128,4096]{1,0:T(8,128)(2,1)}, u32[]{:S(2)}) %copy-start.1) | copy-done | bytes 1048600
  18.3 5.3 %partials.1 = (f32[14,32,128]{2,1,0:T(8,128)S(1)}, bf16[14,32,128]{2,1,0:T(8,128)(2,1)S(1)}, bf16[14,32,128]{2,1,0:T(8,128)(2,1)S(1)}, bf16[14,32,128]{2,1,0:T(8,128)(2,1)S(1)}) custom-call(s32[14,3]{1,0:T(8,128)S(1)} %copy.16.refs_0_, s32[2]{0:T(128)S(1)} %pad_add_fusion.1.refs_1_, bf16[128,4096]{1,0:T(8,128)(2,1)S(1)} %copy-done, ...), custom_call_target="tpu_custom_call" | custom-call | tf_op jit(solution)/shard_map/partials/pallas_call | solution.py:223
  23.6 2.9 %collective-permute-start.4 = (bf16[14,32,128]{2,1,0:T(8,128)(2,1)S(1)}, bf16[14,32,128]{2,1,0:T(8,128)(2,1)S(1)}, u32[]{:S(2)}, u32[]{:S(2)}) collective-permute-start(bf16[14,32,128]{2,1,0:T(8,128)(2,1)S(1)} %get-tuple-element.20), channel_id=1, source_target_pairs={{0,6},{2,4},{4,2},{6,0},{8,14},{10,12},{12,10},{14,8},{16,22},{18,... | collective-permute-start | bytes 344072 | tf_op jit(solution)/shard_map/ppermute | solution.py:27
  26.5 0.5 collective-permute-start.3
  27.1 0.1 collective-permute-start.2
  27.2 3.9 %collective-permute-done.4 = bf16[14,32,128]{2,1,0:T(8,128)(2,1)S(1)} collective-permute-done((bf16[14,32,128]{2,1,0:T(8,128)(2,1)S(1)}, bf16[14,32,128]{2,1,0:T(8,128)(2,1)S(1)}, u32[]{:S(2)}, u32[]{:S(2)}) %collective-permute-start.4) | collective-permute-done | bytes 114720 | tf_op jit(solution)/shard_map/ppermute | solution.py:27
  31.1 1.8 %collective-permute-done.3 = bf16[14,32,128]{2,1,0:T(8,128)(2,1)S(1)} collective-permute-done((bf16[14,32,128]{2,1,0:T(8,128)(2,1)S(1)}, bf16[14,32,128]{2,1,0:T(8,128)(2,1)S(1)}, u32[]{:S(2)}, u32[]{:S(2)}) %collective-permute-start.3) | collective-permute-done | bytes 114720 | tf_op jit(solution)/shard_map/ppermute | solution.py:27
  32.9 0.1 collective-permute-done.2
  33.1 2.1 %collective-permute-start.5 = (bf16[14,32,128]{2,1,0:T(8,128)(2,1)S(1)}, bf16[14,32,128]{2,1,0:T(8,128)(2,1)S(1)}, u32[]{:S(2)}, u32[]{:S(2)}) collective-permute-start(bf16[14,32,128]{2,1,0:T(8,128)(2,1)S(1)} %add_convert_fusion.refs_2_), channel_id=1, source_target_pairs={{0,8},{2,10},{4,12},{6,14},{8,0},{10,2},{12,4},{14,6},{16,24},{18,... | collective-permute-start | bytes 344072 | tf_op jit(solution)/shard_map/ppermute | solution.py:27
  35.1 2.0 %collective-permute-start.6 = (bf16[14,32,128]{2,1,0:T(8,128)(2,1)S(1)}, bf16[14,32,128]{2,1,0:T(8,128)(2,1)S(1)}, u32[]{:S(2)}, u32[]{:S(2)}) collective-permute-start(bf16[14,32,128]{2,1,0:T(8,128)(2,1)S(1)} %add_convert_fusion.refs_2_), channel_id=1, source_target_pairs={{0,16},{2,18},{4,20},{6,22},{8,24},{10,26},{12,28},{14,30},{16,0},... | collective-permute-start | bytes 344072 | tf_op jit(solution)/shard_map/ppermute | solution.py:27
  37.1 0.5 collective-permute-start.7
  37.6 1.7 %collective-permute-done.5.refs_3_ = bf16[14,32,128]{2,1,0:T(8,128)(2,1)S(1)} collective-permute-done((bf16[14,32,128]{2,1,0:T(8,128)(2,1)S(1)}, bf16[14,32,128]{2,1,0:T(8,128)(2,1)S(1)}, u32[]{:S(2)}, u32[]{:S(2)}) %collective-permute-start.5) | collective-permute-done | bytes 114720 | tf_op jit(solution)/shard_map/ppermute | solution.py:27
  39.3 7.5 %collective-permute-done.6.refs_4_ = bf16[14,32,128]{2,1,0:T(8,128)(2,1)S(1)} collective-permute-done((bf16[14,32,128]{2,1,0:T(8,128)(2,1)S(1)}, bf16[14,32,128]{2,1,0:T(8,128)(2,1)S(1)}, u32[]{:S(2)}, u32[]{:S(2)}) %collective-permute-start.6) | collective-permute-done | bytes 114720 | tf_op jit(solution)/shard_map/ppermute | solution.py:27
  46.9 2.2 %adam.1 = (bf16[18,32,128]{2,1,0:T(8,128)(2,1)S(1)}, bf16[18,32,128]{2,1,0:T(8,128)(2,1)S(1)}, bf16[18,32,128]{2,1,0:T(8,128)(2,1)S(1)}, bf16[18,32,128]{2,1,0:T(8,128)(2,1)S(1)}) custom-call(s32[14]{0:T(128)S(1)} %copy-done.6, s32[2]{0:T(128)S(1)} %pad_add_fusion.refs_1_.refs_0_, bf16[14,32,128]{2,1,0:T(8,128)(2,1)S(1)} %add_convert_fusion.refs_2_, ...), custom_call_target="tpu_custom_call" | custom-call | tf_op jit(solution)/shard_map/adam/pallas_call | solution.py:243
  49.1 1.0 %collective-permute-start.8 = (bf16[18,32,128]{2,1,0:T(8,128)(2,1)S(1)}, bf16[18,32,128]{2,1,0:T(8,128)(2,1)S(1)}, u32[]{:S(2)}, u32[]{:S(2)}) collective-permute-start(bf16[18,32,128]{2,1,0:T(8,128)(2,1)S(1)} %get-tuple-element.23), channel_id=1, source_target_pairs={{0,2},{2,0},{4,6},{6,4},{8,10},{10,8},{12,14},{14,12},{16,18},{18,... | collective-permute-start | bytes 442376 | tf_op jit(solution)/shard_map/ppermute | solution.py:27
  50.1 0.4 collective-permute-start.9
  50.5 2.2 %collective-permute-start.10 = (bf16[18,32,128]{2,1,0:T(8,128)(2,1)S(1)}, bf16[18,32,128]{2,1,0:T(8,128)(2,1)S(1)}, u32[]{:S(2)}, u32[]{:S(2)}) collective-permute-start(bf16[18,32,128]{2,1,0:T(8,128)(2,1)S(1)} %get-tuple-element.25), channel_id=1, source_target_pairs={{0,6},{2,4},{4,2},{6,0},{8,14},{10,12},{12,10},{14,8},{16,22},{18,... | collective-permute-start | bytes 442376 | tf_op jit(solution)/shard_map/ppermute | solution.py:27
  52.7 1.8 %collective-permute-done.8.refs_2_ = bf16[18,32,128]{2,1,0:T(8,128)(2,1)S(1)} collective-permute-done((bf16[18,32,128]{2,1,0:T(8,128)(2,1)S(1)}, bf16[18,32,128]{2,1,0:T(8,128)(2,1)S(1)}, u32[]{:S(2)}, u32[]{:S(2)}) %collective-permute-start.8) | collective-permute-done | bytes 147488 | tf_op jit(solution)/shard_map/ppermute | solution.py:27
  54.5 2.3 %collective-permute-done.9.refs_3_ = bf16[18,32,128]{2,1,0:T(8,128)(2,1)S(1)} collective-permute-done((bf16[18,32,128]{2,1,0:T(8,128)(2,1)S(1)}, bf16[18,32,128]{2,1,0:T(8,128)(2,1)S(1)}, u32[]{:S(2)}, u32[]{:S(2)}) %collective-permute-start.9) | collective-permute-done | bytes 147488 | tf_op jit(solution)/shard_map/ppermute | solution.py:27
  56.8 1.4 %final.1 = (bf16[14,128,128]{2,1,0:T(8,128)(2,1)}, f32[2,128,128]{2,1,0:T(8,128)S(1)}, f32[2,128,128]{2,1,0:T(8,128)S(1)}) custom-call(s32[2]{0:T(128)S(1)} %pad_add_fusion.refs_1_.refs_0_, bf16[18,32,128]{2,1,0:T(8,128)(2,1)S(1)} %get-tuple-element.22.refs_1_, bf16[18,32,128]{2,1,0:T(8,128)(2,1)S(1)} %collective-permute-done.8.refs_2_, ...), custom_call_target="tpu_custom_call" | custom-call | tf_op jit(solution)/shard_map/final/pallas_call | solution.py:254
  58.2 0.7 %reshape.28 = f32[1,2,16384]{2,1,0:T(2,128)} reshape(f32[2,128,128]{2,1,0:T(8,128)S(1)} %get-tuple-element.29) | data formatting | bytes 262144 | tf_op jit(solution)/shard_map/reshape | solution.py:268
  58.9 0.7 %reshape.29 = f32[1,2,16384]{2,1,0:T(2,128)} reshape(f32[2,128,128]{2,1,0:T(8,128)S(1)} %get-tuple-element.30) | data formatting | bytes 262144 | tf_op jit(solution)/shard_map/reshape | solution.py:269
  (17 shorter events, 0.3 us)
Async XLA Ops:
  0.6 15.2 %collective-permute-start = (bf16[128,4096]{1,0:T(8,128)(2,1)}, bf16[128,4096]{1,0:T(8,128)(2,1)S(1)}, u32[]{:S(2)}, u32[]{:S(2)}) collective-permute-start(bf16[128,4096]{1,0:T(8,128)(2,1)} %refs_2_.1), channel_id=1, source_target_pairs={{0,1},{1,0},{2,3},{3,2},{4,5},{5,4},{6,7},{7,6},{8,9},{9,8},{10,11... | collective-permute-start | bytes 3145736 | tf_op jit(solution)/shard_map/ppermute | solution.py:27
  1.1 14.7 %collective-permute-start.1 = (bf16[128,4096]{1,0:T(8,128)(2,1)}, bf16[128,4096]{1,0:T(8,128)(2,1)S(1)}, u32[]{:S(2)}, u32[]{:S(2)}) collective-permute-start(bf16[128,4096]{1,0:T(8,128)(2,1)} %refs_4_.1), channel_id=1, source_target_pairs={{0,1},{1,0},{2,3},{3,2},{4,5},{5,4},{6,7},{7,6},{8,9},{9,8},{10,11... | collective-permute-start | bytes 3145736 | tf_op jit(solution)/shard_map/ppermute | solution.py:27
  2.2 0.7 %copy-start.2 = (f32[1,2,8]{2,1,0:T(2,128)S(1)}, f32[1,2,8]{2,1,0:T(2,128)}, u32[]{:S(2)}) copy-start(f32[1,2,8]{2,1,0:T(2,128)} %param.22) | copy-start | bytes 196
  2.9 0.7 %copy-start.3 = (f32[1,2,8]{2,1,0:T(2,128)S(1)}, f32[1,2,8]{2,1,0:T(2,128)}, u32[]{:S(2)}) copy-start(f32[1,2,8]{2,1,0:T(2,128)} %param.23) | copy-start | bytes 196
  3.6 0.7 %copy-start.4 = (f32[256]{0:T(256)S(1)}, f32[256]{0:T(256)}, u32[]{:S(2)}) copy-start(f32[256]{0:T(256)} %param.24) | copy-start | bytes 3076
  4.3 0.7 %copy-start.5 = (f32[256]{0:T(256)S(1)}, f32[256]{0:T(256)}, u32[]{:S(2)}) copy-start(f32[256]{0:T(256)} %param.25) | copy-start | bytes 3076
  6.7 30.9 %all-to-all-start = ((bf16[16,4,32,128]{3,2,1,0:T(8,128)(2,1)}), bf16[16,4,32,128]{3,2,1,0:T(8,128)(2,1)S(1)}, u32[]{:S(2)}, u32[]{:S(2)}) async-start(bf16[16,4,32,128]{3,2,1,0:T(8,128)(2,1)} %get-tuple-element.21), calls=%async_computation | async-start | bytes 1048576 | tf_op jit(solution)/shard_map/all_to_all | solution.py:220
  15.8 31.1 %copy-start.6 = (s32[14]{0:T(128)S(1)}, s32[14]{0:T(128)}, u32[]{:S(2)}) copy-start(s32[14]{0:T(128)} %refs_0_.2) | copy-start | bytes 172
  15.9 1.2 %copy-start = (bf16[128,4096]{1,0:T(8,128)(2,1)S(1)}, bf16[128,4096]{1,0:T(8,128)(2,1)}, u32[]{:S(2)}) copy-start(bf16[128,4096]{1,0:T(8,128)(2,1)} %refs_2_.1) | copy-start | bytes 3145732
  17.1 1.2 %copy-start.1 = (bf16[128,4096]{1,0:T(8,128)(2,1)S(1)}, bf16[128,4096]{1,0:T(8,128)(2,1)}, u32[]{:S(2)}) copy-start(bf16[128,4096]{1,0:T(8,128)(2,1)} %refs_4_.1) | copy-start | bytes 3145732
  23.6 7.5 %collective-permute-start.4 = (bf16[14,32,128]{2,1,0:T(8,128)(2,1)S(1)}, bf16[14,32,128]{2,1,0:T(8,128)(2,1)S(1)}, u32[]{:S(2)}, u32[]{:S(2)}) collective-permute-start(bf16[14,32,128]{2,1,0:T(8,128)(2,1)S(1)} %get-tuple-element.20), channel_id=1, source_target_pairs={{0,6},{2,4},{4,2},{6,0},{8,14},{10,12},{12,10},{14,8},{16,22},{18,... | collective-permute-start | bytes 344072 | tf_op jit(solution)/shard_map/ppermute | solution.py:27
  26.5 6.4 %collective-permute-start.3 = (bf16[14,32,128]{2,1,0:T(8,128)(2,1)S(1)}, bf16[14,32,128]{2,1,0:T(8,128)(2,1)S(1)}, u32[]{:S(2)}, u32[]{:S(2)}) collective-permute-start(bf16[14,32,128]{2,1,0:T(8,128)(2,1)S(1)} %get-tuple-element.19), channel_id=1, source_target_pairs={{0,4},{2,6},{4,0},{6,2},{8,12},{10,14},{12,8},{14,10},{16,20},{18,... | collective-permute-start | bytes 344072 | tf_op jit(solution)/shard_map/ppermute | solution.py:27
  27.1 5.9 %collective-permute-start.2 = (bf16[14,32,128]{2,1,0:T(8,128)(2,1)S(1)}, bf16[14,32,128]{2,1,0:T(8,128)(2,1)S(1)}, u32[]{:S(2)}, u32[]{:S(2)}) collective-permute-start(bf16[14,32,128]{2,1,0:T(8,128)(2,1)S(1)} %get-tuple-element.18), channel_id=1, source_target_pairs={{0,2},{2,0},{4,6},{6,4},{8,10},{10,8},{12,14},{14,12},{16,18},{18,... | collective-permute-start | bytes 344072 | tf_op jit(solution)/shard_map/ppermute | solution.py:27
  33.1 6.3 %collective-permute-start.5 = (bf16[14,32,128]{2,1,0:T(8,128)(2,1)S(1)}, bf16[14,32,128]{2,1,0:T(8,128)(2,1)S(1)}, u32[]{:S(2)}, u32[]{:S(2)}) collective-permute-start(bf16[14,32,128]{2,1,0:T(8,128)(2,1)S(1)} %add_convert_fusion.refs_2_), channel_id=1, source_target_pairs={{0,8},{2,10},{4,12},{6,14},{8,0},{10,2},{12,4},{14,6},{16,24},{18,... | collective-permute-start | bytes 344072 | tf_op jit(solution)/shard_map/ppermute | solution.py:27
  35.1 11.7 %collective-permute-start.6 = (bf16[14,32,128]{2,1,0:T(8,128)(2,1)S(1)}, bf16[14,32,128]{2,1,0:T(8,128)(2,1)S(1)}, u32[]{:S(2)}, u32[]{:S(2)}) collective-permute-start(bf16[14,32,128]{2,1,0:T(8,128)(2,1)S(1)} %add_convert_fusion.refs_2_), channel_id=1, source_target_pairs={{0,16},{2,18},{4,20},{6,22},{8,24},{10,26},{12,28},{14,30},{16,0},... | collective-permute-start | bytes 344072 | tf_op jit(solution)/shard_map/ppermute | solution.py:27
  37.1 9.8 %collective-permute-start.7 = (bf16[14,32,128]{2,1,0:T(8,128)(2,1)S(1)}, bf16[14,32,128]{2,1,0:T(8,128)(2,1)S(1)}, u32[]{:S(2)}, u32[]{:S(2)}) collective-permute-start(bf16[14,32,128]{2,1,0:T(8,128)(2,1)S(1)} %add_convert_fusion.refs_2_), channel_id=1, source_target_pairs={{0,24},{2,26},{4,28},{6,30},{8,16},{10,18},{12,20},{14,22},{16,8},... | collective-permute-start | bytes 344072 | tf_op jit(solution)/shard_map/ppermute | solution.py:27
  49.1 5.4 %collective-permute-start.8 = (bf16[18,32,128]{2,1,0:T(8,128)(2,1)S(1)}, bf16[18,32,128]{2,1,0:T(8,128)(2,1)S(1)}, u32[]{:S(2)}, u32[]{:S(2)}) collective-permute-start(bf16[18,32,128]{2,1,0:T(8,128)(2,1)S(1)} %get-tuple-element.23), channel_id=1, source_target_pairs={{0,2},{2,0},{4,6},{6,4},{8,10},{10,8},{12,14},{14,12},{16,18},{18,... | collective-permute-start | bytes 442376 | tf_op jit(solution)/shard_map/ppermute | solution.py:27
  50.1 6.7 %collective-permute-start.9 = (bf16[18,32,128]{2,1,0:T(8,128)(2,1)S(1)}, bf16[18,32,128]{2,1,0:T(8,128)(2,1)S(1)}, u32[]{:S(2)}, u32[]{:S(2)}) collective-permute-start(bf16[18,32,128]{2,1,0:T(8,128)(2,1)S(1)} %get-tuple-element.24), channel_id=1, source_target_pairs={{0,4},{2,6},{4,0},{6,2},{8,12},{10,14},{12,8},{14,10},{16,20},{18,... | collective-permute-start | bytes 442376 | tf_op jit(solution)/shard_map/ppermute | solution.py:27
  50.5 6.3 %collective-permute-start.10 = (bf16[18,32,128]{2,1,0:T(8,128)(2,1)S(1)}, bf16[18,32,128]{2,1,0:T(8,128)(2,1)S(1)}, u32[]{:S(2)}, u32[]{:S(2)}) collective-permute-start(bf16[18,32,128]{2,1,0:T(8,128)(2,1)S(1)} %get-tuple-element.25), channel_id=1, source_target_pairs={{0,6},{2,4},{4,2},{6,0},{8,14},{10,12},{12,10},{14,8},{16,22},{18,... | collective-permute-start | bytes 442376 | tf_op jit(solution)/shard_map/ppermute | solution.py:27

commit v2 on v0

v2 whole, which is shorter than its diff:
```python
import jax
import jax.numpy as jnp
from jax import lax
from jax.experimental import pallas as pl
from jax.experimental.pallas import tpu as pltpu
from jax.sharding import PartitionSpec as P

CAP = 2
TB = 128
STEP = 10
INNER = 8
SHARE = TB // INNER
QUANT = 2048 // TB

BETA_FIRST = 0.9
BETA_SECOND = 0.99
EPSILON = 1e-08

VMEM = pl.BlockSpec(memory_space=pltpu.VMEM)
SMEM = pl.BlockSpec(memory_space=pltpu.SMEM)
HBM = pl.BlockSpec(memory_space=pltpu.HBM)
ROWS = CAP * TB
FIELDS = 2 * CAP
PLANE = 4
HALVES = INNER // PLANE
COST = pl.CostEstimate(flops=10**11, bytes_accessed=10**8, transcendentals=0)
PARAMS = pltpu.CompilerParams(vmem_limit_bytes=32 * 1024 * 1024)
WIDE_PARAMS = pltpu.CompilerParams(vmem_limit_bytes=55 * 1024 * 1024)


def partner(array, axis, distance):
    count = lax.axis_size(axis)
    return lax.ppermute(array, axis, [(i, i ^ distance) for i in range(count)])


def exchange(array):
    count = lax.axis_size("dp")
    groups = [[start + i for i in range(INNER)] for start in range(0, count, INNER)]
    return lax.all_to_all(array, "dp", 0, 0, tiled=True, axis_index_groups=groups)


def interleave(array):
    return array.reshape(CAP, TB, TB).transpose(1, 0, 2).reshape(ROWS, TB)


def separate(array):
    return array.reshape(TB, CAP, TB).transpose(1, 0, 2).reshape(1, CAP, TB * TB)


def grouped(tiles):
    return 7 if tiles % 7 == 0 else 1


def columns(block):
    return pl.ds(pl.multiple_of(block * TB, TB), TB)


def prepare_kernel(*refs):
    tile_list, layer_input, output_grad, *sources = refs[:6]
    tables = refs[6:12]
    side, wide, first_old, second_old, message = refs[12:17]
    targets, held, sems, table_sems = refs[17:20], refs[20:26], refs[26], refs[27]
    tiles = side.shape[0]
    per_piece = layer_input.shape[1] // TB
    owners = message.shape[0]

    copies = [
        pltpu.make_async_copy(source, target, table_sems.at[i]) for i, (source, target) in enumerate(zip(tables, held))
    ]
    for copy in copies:
        copy.start()

    def begin(k, carry):
        for slot, (source, target) in enumerate(zip(sources, targets)):
            pltpu.make_async_copy(source.at[:, columns(tile_list[1, k])], target.at[k], sems.at[k, slot]).start()
        local = columns(lax.rem(tile_list[0, k], per_piece))
        for is_down, source in ((False, layer_input), (True, output_grad)):

            @pl.when((tile_list[2, k] == 2) == is_down)
            def _():
                pltpu.make_async_copy(source.at[:, local], wide.at[k], sems.at[k, 3]).start()

        return carry

    lax.fori_loop(0, tiles, begin, 0)

    for copy in copies:
        copy.wait()
    size = QUANT * CAP
    odd = lax.rem(lax.broadcasted_iota(jnp.int32, (size, TB), 0), CAP) == 1
    for which, old in enumerate((first_old, second_old)):
        codes, scale, levels = held[which::2]
        low = jnp.broadcast_to(levels[0:1, :], (size, TB))
        high = jnp.broadcast_to(levels[1:2, :], (size, TB))
        for block in range(TB // QUANT):
            rows = pl.ds(block * size, size)
            code = codes[rows, :]
            lane = jnp.bitwise_and(code, TB - 1)
            picked = jnp.where(
                code >= TB,
                jnp.take_along_axis(high, lane, axis=1),
                jnp.take_along_axis(low, lane, axis=1),
            )
            old[rows, :] = picked * jnp.where(odd, scale[1, block], scale[0, block])
        for part in range(INNER):
            for slot in range(CAP):
                sent = old[pl.ds(part * SHARE * CAP + slot, SHARE, stride=CAP), :].astype(jnp.bfloat16)
                for owner in range(part, owners, INNER):
                    message[owner, which * CAP + slot] = sent

    group = grouped(tiles)

    def work(step, carry):
        for k in [step * group + i for i in range(group)]:
            for slot, (source, target) in enumerate(zip((*sources, layer_input), (*targets, wide))):
                pltpu.make_async_copy(source.at[:, pl.ds(0, TB)], target.at[k], sems.at[k, slot]).wait()
        gate, up, grad = targets
        for k in [step * group + i for i in range(group)]:
            matrix = tile_list[2, k]
            gate_value = gate[k].astype(jnp.float32)
            up_value = up[k].astype(jnp.float32)
            grad_value = grad[k].astype(jnp.float32)
            sigmoid_gate = 1.0 / (1.0 + jnp.exp(-gate_value))
            silu_gate = gate_value * sigmoid_gate
            gate_side = grad_value * up_value * sigmoid_gate * (1.0 + gate_value * (1.0 - sigmoid_gate))
            side[k] = jnp.where(
                matrix == 0, gate_side, jnp.where(matrix == 1, grad_value * silu_gate, silu_gate * up_value)
            ).astype(jnp.bfloat16)
        return carry

    lax.fori_loop(0, tiles // group, work, 0)


def partial_kernel(pieces, *refs):
    tile_list, side, wide = refs[:3]
    inputs = refs[3 : 2 + pieces]
    grads = refs[2 + pieces : 1 + 2 * pieces]
    messages = refs[1 + 2 * pieces : 1 + 2 * pieces + PLANE]
    part = refs[-1]
    tiles = side.shape[0]
    per_piece = inputs[0].shape[1] // TB if inputs else 1
    me = lax.axis_index("tensor")
    inner = lax.rem(lax.axis_index("dp"), PLANE)
    group = grouped(tiles)

    def work(step, carry):
        for k in [step * group + i for i in range(group)]:
            width = tile_list[0, k]
            is_down = tile_list[2, k] == 2
            distance = jnp.bitwise_xor(width // per_piece, me)
            local = columns(lax.rem(width, per_piece))
            hidden_side = side[k]
            wide_side = wide[k]
            for piece in range(1, pieces):
                other = jnp.where(is_down, grads[piece - 1][:, local], inputs[piece - 1][:, local])
                wide_side = jnp.where(distance == piece, other, wide_side)
            left = jnp.where(is_down, hidden_side, wide_side)
            right = jnp.where(is_down, wide_side, hidden_side)
            part[k] = lax.dot_general(left, right, (((0,), (0,)), ((), ())), preferred_element_type=jnp.float32)
            for distance, ref in enumerate(messages):
                for half in range(HALVES):
                    start = pl.multiple_of((half * PLANE + jnp.bitwise_xor(inner, distance)) * SHARE, SHARE)
                    ref[half, k] = part[k, pl.ds(start, SHARE), :].astype(ref.dtype)
        return carry

    lax.fori_loop(0, tiles // group, work, 0)


def plane_kernel(*refs):
    arrived, (kept, sent) = refs[:PLANE], refs[PLANE:]
    half = lax.rem(lax.axis_index("dp") // PLANE, HALVES)
    for which, ref in ((half, kept), (HALVES - 1 - half, sent)):
        summed = arrived[0][which]
        for piece in arrived[1:]:
            summed = summed + piece[which].astype(jnp.float32)
        ref[...] = summed.astype(ref.dtype)


def adam_kernel(outer, *refs):
    slots = refs[0]
    sums = refs[1 : 1 + outer]
    states, message, total, found = refs[1 + outer :]
    tiles = sums[0].shape[0]
    plane = lax.axis_index("dp") // INNER
    spare = INNER * CAP
    for index in range(spare):
        found[index] = -1
    group = grouped(tiles)

    def work(step, carry):
        for k in [step * group + i for i in range(group)]:
            parts = [ref[k].astype(jnp.float32) for ref in sums]
            while len(parts) > 1:
                parts = [parts[i] + parts[i + 1] for i in range(0, len(parts), 2)]
            grad = parts[0]
            total[k] = grad
            owner, slot = slots[k] // CAP, lax.rem(slots[k], CAP)
            found[jnp.where(owner // INNER == plane, lax.rem(slots[k], spare), spare)] = k
            first_old = states[owner, slot].astype(jnp.float32)
            second_old = states[owner, CAP + slot].astype(jnp.float32)
            first = BETA_FIRST * first_old + (1.0 - BETA_FIRST) * grad
            second = BETA_SECOND * second_old + (1.0 - BETA_SECOND) * grad * grad
            first_hat = first / (1.0 - BETA_FIRST**STEP)
            second_hat = second / (1.0 - BETA_SECOND**STEP)
            update = (first_hat / (jnp.sqrt(second_hat) + EPSILON)).astype(jnp.bfloat16)
            for part in range(INNER):
                message[part, k] = update
        return carry

    lax.fori_loop(0, tiles // group, work, 0)
    for part in range(INNER):
        for slot in range(CAP):
            k = found[part * CAP + slot]
            grad = total[jnp.maximum(k, 0)]
            grad = jnp.where(k >= 0, grad, jnp.zeros_like(grad))
            coarse = grad.astype(jnp.bfloat16)
            message[part, tiles + 2 * slot] = coarse
            message[part, tiles + 2 * slot + 1] = (grad - coarse.astype(jnp.float32)).astype(jnp.bfloat16)


def final_kernel(message, first_old, second_old, update_tiles, first_moment, second_moment, total, first, second, sems):
    tiles = update_tiles.shape[0]
    copies = [
        pltpu.make_async_copy(source, target, sems.at[i])
        for i, (source, target) in enumerate(((first_old, first), (second_old, second)))
    ]
    for copy in copies:
        copy.start()
    for part in range(INNER):
        update_tiles[:, pl.ds(part * SHARE, SHARE), :] = message[part, pl.ds(0, tiles)]
        for slot in range(CAP):
            coarse, fine = message[part, tiles + 2 * slot], message[part, tiles + 2 * slot + 1]
            grad = coarse.astype(jnp.float32) + fine.astype(jnp.float32)
            total[pl.ds(part * SHARE * CAP + slot, SHARE, stride=CAP), :] = grad
    for copy in copies:
        copy.wait()
    grad = total[...]
    first_moment[...] = BETA_FIRST * first[...] + (1.0 - BETA_FIRST) * grad
    second_moment[...] = BETA_SECOND * second[...] + (1.0 - BETA_SECOND) * grad * grad


def body(
    layer_input,
    output_grad,
    gate_pre,
    up_pre,
    hidden_grad,
    tile_list,
    tile_slots,
    first_codes,
    second_codes,
    first_absmax,
    second_absmax,
    signed_map,
    unsigned_map,
):
    tiles = tile_list.shape[0]
    owners = lax.axis_size("dp")
    outer = owners // INNER
    pieces = lax.axis_size("tensor")

    inputs = [partner(layer_input, "tensor", r) for r in range(1, pieces)]
    grads = [partner(output_grad, "tensor", r) for r in range(1, pieces)]
    tile_list = tile_list.T

    old = jax.ShapeDtypeStruct((ROWS, TB), jnp.float32)
    whole = jax.ShapeDtypeStruct((tiles, TB, TB), jnp.bfloat16)
    block = pltpu.VMEM((tiles, TB, TB), jnp.bfloat16)
    codes, levels = pltpu.VMEM((ROWS, TB), jnp.int32), pltpu.VMEM((2, TB), jnp.float32)
    scale = pltpu.SMEM(first_absmax.shape[1:], jnp.float32)
    side, wide, first_old, second_old, state_message = pl.pallas_call(
        prepare_kernel,
        out_shape=(whole, whole, old, old, jax.ShapeDtypeStruct((owners, FIELDS, SHARE, TB), jnp.bfloat16)),
        in_specs=[SMEM] + [HBM] * 11,
        out_specs=(VMEM,) * 5,
        scratch_shapes=[block, block, block, codes, codes, scale, scale, levels, levels]
        + [pltpu.SemaphoreType.DMA((tiles, 4)), pltpu.SemaphoreType.DMA((6,))],
        compiler_params=WIDE_PARAMS,
        name="prepare",
    )(
        tile_list,
        layer_input,
        output_grad,
        gate_pre,
        up_pre,
        hidden_grad,
        interleave(first_codes),
        interleave(second_codes),
        first_absmax[0],
        second_absmax[0],
        signed_map.reshape(2, TB),
        unsigned_map.reshape(2, TB),
    )

    halves = (HALVES, tiles, SHARE, TB)
    messages = pl.pallas_call(
        lambda *refs: partial_kernel(pieces, *refs),
        out_shape=(jax.ShapeDtypeStruct(halves, jnp.float32),)
        + (jax.ShapeDtypeStruct(halves, jnp.bfloat16),) * (PLANE - 1),
        in_specs=[SMEM] + [VMEM] * (2 * pieces),
        out_specs=(VMEM,) * PLANE,
        scratch_shapes=[pltpu.VMEM((tiles, TB, TB), jnp.float32)],
        compiler_params=PARAMS,
        name="partials",
    )(tile_list, side, wide, *inputs, *grads)
    arrived = [messages[0]] + [partner(messages[r], "dp", r) for r in range(1, PLANE)]

    state_message = lax.optimization_barrier((state_message, messages[0]))[0]
    states = lax.all_to_all(state_message, "dp", 0, 0, tiled=True)

    share = (tiles, SHARE, TB)
    kept, sent = pl.pallas_call(
        plane_kernel,
        out_shape=(jax.ShapeDtypeStruct(share, jnp.float32), jax.ShapeDtypeStruct(share, jnp.bfloat16)),
        in_specs=[VMEM] * PLANE,
        out_specs=(VMEM, VMEM),
        compiler_params=PARAMS,
        cost_estimate=COST,
        name="plane",
    )(*arrived)
    summed = (kept + partner(sent, "dp", PLANE).astype(jnp.float32)).astype(jnp.bfloat16)
    sums = [summed] + [partner(summed, "dp", r * INNER) for r in range(1, outer)]

    message = pl.pallas_call(
        lambda *refs: adam_kernel(outer, *refs),
        out_shape=jax.ShapeDtypeStruct((INNER, tiles + 2 * CAP, SHARE, TB), jnp.bfloat16),
        in_specs=[SMEM] + [VMEM] * (outer + 1),
        out_specs=VMEM,
        scratch_shapes=[
            pltpu.VMEM((tiles, SHARE, TB), jnp.float32),
            pltpu.SMEM((INNER * CAP + 1,), jnp.int32),
        ],
        compiler_params=PARAMS,
        name="adam",
    )(tile_slots, *sums, states)
    message = exchange(message)

    update_tiles, first_moment, second_moment = pl.pallas_call(
        final_kernel,
        out_shape=(jax.ShapeDtypeStruct((tiles, TB, TB), jnp.bfloat16), old, old),
        in_specs=[VMEM, HBM, HBM],
        out_specs=(VMEM,) * 3,
        scratch_shapes=[pltpu.VMEM((ROWS, TB), jnp.float32)] * 3 + [pltpu.SemaphoreType.DMA((2,))],
        compiler_params=PARAMS,
        name="final",
    )(message, first_old, second_old)
    return update_tiles, separate(first_moment), separate(second_moment)


def solution(mesh):
    in_specs = (
        P("dp", "tensor"),
        P("dp", "tensor"),
        P("dp", "tensor"),
        P("dp", "tensor"),
        P("dp", "tensor"),
        P("tensor", None),
        P("tensor"),
        P("tensor", "dp", None),
        P("tensor", "dp", None),
        P("tensor", "dp", None),
        P("tensor", "dp", None),
        P(),
        P(),
    )
    out_specs = (P("tensor", None, None), P("tensor", "dp", None), P("tensor", "dp", None))
    return jax.shard_map(body, mesh=mesh, in_specs=in_specs, out_specs=out_specs, check_vma=False)
```

time: 242 us -> 48 us (0.20)
  waiting for transfers between devices: 135 us -> 7.03 us
  local copies, waits for them, and re-layouts: 64.9 us -> 2.05 us
  starting transfers between devices: 3.98 us -> 17.7 us
  between operations: 14.2 us -> 0.76 us
  other arithmetic: 13.4 us -> 0.02 us
  blocking collectives: 0 us -> 12.1 us
  matrix products: 9.2 us -> 0 us
  Pallas kernels: 0 us -> 7.96 us
    reduce_scatter x1 -> x0, waiting for transfers between devices: 77.7 us -> none  [body(): lax.psum_scatter(partial_value, 'dp', scatter_dimension=1, tiled=True)]
    all_gather x3 -> x0, waiting for transfers between devices: 51.1 us -> none  [the longest x1 51.1 us: body(): everyone = lax.all_gather(slot_update, 'dp', axis=0, tiled=True)]
    reshape x7 -> x0, local copies, waits for them, and re-layouts: 25.7 us -> none  [the longest x5 25.6 us: blocks(): return jnp.take(source.reshape(tokens_here, -1, TB), block_index, axis=1)]
    unnamed x51 -> x12, local copies, waits for them, and re-layouts: 25.6 us -> 2.05 us
    gather x6 -> x0, local copies, waits for them, and re-layouts: 12.5 us -> none  [the longest x5 11.6 us: blocks(): return jnp.take(source.reshape(tokens_here, -1, TB), block_index, axis=1)]
    all_to_all x0 -> x1, blocking collectives: none -> 12.1 us  [exchange(): lax.all_to_all(array, 'dp', 0, 0, tiled=True, axis_index_groups=groups)]
    ppermute x0 -> x7, starting transfers between devices: none -> 10.4 us  [partner(): return lax.ppermute(array, axis, [(i, i ^ distance) for i in range(count)])]
    convert_element_type x2 -> x1, other arithmetic: 10.1 us -> 0.02 us  [body(): (kept + partner(sent, 'dp', PLANE).astype(jnp.float32)).astype(jnp.bfloat16)]
  transfers between devices with their start and end apart: 5 -> 8, of which waited for: 3 -> 2; matrix products, arithmetic and copies ran while one was open for 28% -> 0% of each run, Pallas kernels for 0% -> 10%
where the time goes in v2:
time: 48 us; the launch traced here: 47.6 us
  starting transfers between devices  17.7 us (37%)
  blocking collectives  12.1 us (25%)
  Pallas kernels  7.96 us (17%)
  waiting for transfers between devices  7.03 us (15%)
  local copies, waits for them, and re-layouts  2.05 us (4%)
  between operations  0.76 us (2%)
    all_to_all x1, blocking collectives, exchange(): lax.all_to_all(array, 'dp', 0, 0, tiled=True, axis_index_groups=groups)  12.1 us
    ppermute x7, starting transfers between devices, partner(): return lax.ppermute(array, axis, [(i, i ^ distance) for i in range(count)])  10.4 us
    all_to_all x1, starting transfers between devices, body(): states = lax.all_to_all(state_message, 'dp', 0, 0, tiled=True)  7.33 us
    ppermute x7, waiting for transfers between devices, partner(): return lax.ppermute(array, axis, [(i, i ^ distance) for i in range(count)])  7.03 us
    pallas_call x1, Pallas kernels, body(): pl.pallas_call(prepare_kernel, out_shape=(whole, whole, old, old, jax.Sha...  4.55 us
    unnamed x12, local copies, waits for them, and re-layouts  2.05 us
    pallas_call x1, Pallas kernels, body(): pl.pallas_call(final_kernel, out_shape=(jax.ShapeDtypeStruct((tiles, TB,...  1.26 us
    pallas_call x1, Pallas kernels, body(): pl.pallas_call(lambda *refs: partial_kernel(pieces, *refs), out_shape=(ja...  1.26 us
  transfers between devices with their start and end apart: 8, of which 2 were waited for; matrix products, arithmetic and copies ran while one was open for 0% of the time, Pallas kernels for 10%

profile of v2, /device:TPU:0, one launch (start us, length us, event | category | flops | bytes accessed | tf_op | source)
XLA Modules:
  0.0 47.6 jit_solution(4817390231425599896)
XLA Ops:
  0.6 0.5 %collective-permute-start = (bf16[128,4096]{1,0:T(8,128)(2,1)}, bf16[128,4096]{1,0:T(8,128)(2,1)S(1)}, u32[]{:S(2)}, u32[]{:S(2)}) collective-permute-start(bf16[128,4096]{1,0:T(8,128)(2,1)} %refs_1_.1), channel_id=1, source_target_pairs={{0,1},{1,0},{2,3},{3,2},{4,5},{5,4},{6,7},{7,6},{8,9},{9,8},{10,11... | collective-permute-start | bytes 3145736 | tf_op jit(solution)/shard_map/ppermute | solution.py:33
  1.2 0.1 collective-permute-start.1
  1.2 4.6 %prepare.1 = (bf16[14,128,128]{2,1,0:T(8,128)(2,1)}, bf16[14,128,128]{2,1,0:T(8,128)(2,1)}, f32[256,128]{1,0:T(8,128)}, f32[256,128]{1,0:T(8,128)}, bf16[16,4,16,128]{3,2,1,0:T(8,128)(2,1)}) custom-call(s32[3,14]{1,0:T(4,128)} %bitcast.25, bf16[128,4096]{1,0:T(8,128)(2,1)} %refs_1_.1, bf16[128,4096]{1,0:T(8,128)(2,1)} %refs_2_.1, ...), custom_call_target="tpu_custom_call" | custom-call | tf_op jit(solution)/shard_map/prepare/pallas_call | solution.py:271
  5.8 0.0 collective-permute-done.refs_3_
  5.8 0.0 collective-permute-done.1.refs_4_
  5.8 0.0 copy-done.4
  5.8 0.0 copy-start
  5.8 1.0 %copy-done = bf16[14,128,128]{2,1,0:T(8,128)(2,1)S(1)} copy-done((bf16[14,128,128]{2,1,0:T(8,128)(2,1)S(1)}, bf16[14,128,128]{2,1,0:T(8,128)(2,1)}, u32[]{:S(2)}) %copy-start) | copy-done | bytes 458776
  6.8 1.0 %copy-done.1 = bf16[14,128,128]{2,1,0:T(8,128)(2,1)S(1)} copy-done((bf16[14,128,128]{2,1,0:T(8,128)(2,1)S(1)}, bf16[14,128,128]{2,1,0:T(8,128)(2,1)}, u32[]{:S(2)}) %copy-start.1) | copy-done | bytes 458776
  7.9 1.3 %partials.1 = (f32[2,14,16,128]{3,2,1,0:T(8,128)S(1)}, bf16[2,14,16,128]{3,2,1,0:T(8,128)(2,1)S(1)}, bf16[2,14,16,128]{3,2,1,0:T(8,128)(2,1)S(1)}, bf16[2,14,16,128]{3,2,1,0:T(8,128)(2,1)S(1)}) custom-call(s32[3,14]{1,0:T(4,128)S(1)} %bitcast.26, bf16[14,128,128]{2,1,0:T(8,128)(2,1)S(1)} %copy-done, bf16[14,128,128]{2,1,0:T(8,128)(2,1)S(1)} %copy-done.1, ...), custom_call_target="tpu_custom_call" | custom-call | tf_op jit(solution)/shard_map/partials/pallas_call | solution.py:296
  9.1 3.0 %collective-permute-start.2 = (bf16[2,14,16,128]{3,2,1,0:T(8,128)(2,1)S(1)}, bf16[2,14,16,128]{3,2,1,0:T(8,128)(2,1)S(1)}, u32[]{:S(2)}, u32[]{:S(2)}) collective-permute-start(bf16[2,14,16,128]{3,2,1,0:T(8,128)(2,1)S(1)} %get-tuple-element.21), channel_id=1, source_target_pairs={{0,2},{2,0},{4,6},{6,4},{8,10},{10,8},{12,14},{14,12},{16,18},{18,... | collective-permute-start | bytes 344072 | tf_op jit(solution)/shard_map/ppermute | solution.py:33
  12.1 1.5 %collective-permute-start.3 = (bf16[2,14,16,128]{3,2,1,0:T(8,128)(2,1)S(1)}, bf16[2,14,16,128]{3,2,1,0:T(8,128)(2,1)S(1)}, u32[]{:S(2)}, u32[]{:S(2)}) collective-permute-start(bf16[2,14,16,128]{3,2,1,0:T(8,128)(2,1)S(1)} %get-tuple-element.22), channel_id=1, source_target_pairs={{0,4},{2,6},{4,0},{6,2},{8,12},{10,14},{12,8},{14,10},{16,20},{18,... | collective-permute-start | bytes 344072 | tf_op jit(solution)/shard_map/ppermute | solution.py:33
  13.6 0.0 collective-permute-start.4
  13.7 7.3 %all-to-all-start = ((bf16[16,4,16,128]{3,2,1,0:T(8,128)(2,1)}), bf16[16,4,16,128]{3,2,1,0:T(8,128)(2,1)S(1)}, u32[]{:S(2)}, u32[]{:S(2)}) async-start(bf16[16,4,16,128]{3,2,1,0:T(8,128)(2,1)} %get-tuple-element.27), calls=%async_computation | async-start | bytes 524288 | tf_op jit(solution)/shard_map/all_to_all | solution.py:309
  21.0 0.0 copy-start.5
  21.0 0.0 copy-start.2
  21.0 0.0 copy-start.3
  21.0 0.0 collective-permute-done.2.refs_1_
  21.0 0.0 collective-permute-done.3.refs_2_
  21.0 0.0 collective-permute-done.4.refs_3_
  21.1 0.1 plane.1
  21.1 2.0 %collective-permute-start.5 = (bf16[14,16,128]{2,1,0:T(8,128)(2,1)S(1)}, bf16[14,16,128]{2,1,0:T(8,128)(2,1)S(1)}, u32[]{:S(2)}, u32[]{:S(2)}) collective-permute-start(bf16[14,16,128]{2,1,0:T(8,128)(2,1)S(1)} %get-tuple-element.25), channel_id=1, source_target_pairs={{0,8},{2,10},{4,12},{6,14},{8,0},{10,2},{12,4},{14,6},{16,24},{18,... | collective-permute-start | bytes 172040 | tf_op jit(solution)/shard_map/ppermute | solution.py:33
  23.1 4.2 %collective-permute-done.5 = bf16[14,16,128]{2,1,0:T(8,128)(2,1)S(1)} collective-permute-done((bf16[14,16,128]{2,1,0:T(8,128)(2,1)S(1)}, bf16[14,16,128]{2,1,0:T(8,128)(2,1)S(1)}, u32[]{:S(2)}, u32[]{:S(2)}) %collective-permute-start.5) | collective-permute-done | bytes 57376 | tf_op jit(solution)/shard_map/ppermute | solution.py:33
  27.4 3.3 %collective-permute-start.6 = (bf16[14,16,128]{2,1,0:T(8,128)(2,1)S(1)}, bf16[14,16,128]{2,1,0:T(8,128)(2,1)S(1)}, u32[]{:S(2)}, u32[]{:S(2)}) collective-permute-start(bf16[14,16,128]{2,1,0:T(8,128)(2,1)S(1)} %add_convert_fusion.refs_1_), channel_id=1, source_target_pairs={{0,16},{2,18},{4,20},{6,22},{8,24},{10,26},{12,28},{14,30},{16,0},... | collective-permute-start | bytes 172040 | tf_op jit(solution)/shard_map/ppermute | solution.py:33
  30.7 2.8 %collective-permute-done.6.refs_2_ = bf16[14,16,128]{2,1,0:T(8,128)(2,1)S(1)} collective-permute-done((bf16[14,16,128]{2,1,0:T(8,128)(2,1)S(1)}, bf16[14,16,128]{2,1,0:T(8,128)(2,1)S(1)}, u32[]{:S(2)}, u32[]{:S(2)}) %collective-permute-start.6) | collective-permute-done | bytes 57376 | tf_op jit(solution)/shard_map/ppermute | solution.py:33
  33.4 0.0 all-to-all-done.refs_3_
  33.4 0.0 copy-done.5
  33.4 0.8 %adam.1 = bf16[8,18,16,128]{3,2,1,0:T(8,128)(2,1)S(1)} custom-call(s32[14]{0:T(128)S(1)} %copy-done.5, bf16[14,16,128]{2,1,0:T(8,128)(2,1)S(1)} %add_convert_fusion.refs_1_, bf16[14,16,128]{2,1,0:T(8,128)(2,1)S(1)} %collective-permute-done.6.refs_2_, bf16[16,4,16,128]{3,2,1,0:T(8,128)(2,1)S(1)} %all-to-all-done.refs_3_), custom_call_target="tpu_custom_call" | custom-call | tf_op jit(solution)/shard_map/adam/pallas_call | solution.py:324
  34.2 12.1 %all_to_all.10.message = bf16[8,18,16,128]{3,2,1,0:T(8,128)(2,1)S(1)} all-to-all(bf16[8,18,16,128]{3,2,1,0:T(8,128)(2,1)S(1)} %adam.1), channel_id=1, replica_groups={{0,2,4,6,8,10,12,14},{16,18,20,22,24,26,28,30},{1,3,5,7,9,11,13,15},{17..., dimensions={0} | all-to-all | bytes 1179648 | tf_op jit(solution)/shard_map/all_to_all | solution.py:39
  46.3 0.0 copy-done.2
  46.3 0.0 copy-done.3
  46.3 1.3 %final.1 = (bf16[14,128,128]{2,1,0:T(8,128)(2,1)}, f32[256,128]{1,0:T(8,128)}, f32[256,128]{1,0:T(8,128)}) custom-call(bf16[8,18,16,128]{3,2,1,0:T(8,128)(2,1)S(1)} %all_to_all.10.message, f32[256,128]{1,0:T(8,128)S(1)} %copy-done.2, f32[256,128]{1,0:T(8,128)S(1)} %copy-done.3), custom_call_target="tpu_custom_call" | custom-call | tf_op jit(solution)/shard_map/final/pallas_call | solution.py:338
  (3 shorter events, 0.0 us)
Async XLA Ops:
  0.6 5.2 %collective-permute-start = (bf16[128,4096]{1,0:T(8,128)(2,1)}, bf16[128,4096]{1,0:T(8,128)(2,1)S(1)}, u32[]{:S(2)}, u32[]{:S(2)}) collective-permute-start(bf16[128,4096]{1,0:T(8,128)(2,1)} %refs_1_.1), channel_id=1, source_target_pairs={{0,1},{1,0},{2,3},{3,2},{4,5},{5,4},{6,7},{7,6},{8,9},{9,8},{10,11... | collective-permute-start | bytes 3145736 | tf_op jit(solution)/shard_map/ppermute | solution.py:33
  1.2 4.7 %collective-permute-start.1 = (bf16[128,4096]{1,0:T(8,128)(2,1)}, bf16[128,4096]{1,0:T(8,128)(2,1)S(1)}, u32[]{:S(2)}, u32[]{:S(2)}) collective-permute-start(bf16[128,4096]{1,0:T(8,128)(2,1)} %refs_2_.1), channel_id=1, source_target_pairs={{0,1},{1,0},{2,3},{3,2},{4,5},{5,4},{6,7},{7,6},{8,9},{9,8},{10,11... | collective-permute-start | bytes 3145736 | tf_op jit(solution)/shard_map/ppermute | solution.py:33
  1.2 4.6 %copy-start.4 = (s32[14,3]{0,1:T(4,128)S(1)}, s32[14,3]{0,1:T(4,128)}, u32[]{:S(2)}) copy-start(s32[14,3]{0,1:T(4,128)} %param.18) | copy-start | bytes 508
  5.8 1.0 %copy-start = (bf16[14,128,128]{2,1,0:T(8,128)(2,1)S(1)}, bf16[14,128,128]{2,1,0:T(8,128)(2,1)}, u32[]{:S(2)}) copy-start(bf16[14,128,128]{2,1,0:T(8,128)(2,1)} %get-tuple-element.18.refs_1_) | copy-start | bytes 1376260
  6.8 1.0 %copy-start.1 = (bf16[14,128,128]{2,1,0:T(8,128)(2,1)S(1)}, bf16[14,128,128]{2,1,0:T(8,128)(2,1)}, u32[]{:S(2)}) copy-start(bf16[14,128,128]{2,1,0:T(8,128)(2,1)} %get-tuple-element.19.refs_2_) | copy-start | bytes 1376260
  9.1 11.9 %collective-permute-start.2 = (bf16[2,14,16,128]{3,2,1,0:T(8,128)(2,1)S(1)}, bf16[2,14,16,128]{3,2,1,0:T(8,128)(2,1)S(1)}, u32[]{:S(2)}, u32[]{:S(2)}) collective-permute-start(bf16[2,14,16,128]{3,2,1,0:T(8,128)(2,1)S(1)} %get-tuple-element.21), channel_id=1, source_target_pairs={{0,2},{2,0},{4,6},{6,4},{8,10},{10,8},{12,14},{14,12},{16,18},{18,... | collective-permute-start | bytes 344072 | tf_op jit(solution)/shard_map/ppermute | solution.py:33
  12.1 8.9 %collective-permute-start.3 = (bf16[2,14,16,128]{3,2,1,0:T(8,128)(2,1)S(1)}, bf16[2,14,16,128]{3,2,1,0:T(8,128)(2,1)S(1)}, u32[]{:S(2)}, u32[]{:S(2)}) collective-permute-start(bf16[2,14,16,128]{3,2,1,0:T(8,128)(2,1)S(1)} %get-tuple-element.22), channel_id=1, source_target_pairs={{0,4},{2,6},{4,0},{6,2},{8,12},{10,14},{12,8},{14,10},{16,20},{18,... | collective-permute-start | bytes 344072 | tf_op jit(solution)/shard_map/ppermute | solution.py:33
  13.6 7.4 %collective-permute-start.4 = (bf16[2,14,16,128]{3,2,1,0:T(8,128)(2,1)S(1)}, bf16[2,14,16,128]{3,2,1,0:T(8,128)(2,1)S(1)}, u32[]{:S(2)}, u32[]{:S(2)}) collective-permute-start(bf16[2,14,16,128]{3,2,1,0:T(8,128)(2,1)S(1)} %get-tuple-element.23), channel_id=1, source_target_pairs={{0,6},{2,4},{4,2},{6,0},{8,14},{10,12},{12,10},{14,8},{16,22},{18,... | collective-permute-start | bytes 344072 | tf_op jit(solution)/shard_map/ppermute | solution.py:33
  13.7 19.8 %all-to-all-start = ((bf16[16,4,16,128]{3,2,1,0:T(8,128)(2,1)}), bf16[16,4,16,128]{3,2,1,0:T(8,128)(2,1)S(1)}, u32[]{:S(2)}, u32[]{:S(2)}) async-start(bf16[16,4,16,128]{3,2,1,0:T(8,128)(2,1)} %get-tuple-element.27), calls=%async_computation | async-start | bytes 524288 | tf_op jit(solution)/shard_map/all_to_all | solution.py:309
  21.0 12.4 %copy-start.5 = (s32[14]{0:T(128)S(1)}, s32[14]{0:T(128)}, u32[]{:S(2)}) copy-start(s32[14]{0:T(128)} %refs_0_.1) | copy-start | bytes 172
  21.0 25.3 %copy-start.2 = (f32[256,128]{1,0:T(8,128)S(1)}, f32[256,128]{1,0:T(8,128)}, u32[]{:S(2)}) copy-start(f32[256,128]{1,0:T(8,128)} %get-tuple-element.28.first_old) | copy-start | bytes 393220
  21.0 25.3 %copy-start.3 = (f32[256,128]{1,0:T(8,128)S(1)}, f32[256,128]{1,0:T(8,128)}, u32[]{:S(2)}) copy-start(f32[256,128]{1,0:T(8,128)} %get-tuple-element.29.second_old) | copy-start | bytes 393220
  21.1 6.2 %collective-permute-start.5 = (bf16[14,16,128]{2,1,0:T(8,128)(2,1)S(1)}, bf16[14,16,128]{2,1,0:T(8,128)(2,1)S(1)}, u32[]{:S(2)}, u32[]{:S(2)}) collective-permute-start(bf16[14,16,128]{2,1,0:T(8,128)(2,1)S(1)} %get-tuple-element.25), channel_id=1, source_target_pairs={{0,8},{2,10},{4,12},{6,14},{8,0},{10,2},{12,4},{14,6},{16,24},{18,... | collective-permute-start | bytes 172040 | tf_op jit(solution)/shard_map/ppermute | solution.py:33
  27.4 6.0 %collective-permute-start.6 = (bf16[14,16,128]{2,1,0:T(8,128)(2,1)S(1)}, bf16[14,16,128]{2,1,0:T(8,128)(2,1)S(1)}, u32[]{:S(2)}, u32[]{:S(2)}) collective-permute-start(bf16[14,16,128]{2,1,0:T(8,128)(2,1)S(1)} %add_convert_fusion.refs_1_), channel_id=1, source_target_pairs={{0,16},{2,18},{4,20},{6,22},{8,24},{10,26},{12,28},{14,30},{16,0},... | collective-permute-start | bytes 172040 | tf_op jit(solution)/shard_map/ppermute | solution.py:33

commit v3 on v2

--- a/solution.py
+++ b/solution.py
@@ -25,7 +25,11 @@
 HALVES = INNER // PLANE
 COST = pl.CostEstimate(flops=10**11, bytes_accessed=10**8, transcendentals=0)
 PARAMS = pltpu.CompilerParams(vmem_limit_bytes=32 * 1024 * 1024)
-WIDE_PARAMS = pltpu.CompilerParams(vmem_limit_bytes=55 * 1024 * 1024)
+WIDE_PARAMS = pltpu.CompilerParams(vmem_limit_bytes=32 * 1024 * 1024)
+
+
+def pinned(array):
+    return pltpu.with_memory_space_constraint(array, pltpu.HBM)
 
 
 def partner(array, axis, distance):
@@ -56,19 +60,22 @@
 
 
 def prepare_kernel(*refs):
-    tile_list, layer_input, output_grad, *sources = refs[:6]
+    tile_source, layer_input, output_grad, *sources = refs[:6]
     tables = refs[6:12]
     side, wide, first_old, second_old, message = refs[12:17]
-    targets, held, sems, table_sems = refs[17:20], refs[20:26], refs[26], refs[27]
+    targets, held, tile_list, sems, table_sems = refs[17:20], refs[20:26], *refs[26:]
     tiles = side.shape[0]
     per_piece = layer_input.shape[1] // TB
     owners = message.shape[0]
 
-    copies = [
-        pltpu.make_async_copy(source, target, table_sems.at[i]) for i, (source, target) in enumerate(zip(tables, held))
+    tile_copy, *copies = [
+        pltpu.make_async_copy(source, target, table_sems.at[i])
+        for i, (source, target) in enumerate(zip((tile_source, *tables), (tile_list, *held)))
     ]
+    tile_copy.start()
     for copy in copies:
         copy.start()
+    tile_copy.wait()
 
     def begin(k, carry):
         for slot, (source, target) in enumerate(zip(sources, targets)):
@@ -101,7 +108,7 @@
                 jnp.take_along_axis(high, lane, axis=1),
                 jnp.take_along_axis(low, lane, axis=1),
             )
-            old[rows, :] = picked * jnp.where(odd, scale[1, block], scale[0, block])
+            old[rows, :] = picked * jnp.where(odd, scale[1:2, block : block + 1], scale[0:1, block : block + 1])
         for part in range(INNER):
             for slot in range(CAP):
                 sent = old[pl.ds(part * SHARE * CAP + slot, SHARE, stride=CAP), :].astype(jnp.bfloat16)
@@ -218,25 +225,17 @@
             message[part, tiles + 2 * slot + 1] = (grad - coarse.astype(jnp.float32)).astype(jnp.bfloat16)
 
 
-def final_kernel(message, first_old, second_old, update_tiles, first_moment, second_moment, total, first, second, sems):
+def final_kernel(message, first_old, second_old, update_tiles, first_moment, second_moment, total):
     tiles = update_tiles.shape[0]
-    copies = [
-        pltpu.make_async_copy(source, target, sems.at[i])
-        for i, (source, target) in enumerate(((first_old, first), (second_old, second)))
-    ]
-    for copy in copies:
-        copy.start()
     for part in range(INNER):
         update_tiles[:, pl.ds(part * SHARE, SHARE), :] = message[part, pl.ds(0, tiles)]
         for slot in range(CAP):
             coarse, fine = message[part, tiles + 2 * slot], message[part, tiles + 2 * slot + 1]
             grad = coarse.astype(jnp.float32) + fine.astype(jnp.float32)
             total[pl.ds(part * SHARE * CAP + slot, SHARE, stride=CAP), :] = grad
-    for copy in copies:
-        copy.wait()
     grad = total[...]
-    first_moment[...] = BETA_FIRST * first[...] + (1.0 - BETA_FIRST) * grad
-    second_moment[...] = BETA_SECOND * second[...] + (1.0 - BETA_SECOND) * grad * grad
+    first_moment[...] = BETA_FIRST * first_old[...] + (1.0 - BETA_FIRST) * grad
+    second_moment[...] = BETA_SECOND * second_old[...] + (1.0 - BETA_SECOND) * grad * grad
 
 
 def body(
@@ -264,32 +263,38 @@
     tile_list = tile_list.T
 
     old = jax.ShapeDtypeStruct((ROWS, TB), jnp.float32)
-    whole = jax.ShapeDtypeStruct((tiles, TB, TB), jnp.bfloat16)
+    kept_whole = pltpu.VMEM((tiles, TB, TB), jnp.bfloat16)
+    kept_old = pltpu.VMEM((ROWS, TB), jnp.float32)
     block = pltpu.VMEM((tiles, TB, TB), jnp.bfloat16)
     codes, levels = pltpu.VMEM((ROWS, TB), jnp.int32), pltpu.VMEM((2, TB), jnp.float32)
-    scale = pltpu.SMEM(first_absmax.shape[1:], jnp.float32)
+    scale = pltpu.VMEM(first_absmax.shape[1:], jnp.float32)
     side, wide, first_old, second_old, state_message = pl.pallas_call(
         prepare_kernel,
-        out_shape=(whole, whole, old, old, jax.ShapeDtypeStruct((owners, FIELDS, SHARE, TB), jnp.bfloat16)),
-        in_specs=[SMEM] + [HBM] * 11,
+        out_shape=(kept_whole, kept_whole, kept_old, kept_old, pltpu.VMEM((owners, FIELDS, SHARE, TB), jnp.bfloat16)),
+        in_specs=[HBM] * 12,
         out_specs=(VMEM,) * 5,
         scratch_shapes=[block, block, block, codes, codes, scale, scale, levels, levels]
-        + [pltpu.SemaphoreType.DMA((tiles, 4)), pltpu.SemaphoreType.DMA((6,))],
+        + [pltpu.SMEM(tile_list.shape, jnp.int32), pltpu.SemaphoreType.DMA((tiles, 4)), pltpu.SemaphoreType.DMA((7,))],
         compiler_params=WIDE_PARAMS,
         name="prepare",
     )(
-        tile_list,
-        layer_input,
-        output_grad,
-        gate_pre,
-        up_pre,
-        hidden_grad,
-        interleave(first_codes),
-        interleave(second_codes),
-        first_absmax[0],
-        second_absmax[0],
-        signed_map.reshape(2, TB),
-        unsigned_map.reshape(2, TB),
+        *map(
+            pinned,
+            (
+                tile_list,
+                layer_input,
+                output_grad,
+                gate_pre,
+                up_pre,
+                hidden_grad,
+                interleave(first_codes),
+                interleave(second_codes),
+                first_absmax[0],
+                second_absmax[0],
+                signed_map.reshape(2, TB),
+                unsigned_map.reshape(2, TB),
+            ),
+        ),
     )
 
     halves = (HALVES, tiles, SHARE, TB)
@@ -338,9 +343,9 @@
     update_tiles, first_moment, second_moment = pl.pallas_call(
         final_kernel,
         out_shape=(jax.ShapeDtypeStruct((tiles, TB, TB), jnp.bfloat16), old, old),
-        in_specs=[VMEM, HBM, HBM],
+        in_specs=[VMEM] * 3,
         out_specs=(VMEM,) * 3,
-        scratch_shapes=[pltpu.VMEM((ROWS, TB), jnp.float32)] * 3 + [pltpu.SemaphoreType.DMA((2,))],
+        scratch_shapes=[pltpu.VMEM((ROWS, TB), jnp.float32)],
         compiler_params=PARAMS,
         name="final",
     )(message, first_old, second_old)

time: 48 us -> 44.9 us (0.935)
  local copies, waits for them, and re-layouts: 2.05 us -> 0.01 us
  Pallas kernels: 7.96 us -> 6.89 us
    unnamed x12 -> x4, local copies, waits for them, and re-layouts: 2.05 us -> 0.01 us
    pallas_call x1, Pallas kernels: 4.55 us -> 3.85 us  [body(): pl.pallas_call(prepare_kernel, out_shape=(kept_whole, kept_whole, kept_ol...]
  transfers between devices with their start and end apart: 8 -> 8, of which waited for: 2 -> 2; matrix products, arithmetic and copies ran while one was open for 0% -> 0% of each run, Pallas kernels for 10% -> 9%
where the time goes in v3:
time: 44.9 us; the launch traced here: 44.5 us
  starting transfers between devices  17.6 us (39%)
  blocking collectives  12.1 us (27%)
  waiting for transfers between devices  7.15 us (16%)
  Pallas kernels  6.89 us (15%)
  between operations  0.71 us (2%)
    all_to_all x1, blocking collectives, exchange(): lax.all_to_all(array, 'dp', 0, 0, tiled=True, axis_index_groups=groups)  12.1 us
    ppermute x7, starting transfers between devices, partner(): return lax.ppermute(array, axis, [(i, i ^ distance) for i in range(count)])  10.3 us
    all_to_all x1, starting transfers between devices, body(): states = lax.all_to_all(state_message, 'dp', 0, 0, tiled=True)  7.33 us
    ppermute x7, waiting for transfers between devices, partner(): return lax.ppermute(array, axis, [(i, i ^ distance) for i in range(count)])  7.14 us
    pallas_call x1, Pallas kernels, body(): pl.pallas_call(prepare_kernel, out_shape=(kept_whole, kept_whole, kept_ol...  3.85 us
    pallas_call x1, Pallas kernels, body(): pl.pallas_call(lambda *refs: partial_kernel(pieces, *refs), out_shape=(ja...  1.25 us
    pallas_call x1, Pallas kernels, body(): pl.pallas_call(final_kernel, out_shape=(jax.ShapeDtypeStruct((tiles, TB,...  0.9 us
  transfers between devices with their start and end apart: 8, of which 2 were waited for; matrix products, arithmetic and copies ran while one was open for 0% of the time, Pallas kernels for 9%

profile of v3, /device:TPU:0, one launch (start us, length us, event | category | flops | bytes accessed | tf_op | source)
XLA Modules:
  0.0 44.5 jit_solution(2909370225942567395)
XLA Ops:
  0.6 0.5 %collective-permute-start = (bf16[128,4096]{1,0:T(8,128)(2,1)}, bf16[128,4096]{1,0:T(8,128)(2,1)S(1)}, u32[]{:S(2)}, u32[]{:S(2)}) collective-permute-start(bf16[128,4096]{1,0:T(8,128)(2,1)} %refs_1_.1), channel_id=1, source_target_pairs={{0,1},{1,0},{2,3},{3,2},{4,5},{5,4},{6,7},{7,6},{8,9},{9,8},{10,11... | collective-permute-start | bytes 3145736 | tf_op jit(solution)/shard_map/ppermute | solution.py:37
  1.2 0.1 collective-permute-start.1
  1.2 0.0 copy-start
  1.2 3.9 %prepare.1 = (bf16[14,128,128]{2,1,0:T(8,128)(2,1)S(1)}, bf16[14,128,128]{2,1,0:T(8,128)(2,1)S(1)}, f32[256,128]{1,0:T(8,128)S(1)}, f32[256,128]{1,0:T(8,128)S(1)}, bf16[16,4,16,128]{3,2,1,0:T(8,128)(2,1)}) custom-call(s32[3,14]{1,0:T(4,128)} %bitcast.25, bf16[128,4096]{1,0:T(8,128)(2,1)} %refs_1_.1, bf16[128,4096]{1,0:T(8,128)(2,1)} %refs_2_.1, ...), custom_call_target="tpu_custom_call" | custom-call | tf_op jit(solution)/shard_map/prepare/pallas_call | solution.py:271
  5.1 0.0 collective-permute-done.refs_3_
  5.1 0.0 collective-permute-done.1.refs_4_
  5.1 0.0 copy-done
  5.2 1.3 %partials.1 = (f32[2,14,16,128]{3,2,1,0:T(8,128)S(1)}, bf16[2,14,16,128]{3,2,1,0:T(8,128)(2,1)S(1)}, bf16[2,14,16,128]{3,2,1,0:T(8,128)(2,1)S(1)}, bf16[2,14,16,128]{3,2,1,0:T(8,128)(2,1)S(1)}) custom-call(s32[3,14]{1,0:T(4,128)S(1)} %bitcast.26, bf16[14,128,128]{2,1,0:T(8,128)(2,1)S(1)} %get-tuple-element.18.refs_1_, ...), custom_call_target="tpu_custom_call" | custom-call | tf_op jit(solution)/shard_map/partials/pallas_call | solution.py:301
  6.4 3.0 %collective-permute-start.2 = (bf16[2,14,16,128]{3,2,1,0:T(8,128)(2,1)S(1)}, bf16[2,14,16,128]{3,2,1,0:T(8,128)(2,1)S(1)}, u32[]{:S(2)}, u32[]{:S(2)}) collective-permute-start(bf16[2,14,16,128]{3,2,1,0:T(8,128)(2,1)S(1)} %get-tuple-element.21), channel_id=1, source_target_pairs={{0,2},{2,0},{4,6},{6,4},{8,10},{10,8},{12,14},{14,12},{16,18},{18,... | collective-permute-start | bytes 344072 | tf_op jit(solution)/shard_map/ppermute | solution.py:37
  9.4 1.5 %collective-permute-start.3 = (bf16[2,14,16,128]{3,2,1,0:T(8,128)(2,1)S(1)}, bf16[2,14,16,128]{3,2,1,0:T(8,128)(2,1)S(1)}, u32[]{:S(2)}, u32[]{:S(2)}) collective-permute-start(bf16[2,14,16,128]{3,2,1,0:T(8,128)(2,1)S(1)} %get-tuple-element.22), channel_id=1, source_target_pairs={{0,4},{2,6},{4,0},{6,2},{8,12},{10,14},{12,8},{14,10},{16,20},{18,... | collective-permute-start | bytes 344072 | tf_op jit(solution)/shard_map/ppermute | solution.py:37
  10.9 0.0 collective-permute-start.4
  10.9 7.3 %all-to-all-start = ((bf16[16,4,16,128]{3,2,1,0:T(8,128)(2,1)}), bf16[16,4,16,128]{3,2,1,0:T(8,128)(2,1)S(1)}, u32[]{:S(2)}, u32[]{:S(2)}) async-start(bf16[16,4,16,128]{3,2,1,0:T(8,128)(2,1)} %get-tuple-element.27), calls=%async_computation | async-start | bytes 524288 | tf_op jit(solution)/shard_map/all_to_all | solution.py:314
  18.2 0.0 copy-start.1
  18.3 0.0 collective-permute-done.2.refs_1_
  18.3 0.0 collective-permute-done.3.refs_2_
  18.3 0.0 collective-permute-done.4.refs_3_
  18.3 0.1 plane.1
  18.4 2.0 %collective-permute-start.5 = (bf16[14,16,128]{2,1,0:T(8,128)(2,1)S(1)}, bf16[14,16,128]{2,1,0:T(8,128)(2,1)S(1)}, u32[]{:S(2)}, u32[]{:S(2)}) collective-permute-start(bf16[14,16,128]{2,1,0:T(8,128)(2,1)S(1)} %get-tuple-element.25), channel_id=1, source_target_pairs={{0,8},{2,10},{4,12},{6,14},{8,0},{10,2},{12,4},{14,6},{16,24},{18,... | collective-permute-start | bytes 172040 | tf_op jit(solution)/shard_map/ppermute | solution.py:37
  20.4 4.3 %collective-permute-done.5 = bf16[14,16,128]{2,1,0:T(8,128)(2,1)S(1)} collective-permute-done((bf16[14,16,128]{2,1,0:T(8,128)(2,1)S(1)}, bf16[14,16,128]{2,1,0:T(8,128)(2,1)S(1)}, u32[]{:S(2)}, u32[]{:S(2)}) %collective-permute-start.5) | collective-permute-done | bytes 57376 | tf_op jit(solution)/shard_map/ppermute | solution.py:37
  24.7 3.2 %collective-permute-start.6 = (bf16[14,16,128]{2,1,0:T(8,128)(2,1)S(1)}, bf16[14,16,128]{2,1,0:T(8,128)(2,1)S(1)}, u32[]{:S(2)}, u32[]{:S(2)}) collective-permute-start(bf16[14,16,128]{2,1,0:T(8,128)(2,1)S(1)} %add_convert_fusion.refs_1_), channel_id=1, source_target_pairs={{0,16},{2,18},{4,20},{6,22},{8,24},{10,26},{12,28},{14,30},{16,0},... | collective-permute-start | bytes 172040 | tf_op jit(solution)/shard_map/ppermute | solution.py:37
  27.9 2.8 %collective-permute-done.6.refs_2_ = bf16[14,16,128]{2,1,0:T(8,128)(2,1)S(1)} collective-permute-done((bf16[14,16,128]{2,1,0:T(8,128)(2,1)S(1)}, bf16[14,16,128]{2,1,0:T(8,128)(2,1)S(1)}, u32[]{:S(2)}, u32[]{:S(2)}) %collective-permute-start.6) | collective-permute-done | bytes 57376 | tf_op jit(solution)/shard_map/ppermute | solution.py:37
  30.7 0.0 all-to-all-done.refs_3_
  30.7 0.0 copy-done.1
  30.7 0.8 %adam.1 = bf16[8,18,16,128]{3,2,1,0:T(8,128)(2,1)S(1)} custom-call(s32[14]{0:T(128)S(1)} %copy-done.1, bf16[14,16,128]{2,1,0:T(8,128)(2,1)S(1)} %add_convert_fusion.refs_1_, bf16[14,16,128]{2,1,0:T(8,128)(2,1)S(1)} %collective-permute-done.6.refs_2_, bf16[16,4,16,128]{3,2,1,0:T(8,128)(2,1)S(1)} %all-to-all-done.refs_3_), custom_call_target="tpu_custom_call" | custom-call | tf_op jit(solution)/shard_map/adam/pallas_call | solution.py:329
  31.5 12.1 %all_to_all.10.message = bf16[8,18,16,128]{3,2,1,0:T(8,128)(2,1)S(1)} all-to-all(bf16[8,18,16,128]{3,2,1,0:T(8,128)(2,1)S(1)} %adam.1), channel_id=1, replica_groups={{0,2,4,6,8,10,12,14},{16,18,20,22,24,26,28,30},{1,3,5,7,9,11,13,15},{17..., dimensions={0} | all-to-all | bytes 1179648 | tf_op jit(solution)/shard_map/all_to_all | solution.py:43
  43.6 0.9 %final.1 = (bf16[14,128,128]{2,1,0:T(8,128)(2,1)}, f32[256,128]{1,0:T(8,128)}, f32[256,128]{1,0:T(8,128)}) custom-call(bf16[8,18,16,128]{3,2,1,0:T(8,128)(2,1)S(1)} %all_to_all.10.message, f32[256,128]{1,0:T(8,128)S(1)} %get-tuple-element.28.first_old, f32[256,128]{1,0:T(8,128)S(1)} %get-tuple-element.29.second_old), custom_call_target="tpu_custom_call" | custom-call | tf_op jit(solution)/shard_map/final/pallas_call | solution.py:343
  (1 shorter events, 0.0 us)
Async XLA Ops:
  0.6 4.5 %collective-permute-start = (bf16[128,4096]{1,0:T(8,128)(2,1)}, bf16[128,4096]{1,0:T(8,128)(2,1)S(1)}, u32[]{:S(2)}, u32[]{:S(2)}) collective-permute-start(bf16[128,4096]{1,0:T(8,128)(2,1)} %refs_1_.1), channel_id=1, source_target_pairs={{0,1},{1,0},{2,3},{3,2},{4,5},{5,4},{6,7},{7,6},{8,9},{9,8},{10,11... | collective-permute-start | bytes 3145736 | tf_op jit(solution)/shard_map/ppermute | solution.py:37
  1.2 4.0 %collective-permute-start.1 = (bf16[128,4096]{1,0:T(8,128)(2,1)}, bf16[128,4096]{1,0:T(8,128)(2,1)S(1)}, u32[]{:S(2)}, u32[]{:S(2)}) collective-permute-start(bf16[128,4096]{1,0:T(8,128)(2,1)} %refs_2_.1), channel_id=1, source_target_pairs={{0,1},{1,0},{2,3},{3,2},{4,5},{5,4},{6,7},{7,6},{8,9},{9,8},{10,11... | collective-permute-start | bytes 3145736 | tf_op jit(solution)/shard_map/ppermute | solution.py:37
  1.2 3.9 %copy-start = (s32[14,3]{0,1:T(4,128)S(1)}, s32[14,3]{0,1:T(4,128)}, u32[]{:S(2)}) copy-start(s32[14,3]{0,1:T(4,128)} %param.18) | copy-start | bytes 508
  6.4 11.8 %collective-permute-start.2 = (bf16[2,14,16,128]{3,2,1,0:T(8,128)(2,1)S(1)}, bf16[2,14,16,128]{3,2,1,0:T(8,128)(2,1)S(1)}, u32[]{:S(2)}, u32[]{:S(2)}) collective-permute-start(bf16[2,14,16,128]{3,2,1,0:T(8,128)(2,1)S(1)} %get-tuple-element.21), channel_id=1, source_target_pairs={{0,2},{2,0},{4,6},{6,4},{8,10},{10,8},{12,14},{14,12},{16,18},{18,... | collective-permute-start | bytes 344072 | tf_op jit(solution)/shard_map/ppermute | solution.py:37
  9.4 8.9 %collective-permute-start.3 = (bf16[2,14,16,128]{3,2,1,0:T(8,128)(2,1)S(1)}, bf16[2,14,16,128]{3,2,1,0:T(8,128)(2,1)S(1)}, u32[]{:S(2)}, u32[]{:S(2)}) collective-permute-start(bf16[2,14,16,128]{3,2,1,0:T(8,128)(2,1)S(1)} %get-tuple-element.22), channel_id=1, source_target_pairs={{0,4},{2,6},{4,0},{6,2},{8,12},{10,14},{12,8},{14,10},{16,20},{18,... | collective-permute-start | bytes 344072 | tf_op jit(solution)/shard_map/ppermute | solution.py:37
  10.9 7.4 %collective-permute-start.4 = (bf16[2,14,16,128]{3,2,1,0:T(8,128)(2,1)S(1)}, bf16[2,14,16,128]{3,2,1,0:T(8,128)(2,1)S(1)}, u32[]{:S(2)}, u32[]{:S(2)}) collective-permute-start(bf16[2,14,16,128]{3,2,1,0:T(8,128)(2,1)S(1)} %get-tuple-element.23), channel_id=1, source_target_pairs={{0,6},{2,4},{4,2},{6,0},{8,14},{10,12},{12,10},{14,8},{16,22},{18,... | collective-permute-start | bytes 344072 | tf_op jit(solution)/shard_map/ppermute | solution.py:37
  10.9 19.8 %all-to-all-start = ((bf16[16,4,16,128]{3,2,1,0:T(8,128)(2,1)}), bf16[16,4,16,128]{3,2,1,0:T(8,128)(2,1)S(1)}, u32[]{:S(2)}, u32[]{:S(2)}) async-start(bf16[16,4,16,128]{3,2,1,0:T(8,128)(2,1)} %get-tuple-element.27), calls=%async_computation | async-start | bytes 524288 | tf_op jit(solution)/shard_map/all_to_all | solution.py:314
  18.2 12.5 %copy-start.1 = (s32[14]{0:T(128)S(1)}, s32[14]{0:T(128)}, u32[]{:S(2)}) copy-start(s32[14]{0:T(128)} %refs_0_.1) | copy-start | bytes 172
  18.4 6.3 %collective-permute-start.5 = (bf16[14,16,128]{2,1,0:T(8,128)(2,1)S(1)}, bf16[14,16,128]{2,1,0:T(8,128)(2,1)S(1)}, u32[]{:S(2)}, u32[]{:S(2)}) collective-permute-start(bf16[14,16,128]{2,1,0:T(8,128)(2,1)S(1)} %get-tuple-element.25), channel_id=1, source_target_pairs={{0,8},{2,10},{4,12},{6,14},{8,0},{10,2},{12,4},{14,6},{16,24},{18,... | collective-permute-start | bytes 172040 | tf_op jit(solution)/shard_map/ppermute | solution.py:37
  24.7 6.0 %collective-permute-start.6 = (bf16[14,16,128]{2,1,0:T(8,128)(2,1)S(1)}, bf16[14,16,128]{2,1,0:T(8,128)(2,1)S(1)}, u32[]{:S(2)}, u32[]{:S(2)}) collective-permute-start(bf16[14,16,128]{2,1,0:T(8,128)(2,1)S(1)} %add_convert_fusion.refs_1_), channel_id=1, source_target_pairs={{0,16},{2,18},{4,20},{6,22},{8,24},{10,26},{12,28},{14,30},{16,0},... | collective-permute-start | bytes 172040 | tf_op jit(solution)/shard_map/ppermute | solution.py:37

commit v4 on v3

--- a/solution.py
+++ b/solution.py
@@ -148,29 +148,25 @@
     per_piece = inputs[0].shape[1] // TB if inputs else 1
     me = lax.axis_index("tensor")
     inner = lax.rem(lax.axis_index("dp"), PLANE)
-    group = grouped(tiles)
-
-    def work(step, carry):
-        for k in [step * group + i for i in range(group)]:
-            width = tile_list[0, k]
-            is_down = tile_list[2, k] == 2
-            distance = jnp.bitwise_xor(width // per_piece, me)
-            local = columns(lax.rem(width, per_piece))
-            hidden_side = side[k]
-            wide_side = wide[k]
-            for piece in range(1, pieces):
-                other = jnp.where(is_down, grads[piece - 1][:, local], inputs[piece - 1][:, local])
-                wide_side = jnp.where(distance == piece, other, wide_side)
-            left = jnp.where(is_down, hidden_side, wide_side)
-            right = jnp.where(is_down, wide_side, hidden_side)
-            part[k] = lax.dot_general(left, right, (((0,), (0,)), ((), ())), preferred_element_type=jnp.float32)
-            for distance, ref in enumerate(messages):
-                for half in range(HALVES):
-                    start = pl.multiple_of((half * PLANE + jnp.bitwise_xor(inner, distance)) * SHARE, SHARE)
-                    ref[half, k] = part[k, pl.ds(start, SHARE), :].astype(ref.dtype)
-        return carry
-
-    lax.fori_loop(0, tiles // group, work, 0)
+    listed = tile_list[...]
+
+    for k in range(tiles):
+        width = listed[0, k]
+        is_down = listed[2, k] == 2
+        distance = jnp.bitwise_xor(width // per_piece, me)
+        local = columns(lax.rem(width, per_piece))
+        hidden_side = side[k]
+        wide_side = wide[k]
+        for piece in range(1, pieces):
+            other = jnp.where(is_down, grads[piece - 1][:, local], inputs[piece - 1][:, local])
+            wide_side = jnp.where(distance == piece, other, wide_side)
+        left = jnp.where(is_down, hidden_side, wide_side)
+        right = jnp.where(is_down, wide_side, hidden_side)
+        part[k] = lax.dot_general(left, right, (((0,), (0,)), ((), ())), preferred_element_type=jnp.float32)
+        for distance, ref in enumerate(messages):
+            for half in range(HALVES):
+                start = pl.multiple_of((half * PLANE + jnp.bitwise_xor(inner, distance)) * SHARE, SHARE)
+                ref[half, k] = part[k, pl.ds(start, SHARE), :].astype(ref.dtype)
 
 
 def plane_kernel(*refs):
@@ -192,29 +188,25 @@
     spare = INNER * CAP
     for index in range(spare):
         found[index] = -1
-    group = grouped(tiles)
-
-    def work(step, carry):
-        for k in [step * group + i for i in range(group)]:
-            parts = [ref[k].astype(jnp.float32) for ref in sums]
-            while len(parts) > 1:
-                parts = [parts[i] + parts[i + 1] for i in range(0, len(parts), 2)]
-            grad = parts[0]
-            total[k] = grad
-            owner, slot = slots[k] // CAP, lax.rem(slots[k], CAP)
-            found[jnp.where(owner // INNER == plane, lax.rem(slots[k], spare), spare)] = k
-            first_old = states[owner, slot].astype(jnp.float32)
-            second_old = states[owner, CAP + slot].astype(jnp.float32)
-            first = BETA_FIRST * first_old + (1.0 - BETA_FIRST) * grad
-            second = BETA_SECOND * second_old + (1.0 - BETA_SECOND) * grad * grad
-            first_hat = first / (1.0 - BETA_FIRST**STEP)
-            second_hat = second / (1.0 - BETA_SECOND**STEP)
-            update = (first_hat / (jnp.sqrt(second_hat) + EPSILON)).astype(jnp.bfloat16)
-            for part in range(INNER):
-                message[part, k] = update
-        return carry
-
-    lax.fori_loop(0, tiles // group, work, 0)
+    listed = [slots[0, k] for k in range(tiles)]
+
+    for k in range(tiles):
+        parts = [ref[k].astype(jnp.float32) for ref in sums]
+        while len(parts) > 1:
+            parts = [parts[i] + parts[i + 1] for i in range(0, len(parts), 2)]
+        grad = parts[0]
+        total[k] = grad
+        owner, slot = listed[k] // CAP, lax.rem(listed[k], CAP)
+        found[jnp.where(owner // INNER == plane, lax.rem(listed[k], spare), spare)] = k
+        first_old = states[owner, slot].astype(jnp.float32)
+        second_old = states[owner, CAP + slot].astype(jnp.float32)
+        first = BETA_FIRST * first_old + (1.0 - BETA_FIRST) * grad
+        second = BETA_SECOND * second_old + (1.0 - BETA_SECOND) * grad * grad
+        first_hat = first / (1.0 - BETA_FIRST**STEP)
+        second_hat = second / (1.0 - BETA_SECOND**STEP)
+        update = (first_hat / (jnp.sqrt(second_hat) + EPSILON)).astype(jnp.bfloat16)
+        for part in range(INNER):
+            message[part, k] = update
     for part in range(INNER):
         for slot in range(CAP):
             k = found[part * CAP + slot]
@@ -302,7 +294,7 @@
         lambda *refs: partial_kernel(pieces, *refs),
         out_shape=(jax.ShapeDtypeStruct(halves, jnp.float32),)
         + (jax.ShapeDtypeStruct(halves, jnp.bfloat16),) * (PLANE - 1),
-        in_specs=[SMEM] + [VMEM] * (2 * pieces),
+        in_specs=[VMEM] * (2 * pieces + 1),
         out_specs=(VMEM,) * PLANE,
         scratch_shapes=[pltpu.VMEM((tiles, TB, TB), jnp.float32)],
         compiler_params=PARAMS,
@@ -329,7 +321,7 @@
     message = pl.pallas_call(
         lambda *refs: adam_kernel(outer, *refs),
         out_shape=jax.ShapeDtypeStruct((INNER, tiles + 2 * CAP, SHARE, TB), jnp.bfloat16),
-        in_specs=[SMEM] + [VMEM] * (outer + 1),
+        in_specs=[VMEM] * (outer + 2),
         out_specs=VMEM,
         scratch_shapes=[
             pltpu.VMEM((tiles, SHARE, TB), jnp.float32),
@@ -337,7 +329,7 @@
         ],
         compiler_params=PARAMS,
         name="adam",
-    )(tile_slots, *sums, states)
+    )(tile_slots[None], *sums, states)
     message = exchange(message)
 
     update_tiles, first_moment, second_moment = pl.pallas_call(

time: 44.9 us -> 43.7 us (0.973)
  Pallas kernels: 6.89 us -> 5.78 us
    pallas_call x1, Pallas kernels: 1.25 us -> 0.62 us  [body(): pl.pallas_call(lambda *refs: partial_kernel(pieces, *refs), out_shape=(ja...]
    pallas_call x1, Pallas kernels: 0.81 us -> 0.31 us  [body(): pl.pallas_call(lambda *refs: adam_kernel(outer, *refs), out_shape=jax.Sha...]
where the time goes in v4:
time: 43.7 us; the launch traced here: 43.4 us
  starting transfers between devices  17.7 us (41%)
  blocking collectives  12.1 us (28%)
  waiting for transfers between devices  7.11 us (16%)
  Pallas kernels  5.78 us (13%)
  between operations  0.71 us (2%)
    all_to_all x1, blocking collectives, exchange(): lax.all_to_all(array, 'dp', 0, 0, tiled=True, axis_index_groups=groups)  12.1 us
    ppermute x7, starting transfers between devices, partner(): return lax.ppermute(array, axis, [(i, i ^ distance) for i in range(count)])  10.3 us
    all_to_all x1, starting transfers between devices, body(): states = lax.all_to_all(state_message, 'dp', 0, 0, tiled=True)  7.34 us
    ppermute x7, waiting for transfers between devices, partner(): return lax.ppermute(array, axis, [(i, i ^ distance) for i in range(count)])  7.11 us
    pallas_call x1, Pallas kernels, body(): pl.pallas_call(prepare_kernel, out_shape=(kept_whole, kept_whole, kept_ol...  3.87 us
    pallas_call x1, Pallas kernels, body(): pl.pallas_call(final_kernel, out_shape=(jax.ShapeDtypeStruct((tiles, TB,...  0.9 us
  transfers between devices with their start and end apart: 8, of which 2 were waited for; matrix products, arithmetic and copies ran while one was open for 0% of the time, Pallas kernels for 9%

profile of v4, /device:TPU:0, one launch (start us, length us, event | category | flops | bytes accessed | tf_op | source)
XLA Modules:
  0.0 43.4 jit_solution(17330073827971847080)
XLA Ops:
  0.6 0.5 %collective-permute-start = (bf16[128,4096]{1,0:T(8,128)(2,1)}, bf16[128,4096]{1,0:T(8,128)(2,1)S(1)}, u32[]{:S(2)}, u32[]{:S(2)}) collective-permute-start(bf16[128,4096]{1,0:T(8,128)(2,1)} %refs_1_.1), channel_id=1, source_target_pairs={{0,1},{1,0},{2,3},{3,2},{4,5},{5,4},{6,7},{7,6},{8,9},{9,8},{10,11... | collective-permute-start | bytes 3145736 | tf_op jit(solution)/shard_map/ppermute | solution.py:37
  1.2 0.1 collective-permute-start.1
  1.2 0.0 copy-start
  1.2 3.9 %prepare.1 = (bf16[14,128,128]{2,1,0:T(8,128)(2,1)S(1)}, bf16[14,128,128]{2,1,0:T(8,128)(2,1)S(1)}, f32[256,128]{1,0:T(8,128)S(1)}, f32[256,128]{1,0:T(8,128)S(1)}, bf16[16,4,16,128]{3,2,1,0:T(8,128)(2,1)}) custom-call(s32[3,14]{1,0:T(4,128)} %bitcast.26, bf16[128,4096]{1,0:T(8,128)(2,1)} %refs_1_.1, bf16[128,4096]{1,0:T(8,128)(2,1)} %refs_2_.1, ...), custom_call_target="tpu_custom_call" | custom-call | tf_op jit(solution)/shard_map/prepare/pallas_call | solution.py:263
  5.1 0.0 collective-permute-done.refs_3_
  5.1 0.0 collective-permute-done.1.refs_4_
  5.1 0.0 copy-done
  5.2 0.6 %partials.1 = (f32[2,14,16,128]{3,2,1,0:T(8,128)S(1)}, bf16[2,14,16,128]{3,2,1,0:T(8,128)(2,1)S(1)}, bf16[2,14,16,128]{3,2,1,0:T(8,128)(2,1)S(1)}, bf16[2,14,16,128]{3,2,1,0:T(8,128)(2,1)S(1)}) custom-call(s32[3,14]{1,0:T(4,128)S(1)} %bitcast.27, bf16[14,128,128]{2,1,0:T(8,128)(2,1)S(1)} %get-tuple-element.18.refs_1_, ...), custom_call_target="tpu_custom_call" | custom-call | tf_op jit(solution)/shard_map/partials/pallas_call | solution.py:293
  5.8 3.0 %collective-permute-start.2 = (bf16[2,14,16,128]{3,2,1,0:T(8,128)(2,1)S(1)}, bf16[2,14,16,128]{3,2,1,0:T(8,128)(2,1)S(1)}, u32[]{:S(2)}, u32[]{:S(2)}) collective-permute-start(bf16[2,14,16,128]{3,2,1,0:T(8,128)(2,1)S(1)} %get-tuple-element.21), channel_id=1, source_target_pairs={{0,2},{2,0},{4,6},{6,4},{8,10},{10,8},{12,14},{14,12},{16,18},{18,... | collective-permute-start | bytes 344072 | tf_op jit(solution)/shard_map/ppermute | solution.py:37
  8.7 1.5 %collective-permute-start.3 = (bf16[2,14,16,128]{3,2,1,0:T(8,128)(2,1)S(1)}, bf16[2,14,16,128]{3,2,1,0:T(8,128)(2,1)S(1)}, u32[]{:S(2)}, u32[]{:S(2)}) collective-permute-start(bf16[2,14,16,128]{3,2,1,0:T(8,128)(2,1)S(1)} %get-tuple-element.22), channel_id=1, source_target_pairs={{0,4},{2,6},{4,0},{6,2},{8,12},{10,14},{12,8},{14,10},{16,20},{18,... | collective-permute-start | bytes 344072 | tf_op jit(solution)/shard_map/ppermute | solution.py:37
  10.3 0.0 collective-permute-start.4
  10.3 7.3 %all-to-all-start = ((bf16[16,4,16,128]{3,2,1,0:T(8,128)(2,1)}), bf16[16,4,16,128]{3,2,1,0:T(8,128)(2,1)S(1)}, u32[]{:S(2)}, u32[]{:S(2)}) async-start(bf16[16,4,16,128]{3,2,1,0:T(8,128)(2,1)} %get-tuple-element.27), calls=%async_computation | async-start | bytes 524288 | tf_op jit(solution)/shard_map/all_to_all | solution.py:306
  17.6 0.0 copy-start.1
  17.7 0.0 collective-permute-done.2.refs_1_
  17.7 0.0 collective-permute-done.3.refs_2_
  17.7 0.0 collective-permute-done.4.refs_3_
  17.7 0.1 plane.1
  17.8 2.0 %collective-permute-start.5 = (bf16[14,16,128]{2,1,0:T(8,128)(2,1)S(1)}, bf16[14,16,128]{2,1,0:T(8,128)(2,1)S(1)}, u32[]{:S(2)}, u32[]{:S(2)}) collective-permute-start(bf16[14,16,128]{2,1,0:T(8,128)(2,1)S(1)} %get-tuple-element.25), channel_id=1, source_target_pairs={{0,8},{2,10},{4,12},{6,14},{8,0},{10,2},{12,4},{14,6},{16,24},{18,... | collective-permute-start | bytes 172040 | tf_op jit(solution)/shard_map/ppermute | solution.py:37
  19.8 4.3 %collective-permute-done.5 = bf16[14,16,128]{2,1,0:T(8,128)(2,1)S(1)} collective-permute-done((bf16[14,16,128]{2,1,0:T(8,128)(2,1)S(1)}, bf16[14,16,128]{2,1,0:T(8,128)(2,1)S(1)}, u32[]{:S(2)}, u32[]{:S(2)}) %collective-permute-start.5) | collective-permute-done | bytes 57376 | tf_op jit(solution)/shard_map/ppermute | solution.py:37
  24.1 3.2 %collective-permute-start.6 = (bf16[14,16,128]{2,1,0:T(8,128)(2,1)S(1)}, bf16[14,16,128]{2,1,0:T(8,128)(2,1)S(1)}, u32[]{:S(2)}, u32[]{:S(2)}) collective-permute-start(bf16[14,16,128]{2,1,0:T(8,128)(2,1)S(1)} %add_convert_fusion.refs_1_), channel_id=1, source_target_pairs={{0,16},{2,18},{4,20},{6,22},{8,24},{10,26},{12,28},{14,30},{16,0},... | collective-permute-start | bytes 172040 | tf_op jit(solution)/shard_map/ppermute | solution.py:37
  27.3 2.8 %collective-permute-done.6.refs_2_ = bf16[14,16,128]{2,1,0:T(8,128)(2,1)S(1)} collective-permute-done((bf16[14,16,128]{2,1,0:T(8,128)(2,1)S(1)}, bf16[14,16,128]{2,1,0:T(8,128)(2,1)S(1)}, u32[]{:S(2)}, u32[]{:S(2)}) %collective-permute-start.6) | collective-permute-done | bytes 57376 | tf_op jit(solution)/shard_map/ppermute | solution.py:37
  30.1 0.0 all-to-all-done.refs_3_
  30.1 0.0 copy-done.1
  30.1 0.3 adam.1
  30.4 12.1 %all_to_all.10.message = bf16[8,18,16,128]{3,2,1,0:T(8,128)(2,1)S(1)} all-to-all(bf16[8,18,16,128]{3,2,1,0:T(8,128)(2,1)S(1)} %adam.1), channel_id=1, replica_groups={{0,2,4,6,8,10,12,14},{16,18,20,22,24,26,28,30},{1,3,5,7,9,11,13,15},{17..., dimensions={0} | all-to-all | bytes 1179648 | tf_op jit(solution)/shard_map/all_to_all | solution.py:43
  42.5 0.9 %final.1 = (bf16[14,128,128]{2,1,0:T(8,128)(2,1)}, f32[256,128]{1,0:T(8,128)}, f32[256,128]{1,0:T(8,128)}) custom-call(bf16[8,18,16,128]{3,2,1,0:T(8,128)(2,1)S(1)} %all_to_all.10.message, f32[256,128]{1,0:T(8,128)S(1)} %get-tuple-element.28.first_old, f32[256,128]{1,0:T(8,128)S(1)} %get-tuple-element.29.second_old), custom_call_target="tpu_custom_call" | custom-call | tf_op jit(solution)/shard_map/final/pallas_call | solution.py:335
  (1 shorter events, 0.0 us)
Async XLA Ops:
  0.6 4.5 %collective-permute-start = (bf16[128,4096]{1,0:T(8,128)(2,1)}, bf16[128,4096]{1,0:T(8,128)(2,1)S(1)}, u32[]{:S(2)}, u32[]{:S(2)}) collective-permute-start(bf16[128,4096]{1,0:T(8,128)(2,1)} %refs_1_.1), channel_id=1, source_target_pairs={{0,1},{1,0},{2,3},{3,2},{4,5},{5,4},{6,7},{7,6},{8,9},{9,8},{10,11... | collective-permute-start | bytes 3145736 | tf_op jit(solution)/shard_map/ppermute | solution.py:37
  1.2 4.0 %collective-permute-start.1 = (bf16[128,4096]{1,0:T(8,128)(2,1)}, bf16[128,4096]{1,0:T(8,128)(2,1)S(1)}, u32[]{:S(2)}, u32[]{:S(2)}) collective-permute-start(bf16[128,4096]{1,0:T(8,128)(2,1)} %refs_2_.1), channel_id=1, source_target_pairs={{0,1},{1,0},{2,3},{3,2},{4,5},{5,4},{6,7},{7,6},{8,9},{9,8},{10,11... | collective-permute-start | bytes 3145736 | tf_op jit(solution)/shard_map/ppermute | solution.py:37
  1.2 3.9 %copy-start = (s32[14,3]{0,1:T(4,128)S(1)}, s32[14,3]{0,1:T(4,128)}, u32[]{:S(2)}) copy-start(s32[14,3]{0,1:T(4,128)} %param.18) | copy-start | bytes 508
  5.8 11.9 %collective-permute-start.2 = (bf16[2,14,16,128]{3,2,1,0:T(8,128)(2,1)S(1)}, bf16[2,14,16,128]{3,2,1,0:T(8,128)(2,1)S(1)}, u32[]{:S(2)}, u32[]{:S(2)}) collective-permute-start(bf16[2,14,16,128]{3,2,1,0:T(8,128)(2,1)S(1)} %get-tuple-element.21), channel_id=1, source_target_pairs={{0,2},{2,0},{4,6},{6,4},{8,10},{10,8},{12,14},{14,12},{16,18},{18,... | collective-permute-start | bytes 344072 | tf_op jit(solution)/shard_map/ppermute | solution.py:37
  8.7 8.9 %collective-permute-start.3 = (bf16[2,14,16,128]{3,2,1,0:T(8,128)(2,1)S(1)}, bf16[2,14,16,128]{3,2,1,0:T(8,128)(2,1)S(1)}, u32[]{:S(2)}, u32[]{:S(2)}) collective-permute-start(bf16[2,14,16,128]{3,2,1,0:T(8,128)(2,1)S(1)} %get-tuple-element.22), channel_id=1, source_target_pairs={{0,4},{2,6},{4,0},{6,2},{8,12},{10,14},{12,8},{14,10},{16,20},{18,... | collective-permute-start | bytes 344072 | tf_op jit(solution)/shard_map/ppermute | solution.py:37
  10.3 7.4 %collective-permute-start.4 = (bf16[2,14,16,128]{3,2,1,0:T(8,128)(2,1)S(1)}, bf16[2,14,16,128]{3,2,1,0:T(8,128)(2,1)S(1)}, u32[]{:S(2)}, u32[]{:S(2)}) collective-permute-start(bf16[2,14,16,128]{3,2,1,0:T(8,128)(2,1)S(1)} %get-tuple-element.23), channel_id=1, source_target_pairs={{0,6},{2,4},{4,2},{6,0},{8,14},{10,12},{12,10},{14,8},{16,22},{18,... | collective-permute-start | bytes 344072 | tf_op jit(solution)/shard_map/ppermute | solution.py:37
  10.3 19.8 %all-to-all-start = ((bf16[16,4,16,128]{3,2,1,0:T(8,128)(2,1)}), bf16[16,4,16,128]{3,2,1,0:T(8,128)(2,1)S(1)}, u32[]{:S(2)}, u32[]{:S(2)}) async-start(bf16[16,4,16,128]{3,2,1,0:T(8,128)(2,1)} %get-tuple-element.27), calls=%async_computation | async-start | bytes 524288 | tf_op jit(solution)/shard_map/all_to_all | solution.py:306
  17.6 12.4 %copy-start.1 = (s32[14]{0:T(128)S(1)}, s32[14]{0:T(128)}, u32[]{:S(2)}) copy-start(s32[14]{0:T(128)} %param.19) | copy-start | bytes 172
  17.8 6.3 %collective-permute-start.5 = (bf16[14,16,128]{2,1,0:T(8,128)(2,1)S(1)}, bf16[14,16,128]{2,1,0:T(8,128)(2,1)S(1)}, u32[]{:S(2)}, u32[]{:S(2)}) collective-permute-start(bf16[14,16,128]{2,1,0:T(8,128)(2,1)S(1)} %get-tuple-element.25), channel_id=1, source_target_pairs={{0,8},{2,10},{4,12},{6,14},{8,0},{10,2},{12,4},{14,6},{16,24},{18,... | collective-permute-start | bytes 172040 | tf_op jit(solution)/shard_map/ppermute | solution.py:37
  24.1 6.0 %collective-permute-start.6 = (bf16[14,16,128]{2,1,0:T(8,128)(2,1)S(1)}, bf16[14,16,128]{2,1,0:T(8,128)(2,1)S(1)}, u32[]{:S(2)}, u32[]{:S(2)}) collective-permute-start(bf16[14,16,128]{2,1,0:T(8,128)(2,1)S(1)} %add_convert_fusion.refs_1_), channel_id=1, source_target_pairs={{0,16},{2,18},{4,20},{6,22},{8,24},{10,26},{12,28},{14,30},{16,0},... | collective-permute-start | bytes 172040 | tf_op jit(solution)/shard_map/ppermute | solution.py:37

commit v5 on v4

--- a/solution.py
+++ b/solution.py
@@ -6,6 +6,7 @@
 from jax.sharding import PartitionSpec as P
 
 CAP = 2
+RAISE = 8.0
 TB = 128
 STEP = 10
 INNER = 8
@@ -23,13 +24,20 @@
 FIELDS = 2 * CAP
 PLANE = 4
 HALVES = INNER // PLANE
-COST = pl.CostEstimate(flops=10**11, bytes_accessed=10**8, transcendentals=0)
 PARAMS = pltpu.CompilerParams(vmem_limit_bytes=32 * 1024 * 1024)
 WIDE_PARAMS = pltpu.CompilerParams(vmem_limit_bytes=32 * 1024 * 1024)
 
 
 def pinned(array):
     return pltpu.with_memory_space_constraint(array, pltpu.HBM)
+
+
+def narrow(array):
+    return lax.optimization_barrier((array * RAISE).astype(jnp.float16))
+
+
+def widen(array):
+    return array.astype(jnp.float32) * (1.0 / RAISE)
 
 
 def partner(array, axis, distance):
@@ -66,7 +74,6 @@
     targets, held, tile_list, sems, table_sems = refs[17:20], refs[20:26], *refs[26:]
     tiles = side.shape[0]
     per_piece = layer_input.shape[1] // TB
-    owners = message.shape[0]
 
     tile_copy, *copies = [
         pltpu.make_async_copy(source, target, table_sems.at[i])
@@ -111,9 +118,7 @@
             old[rows, :] = picked * jnp.where(odd, scale[1:2, block : block + 1], scale[0:1, block : block + 1])
         for part in range(INNER):
             for slot in range(CAP):
-                sent = old[pl.ds(part * SHARE * CAP + slot, SHARE, stride=CAP), :].astype(jnp.bfloat16)
-                for owner in range(part, owners, INNER):
-                    message[owner, which * CAP + slot] = sent
+                message[part, which * CAP + slot] = old[pl.ds(part * SHARE * CAP + slot, SHARE, stride=CAP), :]
 
     group = grouped(tiles)
 
@@ -139,16 +144,21 @@
 
 
 def partial_kernel(pieces, *refs):
-    tile_list, side, wide = refs[:3]
-    inputs = refs[3 : 2 + pieces]
-    grads = refs[2 + pieces : 1 + 2 * pieces]
-    messages = refs[1 + 2 * pieces : 1 + 2 * pieces + PLANE]
+    tile_list, side, wide, states = refs[:4]
+    inputs = refs[4 : 3 + pieces]
+    grads = refs[3 + pieces : 2 + 2 * pieces]
+    messages = refs[2 + 2 * pieces : 2 + 2 * pieces + PLANE]
     part = refs[-1]
     tiles = side.shape[0]
     per_piece = inputs[0].shape[1] // TB if inputs else 1
     me = lax.axis_index("tensor")
     inner = lax.rem(lax.axis_index("dp"), PLANE)
     listed = tile_list[...]
+
+    for distance in range(1, PLANE):
+        for half in range(HALVES):
+            theirs = half * PLANE + jnp.bitwise_xor(inner, distance)
+            messages[distance][half, pl.ds(tiles, FIELDS)] = states[theirs]
 
     for k in range(tiles):
         width = listed[0, k]
@@ -166,65 +176,77 @@
         for distance, ref in enumerate(messages):
             for half in range(HALVES):
                 start = pl.multiple_of((half * PLANE + jnp.bitwise_xor(inner, distance)) * SHARE, SHARE)
-                ref[half, k] = part[k, pl.ds(start, SHARE), :].astype(ref.dtype)
-
-
-def plane_kernel(*refs):
-    arrived, (kept, sent) = refs[:PLANE], refs[PLANE:]
-    half = lax.rem(lax.axis_index("dp") // PLANE, HALVES)
+                ref[half, k] = part[k, pl.ds(start, SHARE), :]
+
+
+def plane_kernel(states, *refs):
+    arrived, (kept, sent, near, far) = refs[:PLANE], refs[PLANE:]
+    tiles = kept.shape[0]
+    me = lax.axis_index("dp")
+    inner, half = lax.rem(me, PLANE), lax.rem(me // PLANE, HALVES)
     for which, ref in ((half, kept), (HALVES - 1 - half, sent)):
         summed = arrived[0][which]
         for piece in arrived[1:]:
-            summed = summed + piece[which].astype(jnp.float32)
-        ref[...] = summed.astype(ref.dtype)
-
-
-def adam_kernel(outer, *refs):
+            summed = summed + piece[which, pl.ds(0, tiles)]
+        ref[pl.ds(0, tiles)] = summed
+    for distance in range(PLANE):
+        for which, targets in ((half, ((near, 0),)), (HALVES - 1 - half, ((far, 0), (sent, tiles)))):
+            if distance == 0:
+                found = states[which * PLANE + inner]
+            else:
+                found = arrived[distance][which, pl.ds(tiles, FIELDS)]
+            for target, start in targets:
+                target[pl.ds(start + distance * FIELDS, FIELDS)] = found
+
+
+def adam_kernel(outer, planes, *refs):
     slots = refs[0]
     sums = refs[1 : 1 + outer]
-    states, message, total, found = refs[1 + outer :]
+    arrived = refs[1 + outer : 1 + outer + planes]
+    message, total, states, found = refs[1 + outer + planes :]
     tiles = sums[0].shape[0]
-    plane = lax.axis_index("dp") // INNER
+    me = lax.axis_index("dp")
+    plane = me // INNER
+    for distance, ref in enumerate(arrived):
+        states[distance] = ref[pl.ds(ref.shape[0] - PLANE * FIELDS, PLANE * FIELDS)]
     spare = INNER * CAP
     for index in range(spare):
         found[index] = -1
     listed = [slots[0, k] for k in range(tiles)]
 
     for k in range(tiles):
-        parts = [ref[k].astype(jnp.float32) for ref in sums]
+        parts = [ref[k] for ref in sums]
         while len(parts) > 1:
             parts = [parts[i] + parts[i + 1] for i in range(0, len(parts), 2)]
         grad = parts[0]
         total[k] = grad
         owner, slot = listed[k] // CAP, lax.rem(listed[k], CAP)
         found[jnp.where(owner // INNER == plane, lax.rem(listed[k], spare), spare)] = k
-        first_old = states[owner, slot].astype(jnp.float32)
-        second_old = states[owner, CAP + slot].astype(jnp.float32)
+        away = jnp.bitwise_xor(owner // PLANE, me // PLANE)
+        field = jnp.bitwise_xor(lax.rem(owner, PLANE), lax.rem(me, PLANE)) * FIELDS + slot
+        first_old = states[away, field]
+        second_old = states[away, field + CAP]
         first = BETA_FIRST * first_old + (1.0 - BETA_FIRST) * grad
         second = BETA_SECOND * second_old + (1.0 - BETA_SECOND) * grad * grad
         first_hat = first / (1.0 - BETA_FIRST**STEP)
         second_hat = second / (1.0 - BETA_SECOND**STEP)
         update = (first_hat / (jnp.sqrt(second_hat) + EPSILON)).astype(jnp.bfloat16)
         for part in range(INNER):
-            message[part, k] = update
+            message[part, k] = update.astype(jnp.float32)
     for part in range(INNER):
         for slot in range(CAP):
             k = found[part * CAP + slot]
             grad = total[jnp.maximum(k, 0)]
             grad = jnp.where(k >= 0, grad, jnp.zeros_like(grad))
-            coarse = grad.astype(jnp.bfloat16)
-            message[part, tiles + 2 * slot] = coarse
-            message[part, tiles + 2 * slot + 1] = (grad - coarse.astype(jnp.float32)).astype(jnp.bfloat16)
+            message[part, tiles + slot] = grad
 
 
 def final_kernel(message, first_old, second_old, update_tiles, first_moment, second_moment, total):
     tiles = update_tiles.shape[0]
     for part in range(INNER):
-        update_tiles[:, pl.ds(part * SHARE, SHARE), :] = message[part, pl.ds(0, tiles)]
+        update_tiles[:, pl.ds(part * SHARE, SHARE), :] = message[part, pl.ds(0, tiles)].astype(jnp.bfloat16)
         for slot in range(CAP):
-            coarse, fine = message[part, tiles + 2 * slot], message[part, tiles + 2 * slot + 1]
-            grad = coarse.astype(jnp.float32) + fine.astype(jnp.float32)
-            total[pl.ds(part * SHARE * CAP + slot, SHARE, stride=CAP), :] = grad
+            total[pl.ds(part * SHARE * CAP + slot, SHARE, stride=CAP), :] = message[part, tiles + slot]
     grad = total[...]
     first_moment[...] = BETA_FIRST * first_old[...] + (1.0 - BETA_FIRST) * grad
     second_moment[...] = BETA_SECOND * second_old[...] + (1.0 - BETA_SECOND) * grad * grad
@@ -262,7 +284,7 @@
     scale = pltpu.VMEM(first_absmax.shape[1:], jnp.float32)
     side, wide, first_old, second_old, state_message = pl.pallas_call(
         prepare_kernel,
-        out_shape=(kept_whole, kept_whole, kept_old, kept_old, pltpu.VMEM((owners, FIELDS, SHARE, TB), jnp.bfloat16)),
+        out_shape=(kept_whole, kept_whole, kept_old, kept_old, pltpu.VMEM((INNER, FIELDS, SHARE, TB), jnp.float32)),
         in_specs=[HBM] * 12,
         out_specs=(VMEM,) * 5,
         scratch_shapes=[block, block, block, codes, codes, scale, scale, levels, levels]
@@ -289,48 +311,59 @@
         ),
     )
 
+    state_message = widen(narrow(state_message))
     halves = (HALVES, tiles, SHARE, TB)
     messages = pl.pallas_call(
         lambda *refs: partial_kernel(pieces, *refs),
         out_shape=(jax.ShapeDtypeStruct(halves, jnp.float32),)
-        + (jax.ShapeDtypeStruct(halves, jnp.bfloat16),) * (PLANE - 1),
-        in_specs=[VMEM] * (2 * pieces + 1),
+        + (jax.ShapeDtypeStruct((HALVES, tiles + FIELDS, SHARE, TB), jnp.float32),) * (PLANE - 1),
+        in_specs=[VMEM] * (2 * pieces + 2),
         out_specs=(VMEM,) * PLANE,
         scratch_shapes=[pltpu.VMEM((tiles, TB, TB), jnp.float32)],
         compiler_params=PARAMS,
         name="partials",
-    )(tile_list, side, wide, *inputs, *grads)
-    arrived = [messages[0]] + [partner(messages[r], "dp", r) for r in range(1, PLANE)]
-
-    state_message = lax.optimization_barrier((state_message, messages[0]))[0]
-    states = lax.all_to_all(state_message, "dp", 0, 0, tiled=True)
+    )(tile_list, side, wide, state_message, *inputs, *grads)
+    arrived = [messages[0]] + [widen(partner(narrow(messages[r]), "dp", r)) for r in range(1, PLANE)]
 
     share = (tiles, SHARE, TB)
-    kept, sent = pl.pallas_call(
+    fields = PLANE * FIELDS
+    kept, sent, near, far = pl.pallas_call(
         plane_kernel,
-        out_shape=(jax.ShapeDtypeStruct(share, jnp.float32), jax.ShapeDtypeStruct(share, jnp.bfloat16)),
-        in_specs=[VMEM] * PLANE,
-        out_specs=(VMEM, VMEM),
+        out_shape=(
+            jax.ShapeDtypeStruct(share, jnp.float32),
+            jax.ShapeDtypeStruct((tiles + fields, SHARE, TB), jnp.float32),
+            jax.ShapeDtypeStruct((fields, SHARE, TB), jnp.float32),
+            jax.ShapeDtypeStruct((fields, SHARE, TB), jnp.float32),
+        ),
+        in_specs=[VMEM] * (PLANE + 1),
+        out_specs=(VMEM,) * 4,
         compiler_params=PARAMS,
-        cost_estimate=COST,
         name="plane",
-    )(*arrived)
-    summed = (kept + partner(sent, "dp", PLANE).astype(jnp.float32)).astype(jnp.bfloat16)
-    sums = [summed] + [partner(summed, "dp", r * INNER) for r in range(1, outer)]
+    )(state_message, *arrived)
+    planes = owners // PLANE
+    near16, far16 = narrow(near), narrow(far)
+    beside = widen(partner(narrow(sent), "dp", PLANE))
+    distant = [partner(far16 if p % HALVES else near16, "dp", p * PLANE) for p in range(2, planes)]
+    summed = narrow(kept + beside[:tiles])
+    sums = [partner(summed, "dp", r * INNER) for r in range(1, outer)]
+    sums, distant = lax.optimization_barrier((sums, distant))
+    states = [near, beside, *map(widen, distant)]
+    sums = [widen(summed), *map(widen, sums)]
 
     message = pl.pallas_call(
-        lambda *refs: adam_kernel(outer, *refs),
-        out_shape=jax.ShapeDtypeStruct((INNER, tiles + 2 * CAP, SHARE, TB), jnp.bfloat16),
-        in_specs=[VMEM] * (outer + 2),
+        lambda *refs: adam_kernel(outer, planes, *refs),
+        out_shape=jax.ShapeDtypeStruct((INNER, tiles + CAP, SHARE, TB), jnp.float32),
+        in_specs=[VMEM] * (outer + planes + 1),
         out_specs=VMEM,
         scratch_shapes=[
             pltpu.VMEM((tiles, SHARE, TB), jnp.float32),
+            pltpu.VMEM((planes, fields, SHARE, TB), jnp.float32),
             pltpu.SMEM((INNER * CAP + 1,), jnp.int32),
         ],
         compiler_params=PARAMS,
         name="adam",
-    )(tile_slots[None], *sums, states)
-    message = exchange(message)
+    )(tile_slots[None], *sums, *states)
+    message = widen(exchange(narrow(message)))
 
     update_tiles, first_moment, second_moment = pl.pallas_call(
         final_kernel,

time: 43.7 us -> 44.4 us (1.016)
  waiting for transfers between devices: 7.11 us -> 13.6 us
  starting transfers between devices: 17.7 us -> 12.5 us
  blocking collectives: 12.1 us -> 11.4 us
  Pallas kernels: 5.78 us -> 5.17 us
  other arithmetic: 0.02 us -> 0.62 us
    all_to_all x1 -> x0, starting transfers between devices: 7.34 us -> none  [body(): states = lax.all_to_all(state_message, 'dp', 0, 0, tiled=True)]
    ppermute x7 -> x9, waiting for transfers between devices: 7.11 us -> 13.6 us  [partner(): return lax.ppermute(array, axis, [(i, i ^ distance) for i in range(count)])]
    ppermute x7 -> x9, starting transfers between devices: 10.3 us -> 12.5 us  [partner(): return lax.ppermute(array, axis, [(i, i ^ distance) for i in range(count)])]
    pallas_call x1, Pallas kernels: 3.87 us -> 3.17 us  [body(): pl.pallas_call(prepare_kernel, out_shape=(kept_whole, kept_whole, kept_ol...]
    all_to_all x1, blocking collectives: 12.1 us -> 11.4 us  [exchange(): lax.all_to_all(array, 'dp', 0, 0, tiled=True, axis_index_groups=groups)]
  transfers between devices with their start and end apart: 8 -> 9, of which waited for: 2 -> 7; matrix products, arithmetic and copies ran while one was open for 0% -> 1% of each run, Pallas kernels for 9% -> 7%
where the time goes in v5:
time: 44.4 us; the launch traced here: 44.1 us
  waiting for transfers between devices  13.6 us (31%)
  starting transfers between devices  12.5 us (28%)
  blocking collectives  11.4 us (26%)
  Pallas kernels  5.17 us (12%)
  between operations  0.8 us (2%)
  other arithmetic  0.62 us (1%)
    ppermute x9, waiting for transfers between devices, partner(): return lax.ppermute(array, axis, [(i, i ^ distance) for i in range(count)])  13.6 us
    ppermute x9, starting transfers between devices, partner(): return lax.ppermute(array, axis, [(i, i ^ distance) for i in range(count)])  12.5 us
    all_to_all x1, blocking collectives, exchange(): lax.all_to_all(array, 'dp', 0, 0, tiled=True, axis_index_groups=groups)  11.4 us
    pallas_call x1, Pallas kernels, body(): pl.pallas_call(prepare_kernel, out_shape=(kept_whole, kept_whole, kept_ol...  3.17 us
    pallas_call x1, Pallas kernels, body(): pl.pallas_call(final_kernel, out_shape=(jax.ShapeDtypeStruct((tiles, TB,...  0.91 us
  transfers between devices with their start and end apart: 9, of which 7 were waited for; matrix products, arithmetic and copies ran while one was open for 1% of the time, Pallas kernels for 7%

profile of v5, /device:TPU:0, one launch (start us, length us, event | category | flops | bytes accessed | tf_op | source)
XLA Modules:
  0.0 44.1 jit_solution(6856527970784240954)
XLA Ops:
  0.6 0.5 %collective-permute-start = (bf16[128,4096]{1,0:T(8,128)(2,1)}, bf16[128,4096]{1,0:T(8,128)(2,1)S(1)}, u32[]{:S(2)}, u32[]{:S(2)}) collective-permute-start(bf16[128,4096]{1,0:T(8,128)(2,1)} %refs_1_.1), channel_id=1, source_target_pairs={{0,1},{1,0},{2,3},{3,2},{4,5},{5,4},{6,7},{7,6},{8,9},{9,8},{10,11... | collective-permute-start | bytes 3145736 | tf_op jit(solution)/shard_map/ppermute | solution.py:45
  1.2 0.1 collective-permute-start.1
  1.2 0.0 copy-start
  1.2 3.2 %prepare.1 = (bf16[14,128,128]{2,1,0:T(8,128)(2,1)S(1)}, bf16[14,128,128]{2,1,0:T(8,128)(2,1)S(1)}, f32[256,128]{1,0:T(8,128)S(1)}, f32[256,128]{1,0:T(8,128)S(1)}, f32[8,4,16,128]{3,2,1,0:T(8,128)S(1)}) custom-call(s32[3,14]{1,0:T(4,128)} %bitcast.26, bf16[128,4096]{1,0:T(8,128)(2,1)} %refs_1_.1, bf16[128,4096]{1,0:T(8,128)(2,1)} %refs_2_.1, ...), custom_call_target="tpu_custom_call" | custom-call | tf_op jit(solution)/shard_map/prepare/pallas_call | solution.py:285
  4.5 0.0 collective-permute-done.refs_4_
  4.5 0.7 %collective-permute-done.1.refs_5_ = bf16[128,4096]{1,0:T(8,128)(2,1)S(1)} collective-permute-done((bf16[128,4096]{1,0:T(8,128)(2,1)}, bf16[128,4096]{1,0:T(8,128)(2,1)S(1)}, u32[]{:S(2)}, u32[]{:S(2)}) %collective-permute-start.1) | collective-permute-done | bytes 1048608 | tf_op jit(solution)/shard_map/ppermute | solution.py:45
  5.1 0.0 copy-done
  5.2 0.6 %partials.1 = (f32[2,14,16,128]{3,2,1,0:T(8,128)S(1)}, f32[2,18,16,128]{3,2,1,0:T(8,128)S(1)}, f32[2,18,16,128]{3,2,1,0:T(8,128)S(1)}, f32[2,18,16,128]{3,2,1,0:T(8,128)S(1)}) custom-call(s32[3,14]{1,0:T(4,128)S(1)} %bitcast.27, bf16[14,128,128]{2,1,0:T(8,128)(2,1)S(1)} %get-tuple-element.23.refs_1_, bf16[14,128,128]{2,1,0:T(8,128)(2,1)S(1)} %get-tuple-element.24.refs_2_, ...), custom_call_target="tpu_custom_call" | custom-call | tf_op jit(solution)/shard_map/partials/pallas_call | solution.py:316
  5.8 0.0 copy-start.1
  5.9 3.9 %collective-permute-start.4 = (f16[2,18,16,128]{3,2,1,0:T(8,128)(2,1)S(1)}, f16[2,18,16,128]{3,2,1,0:T(8,128)(2,1)S(1)}, u32[]{:S(2)}, u32[]{:S(2)}) collective-permute-start(f16[2,18,16,128]{3,2,1,0:T(8,128)(2,1)S(1)} %multiply_convert_fusion.1), channel_id=1, source_target_pairs={{0,6},{2,4},{4,2},{6,0},{8,14},{10,12},{12,10},{14,8},{16,22},{18,... | collective-permute-start | bytes 442376 | tf_op jit(solution)/shard_map/ppermute | solution.py:45
  9.8 0.6 %collective-permute-start.3 = (f16[2,18,16,128]{3,2,1,0:T(8,128)(2,1)S(1)}, f16[2,18,16,128]{3,2,1,0:T(8,128)(2,1)S(1)}, u32[]{:S(2)}, u32[]{:S(2)}) collective-permute-start(f16[2,18,16,128]{3,2,1,0:T(8,128)(2,1)S(1)} %multiply_convert_fusion.2), channel_id=1, source_target_pairs={{0,4},{2,6},{4,0},{6,2},{8,12},{10,14},{12,8},{14,10},{16,20},{18,... | collective-permute-start | bytes 442376 | tf_op jit(solution)/shard_map/ppermute | solution.py:45
  10.4 0.1 collective-permute-start.2
  10.5 3.8 %collective-permute-done.4 = f16[2,18,16,128]{3,2,1,0:T(8,128)(2,1)S(1)} collective-permute-done((f16[2,18,16,128]{3,2,1,0:T(8,128)(2,1)S(1)}, f16[2,18,16,128]{3,2,1,0:T(8,128)(2,1)S(1)}, u32[]{:S(2)}, u32[]{:S(2)}) %collective-permute-start.4) | collective-permute-done | bytes 147488 | tf_op jit(solution)/shard_map/ppermute | solution.py:45
  14.3 2.8 %collective-permute-done.3 = f16[2,18,16,128]{3,2,1,0:T(8,128)(2,1)S(1)} collective-permute-done((f16[2,18,16,128]{3,2,1,0:T(8,128)(2,1)S(1)}, f16[2,18,16,128]{3,2,1,0:T(8,128)(2,1)S(1)}, u32[]{:S(2)}, u32[]{:S(2)}) %collective-permute-start.3) | collective-permute-done | bytes 147488 | tf_op jit(solution)/shard_map/ppermute | solution.py:45
  17.1 0.3 collective-permute-done.2
  17.4 0.1 plane.1
  17.6 1.6 %collective-permute-start.5 = (f16[30,16,128]{2,1,0:T(8,128)(2,1)S(1)}, f16[30,16,128]{2,1,0:T(8,128)(2,1)S(1)}, u32[]{:S(2)}, u32[]{:S(2)}) collective-permute-start(f16[30,16,128]{2,1,0:T(8,128)(2,1)S(1)} %multiply_convert_fusion.5), channel_id=1, source_target_pairs={{0,8},{2,10},{4,12},{6,14},{8,0},{10,2},{12,4},{14,6},{16,24},{18,... | collective-permute-start | bytes 368648 | tf_op jit(solution)/shard_map/ppermute | solution.py:45
  19.2 2.7 %collective-permute-start.7 = (f16[16,16,128]{2,1,0:T(8,128)(2,1)S(1)}, f16[16,16,128]{2,1,0:T(8,128)(2,1)S(1)}, u32[]{:S(2)}, u32[]{:S(2)}) collective-permute-start(f16[16,16,128]{2,1,0:T(8,128)(2,1)S(1)} %multiply_convert_fusion.7), channel_id=1, source_target_pairs={{0,16},{2,18},{4,20},{6,22},{8,24},{10,26},{12,28},{14,30},{16,0},... | collective-permute-start | bytes 196616 | tf_op jit(solution)/shard_map/ppermute | solution.py:45
  21.9 0.2 collective-permute-start.8
  22.1 1.2 %collective-permute-done.5 = f16[30,16,128]{2,1,0:T(8,128)(2,1)S(1)} collective-permute-done((f16[30,16,128]{2,1,0:T(8,128)(2,1)S(1)}, f16[30,16,128]{2,1,0:T(8,128)(2,1)S(1)}, u32[]{:S(2)}, u32[]{:S(2)}) %collective-permute-start.5) | collective-permute-done | bytes 122912 | tf_op jit(solution)/shard_map/ppermute | solution.py:45
  23.4 2.8 %collective-permute-start.6 = (f16[14,16,128]{2,1,0:T(8,128)(2,1)S(1)}, f16[14,16,128]{2,1,0:T(8,128)(2,1)S(1)}, u32[]{:S(2)}, u32[]{:S(2)}) collective-permute-start(f16[14,16,128]{2,1,0:T(8,128)(2,1)S(1)} %fusion.1), channel_id=1, source_target_pairs={{0,16},{2,18},{4,20},{6,22},{8,24},{10,26},{12,28},{14,30},{16,0},... | collective-permute-start | bytes 172040 | tf_op jit(solution)/shard_map/ppermute | solution.py:45
  26.2 2.3 %collective-permute-done.7 = f16[16,16,128]{2,1,0:T(8,128)(2,1)S(1)} collective-permute-done((f16[16,16,128]{2,1,0:T(8,128)(2,1)S(1)}, f16[16,16,128]{2,1,0:T(8,128)(2,1)S(1)}, u32[]{:S(2)}, u32[]{:S(2)}) %collective-permute-start.7) | collective-permute-done | bytes 65568 | tf_op jit(solution)/shard_map/ppermute | solution.py:45
  28.6 0.0 collective-permute-done.8
  28.6 2.5 %collective-permute-done.6 = f16[14,16,128]{2,1,0:T(8,128)(2,1)S(1)} collective-permute-done((f16[14,16,128]{2,1,0:T(8,128)(2,1)S(1)}, f16[14,16,128]{2,1,0:T(8,128)(2,1)S(1)}, u32[]{:S(2)}, u32[]{:S(2)}) %collective-permute-start.6) | collective-permute-done | bytes 57376 | tf_op jit(solution)/shard_map/ppermute | solution.py:45
  31.2 0.0 copy-done.1
  31.2 0.4 adam.1
  31.6 0.1 multiply_convert_fusion
  31.7 11.4 %all_to_all.5 = f16[8,16,16,128]{3,2,1,0:T(8,128)(2,1)S(1)} all-to-all(f16[8,16,16,128]{3,2,1,0:T(8,128)(2,1)S(1)} %multiply_convert_fusion), channel_id=1, replica_groups={{0,2,4,6,8,10,12,14},{16,18,20,22,24,26,28,30},{1,3,5,7,9,11,13,15},{17..., dimensions={0} | all-to-all | bytes 1048576 | tf_op jit(solution)/shard_map/all_to_all | solution.py:51
  43.1 0.1 convert_multiply_fusion.message
  43.2 0.9 %final.1 = (bf16[14,128,128]{2,1,0:T(8,128)(2,1)}, f32[256,128]{1,0:T(8,128)}, f32[256,128]{1,0:T(8,128)}) custom-call(f32[8,16,16,128]{3,2,1,0:T(8,128)S(1)} %convert_multiply_fusion.message, f32[256,128]{1,0:T(8,128)S(1)} %get-tuple-element.36.first_old, f32[256,128]{1,0:T(8,128)S(1)} %get-tuple-element.37.second_old), custom_call_target="tpu_custom_call" | custom-call | tf_op jit(solution)/shard_map/final/pallas_call | solution.py:368
  (16 shorter events, 0.4 us)
Async XLA Ops:
  0.6 3.9 %collective-permute-start = (bf16[128,4096]{1,0:T(8,128)(2,1)}, bf16[128,4096]{1,0:T(8,128)(2,1)S(1)}, u32[]{:S(2)}, u32[]{:S(2)}) collective-permute-start(bf16[128,4096]{1,0:T(8,128)(2,1)} %refs_1_.1), channel_id=1, source_target_pairs={{0,1},{1,0},{2,3},{3,2},{4,5},{5,4},{6,7},{7,6},{8,9},{9,8},{10,11... | collective-permute-start | bytes 3145736 | tf_op jit(solution)/shard_map/ppermute | solution.py:45
  1.2 4.0 %collective-permute-start.1 = (bf16[128,4096]{1,0:T(8,128)(2,1)}, bf16[128,4096]{1,0:T(8,128)(2,1)S(1)}, u32[]{:S(2)}, u32[]{:S(2)}) collective-permute-start(bf16[128,4096]{1,0:T(8,128)(2,1)} %refs_2_.1), channel_id=1, source_target_pairs={{0,1},{1,0},{2,3},{3,2},{4,5},{5,4},{6,7},{7,6},{8,9},{9,8},{10,11... | collective-permute-start | bytes 3145736 | tf_op jit(solution)/shard_map/ppermute | solution.py:45
  1.2 3.9 %copy-start = (s32[14,3]{0,1:T(4,128)S(1)}, s32[14,3]{0,1:T(4,128)}, u32[]{:S(2)}) copy-start(s32[14,3]{0,1:T(4,128)} %param.18) | copy-start | bytes 508
  5.8 25.4 %copy-start.1 = (s32[14]{0:T(128)S(1)}, s32[14]{0:T(128)}, u32[]{:S(2)}) copy-start(s32[14]{0:T(128)} %param.19) | copy-start | bytes 172
  5.9 8.4 %collective-permute-start.4 = (f16[2,18,16,128]{3,2,1,0:T(8,128)(2,1)S(1)}, f16[2,18,16,128]{3,2,1,0:T(8,128)(2,1)S(1)}, u32[]{:S(2)}, u32[]{:S(2)}) collective-permute-start(f16[2,18,16,128]{3,2,1,0:T(8,128)(2,1)S(1)} %multiply_convert_fusion.1), channel_id=1, source_target_pairs={{0,6},{2,4},{4,2},{6,0},{8,14},{10,12},{12,10},{14,8},{16,22},{18,... | collective-permute-start | bytes 442376 | tf_op jit(solution)/shard_map/ppermute | solution.py:45
  9.8 7.3 %collective-permute-start.3 = (f16[2,18,16,128]{3,2,1,0:T(8,128)(2,1)S(1)}, f16[2,18,16,128]{3,2,1,0:T(8,128)(2,1)S(1)}, u32[]{:S(2)}, u32[]{:S(2)}) collective-permute-start(f16[2,18,16,128]{3,2,1,0:T(8,128)(2,1)S(1)} %multiply_convert_fusion.2), channel_id=1, source_target_pairs={{0,4},{2,6},{4,0},{6,2},{8,12},{10,14},{12,8},{14,10},{16,20},{18,... | collective-permute-start | bytes 442376 | tf_op jit(solution)/shard_map/ppermute | solution.py:45
  10.4 7.0 %collective-permute-start.2 = (f16[2,18,16,128]{3,2,1,0:T(8,128)(2,1)S(1)}, f16[2,18,16,128]{3,2,1,0:T(8,128)(2,1)S(1)}, u32[]{:S(2)}, u32[]{:S(2)}) collective-permute-start(f16[2,18,16,128]{3,2,1,0:T(8,128)(2,1)S(1)} %multiply_convert_fusion.3), channel_id=1, source_target_pairs={{0,2},{2,0},{4,6},{6,4},{8,10},{10,8},{12,14},{14,12},{16,18},{18,... | collective-permute-start | bytes 442376 | tf_op jit(solution)/shard_map/ppermute | solution.py:45
  17.6 5.8 %collective-permute-start.5 = (f16[30,16,128]{2,1,0:T(8,128)(2,1)S(1)}, f16[30,16,128]{2,1,0:T(8,128)(2,1)S(1)}, u32[]{:S(2)}, u32[]{:S(2)}) collective-permute-start(f16[30,16,128]{2,1,0:T(8,128)(2,1)S(1)} %multiply_convert_fusion.5), channel_id=1, source_target_pairs={{0,8},{2,10},{4,12},{6,14},{8,0},{10,2},{12,4},{14,6},{16,24},{18,... | collective-permute-start | bytes 368648 | tf_op jit(solution)/shard_map/ppermute | solution.py:45
  19.2 9.4 %collective-permute-start.7 = (f16[16,16,128]{2,1,0:T(8,128)(2,1)S(1)}, f16[16,16,128]{2,1,0:T(8,128)(2,1)S(1)}, u32[]{:S(2)}, u32[]{:S(2)}) collective-permute-start(f16[16,16,128]{2,1,0:T(8,128)(2,1)S(1)} %multiply_convert_fusion.7), channel_id=1, source_target_pairs={{0,16},{2,18},{4,20},{6,22},{8,24},{10,26},{12,28},{14,30},{16,0},... | collective-permute-start | bytes 196616 | tf_op jit(solution)/shard_map/ppermute | solution.py:45
  21.9 6.7 %collective-permute-start.8 = (f16[16,16,128]{2,1,0:T(8,128)(2,1)S(1)}, f16[16,16,128]{2,1,0:T(8,128)(2,1)S(1)}, u32[]{:S(2)}, u32[]{:S(2)}) collective-permute-start(f16[16,16,128]{2,1,0:T(8,128)(2,1)S(1)} %multiply_convert_fusion.6), channel_id=1, source_target_pairs={{0,24},{2,26},{4,28},{6,30},{8,16},{10,18},{12,20},{14,22},{16,8},... | collective-permute-start | bytes 196616 | tf_op jit(solution)/shard_map/ppermute | solution.py:45
  23.4 7.7 %collective-permute-start.6 = (f16[14,16,128]{2,1,0:T(8,128)(2,1)S(1)}, f16[14,16,128]{2,1,0:T(8,128)(2,1)S(1)}, u32[]{:S(2)}, u32[]{:S(2)}) collective-permute-start(f16[14,16,128]{2,1,0:T(8,128)(2,1)S(1)} %fusion.1), channel_id=1, source_target_pairs={{0,16},{2,18},{4,20},{6,22},{8,24},{10,26},{12,28},{14,30},{16,0},... | collective-permute-start | bytes 172040 | tf_op jit(solution)/shard_map/ppermute | solution.py:45

commit v6 on v5

--- a/solution.py
+++ b/solution.py
@@ -188,15 +188,14 @@
         summed = arrived[0][which]
         for piece in arrived[1:]:
             summed = summed + piece[which, pl.ds(0, tiles)]
-        ref[pl.ds(0, tiles)] = summed
+        ref[...] = summed
     for distance in range(PLANE):
-        for which, targets in ((half, ((near, 0),)), (HALVES - 1 - half, ((far, 0), (sent, tiles)))):
+        for which, target in ((half, near), (HALVES - 1 - half, far)):
             if distance == 0:
                 found = states[which * PLANE + inner]
             else:
                 found = arrived[distance][which, pl.ds(tiles, FIELDS)]
-            for target, start in targets:
-                target[pl.ds(start + distance * FIELDS, FIELDS)] = found
+            target[pl.ds(distance * FIELDS, FIELDS)] = found
 
 
 def adam_kernel(outer, planes, *refs):
@@ -331,7 +330,7 @@
         plane_kernel,
         out_shape=(
             jax.ShapeDtypeStruct(share, jnp.float32),
-            jax.ShapeDtypeStruct((tiles + fields, SHARE, TB), jnp.float32),
+            jax.ShapeDtypeStruct(share, jnp.float32),
             jax.ShapeDtypeStruct((fields, SHARE, TB), jnp.float32),
             jax.ShapeDtypeStruct((fields, SHARE, TB), jnp.float32),
         ),
@@ -341,13 +340,14 @@
         name="plane",
     )(state_message, *arrived)
     planes = owners // PLANE
-    near16, far16 = narrow(near), narrow(far)
-    beside = widen(partner(narrow(sent), "dp", PLANE))
-    distant = [partner(far16 if p % HALVES else near16, "dp", p * PLANE) for p in range(2, planes)]
-    summed = narrow(kept + beside[:tiles])
+    sent = narrow(sent)
+    near16, far16 = lax.optimization_barrier((narrow(near), narrow(far), sent))[:2]
+    beside = widen(partner(sent, "dp", PLANE))
+    distant = [partner(far16 if p % HALVES else near16, "dp", p * PLANE) for p in range(1, planes)]
+    summed = narrow(kept + beside)
     sums = [partner(summed, "dp", r * INNER) for r in range(1, outer)]
     sums, distant = lax.optimization_barrier((sums, distant))
-    states = [near, beside, *map(widen, distant)]
+    states = [near, *map(widen, distant)]
     sums = [widen(summed), *map(widen, sums)]
 
     message = pl.pallas_call(

time: 44.4 us -> 44.2 us (level)
  waiting for transfers between devices: 13.6 us -> 12.8 us
  starting transfers between devices: 12.5 us -> 13 us
    ppermute x9 -> x10, waiting for transfers between devices: 13.6 us -> 12.8 us  [partner(): return lax.ppermute(array, axis, [(i, i ^ distance) for i in range(count)])]
    ppermute x9 -> x10, starting transfers between devices: 12.5 us -> 13 us  [partner(): return lax.ppermute(array, axis, [(i, i ^ distance) for i in range(count)])]
  transfers between devices with their start and end apart: 9 -> 10, of which waited for: 7 -> 6; matrix products, arithmetic and copies ran while one was open for 1% -> 1% of each run, Pallas kernels for 7% -> 7%
where the time goes in v6:
time: 44.2 us; the launch traced here: 43.9 us
  starting transfers between devices  13 us (29%)
  waiting for transfers between devices  12.8 us (29%)
  blocking collectives  11.5 us (26%)
  Pallas kernels  5.16 us (12%)
  between operations  0.8 us (2%)
  other arithmetic  0.6 us (1%)
    ppermute x10, starting transfers between devices, partner(): return lax.ppermute(array, axis, [(i, i ^ distance) for i in range(count)])  13 us
    ppermute x10, waiting for transfers between devices, partner(): return lax.ppermute(array, axis, [(i, i ^ distance) for i in range(count)])  12.8 us
    all_to_all x1, blocking collectives, exchange(): lax.all_to_all(array, 'dp', 0, 0, tiled=True, axis_index_groups=groups)  11.5 us
    pallas_call x1, Pallas kernels, body(): pl.pallas_call(prepare_kernel, out_shape=(kept_whole, kept_whole, kept_ol...  3.17 us
    pallas_call x1, Pallas kernels, body(): pl.pallas_call(final_kernel, out_shape=(jax.ShapeDtypeStruct((tiles, TB,...  0.91 us
  transfers between devices with their start and end apart: 10, of which 6 were waited for; matrix products, arithmetic and copies ran while one was open for 1% of the time, Pallas kernels for 7%

profile of v6, /device:TPU:0, one launch (start us, length us, event | category | flops | bytes accessed | tf_op | source)
XLA Modules:
  0.0 43.9 jit_solution(960120513458505173)
XLA Ops:
  0.6 0.5 %collective-permute-start = (bf16[128,4096]{1,0:T(8,128)(2,1)}, bf16[128,4096]{1,0:T(8,128)(2,1)S(1)}, u32[]{:S(2)}, u32[]{:S(2)}) collective-permute-start(bf16[128,4096]{1,0:T(8,128)(2,1)} %refs_1_.1), channel_id=1, source_target_pairs={{0,1},{1,0},{2,3},{3,2},{4,5},{5,4},{6,7},{7,6},{8,9},{9,8},{10,11... | collective-permute-start | bytes 3145736 | tf_op jit(solution)/shard_map/ppermute | solution.py:45
  1.2 0.1 collective-permute-start.1
  1.2 0.0 copy-start
  1.2 3.2 %prepare.1 = (bf16[14,128,128]{2,1,0:T(8,128)(2,1)S(1)}, bf16[14,128,128]{2,1,0:T(8,128)(2,1)S(1)}, f32[256,128]{1,0:T(8,128)S(1)}, f32[256,128]{1,0:T(8,128)S(1)}, f32[8,4,16,128]{3,2,1,0:T(8,128)S(1)}) custom-call(s32[3,14]{1,0:T(4,128)} %bitcast.26, bf16[128,4096]{1,0:T(8,128)(2,1)} %refs_1_.1, bf16[128,4096]{1,0:T(8,128)(2,1)} %refs_2_.1, ...), custom_call_target="tpu_custom_call" | custom-call | tf_op jit(solution)/shard_map/prepare/pallas_call | solution.py:284
  4.5 0.0 collective-permute-done.refs_4_
  4.5 0.7 %collective-permute-done.1.refs_5_ = bf16[128,4096]{1,0:T(8,128)(2,1)S(1)} collective-permute-done((bf16[128,4096]{1,0:T(8,128)(2,1)}, bf16[128,4096]{1,0:T(8,128)(2,1)S(1)}, u32[]{:S(2)}, u32[]{:S(2)}) %collective-permute-start.1) | collective-permute-done | bytes 1048608 | tf_op jit(solution)/shard_map/ppermute | solution.py:45
  5.1 0.0 copy-done
  5.2 0.6 %partials.1 = (f32[2,14,16,128]{3,2,1,0:T(8,128)S(1)}, f32[2,18,16,128]{3,2,1,0:T(8,128)S(1)}, f32[2,18,16,128]{3,2,1,0:T(8,128)S(1)}, f32[2,18,16,128]{3,2,1,0:T(8,128)S(1)}) custom-call(s32[3,14]{1,0:T(4,128)S(1)} %bitcast.27, bf16[14,128,128]{2,1,0:T(8,128)(2,1)S(1)} %get-tuple-element.26.refs_1_, bf16[14,128,128]{2,1,0:T(8,128)(2,1)S(1)} %get-tuple-element.27.refs_2_, ...), custom_call_target="tpu_custom_call" | custom-call | tf_op jit(solution)/shard_map/partials/pallas_call | solution.py:315
  5.8 0.0 copy-start.1
  5.9 3.9 %collective-permute-start.4 = (f16[2,18,16,128]{3,2,1,0:T(8,128)(2,1)S(1)}, f16[2,18,16,128]{3,2,1,0:T(8,128)(2,1)S(1)}, u32[]{:S(2)}, u32[]{:S(2)}) collective-permute-start(f16[2,18,16,128]{3,2,1,0:T(8,128)(2,1)S(1)} %multiply_convert_fusion.1), channel_id=1, source_target_pairs={{0,6},{2,4},{4,2},{6,0},{8,14},{10,12},{12,10},{14,8},{16,22},{18,... | collective-permute-start | bytes 442376 | tf_op jit(solution)/shard_map/ppermute | solution.py:45
  9.8 0.5 %collective-permute-start.3 = (f16[2,18,16,128]{3,2,1,0:T(8,128)(2,1)S(1)}, f16[2,18,16,128]{3,2,1,0:T(8,128)(2,1)S(1)}, u32[]{:S(2)}, u32[]{:S(2)}) collective-permute-start(f16[2,18,16,128]{3,2,1,0:T(8,128)(2,1)S(1)} %multiply_convert_fusion.2), channel_id=1, source_target_pairs={{0,4},{2,6},{4,0},{6,2},{8,12},{10,14},{12,8},{14,10},{16,20},{18,... | collective-permute-start | bytes 442376 | tf_op jit(solution)/shard_map/ppermute | solution.py:45
  10.4 0.1 collective-permute-start.2
  10.5 3.8 %collective-permute-done.4 = f16[2,18,16,128]{3,2,1,0:T(8,128)(2,1)S(1)} collective-permute-done((f16[2,18,16,128]{3,2,1,0:T(8,128)(2,1)S(1)}, f16[2,18,16,128]{3,2,1,0:T(8,128)(2,1)S(1)}, u32[]{:S(2)}, u32[]{:S(2)}) %collective-permute-start.4) | collective-permute-done | bytes 147488 | tf_op jit(solution)/shard_map/ppermute | solution.py:45
  14.3 2.8 %collective-permute-done.3 = f16[2,18,16,128]{3,2,1,0:T(8,128)(2,1)S(1)} collective-permute-done((f16[2,18,16,128]{3,2,1,0:T(8,128)(2,1)S(1)}, f16[2,18,16,128]{3,2,1,0:T(8,128)(2,1)S(1)}, u32[]{:S(2)}, u32[]{:S(2)}) %collective-permute-start.3) | collective-permute-done | bytes 147488 | tf_op jit(solution)/shard_map/ppermute | solution.py:45
  17.1 0.3 collective-permute-done.2
  17.4 0.1 plane.1
  17.5 1.6 %collective-permute-start.5 = (f16[14,16,128]{2,1,0:T(8,128)(2,1)S(1)}, f16[14,16,128]{2,1,0:T(8,128)(2,1)S(1)}, u32[]{:S(2)}, u32[]{:S(2)}) collective-permute-start(f16[14,16,128]{2,1,0:T(8,128)(2,1)S(1)} %multiply_convert_fusion.8), channel_id=1, source_target_pairs={{0,8},{2,10},{4,12},{6,14},{8,0},{10,2},{12,4},{14,6},{16,24},{18,... | collective-permute-start | bytes 172040 | tf_op jit(solution)/shard_map/ppermute | solution.py:45
  19.2 2.5 %collective-permute-start.9 = (f16[16,16,128]{2,1,0:T(8,128)(2,1)S(1)}, f16[16,16,128]{2,1,0:T(8,128)(2,1)S(1)}, u32[]{:S(2)}, u32[]{:S(2)}) collective-permute-start(f16[16,16,128]{2,1,0:T(8,128)(2,1)S(1)} %get-tuple-element.36), channel_id=1, source_target_pairs={{0,24},{2,26},{4,28},{6,30},{8,16},{10,18},{12,20},{14,22},{16,8},... | collective-permute-start | bytes 196616 | tf_op jit(solution)/shard_map/ppermute | solution.py:45
  21.7 0.7 %collective-permute-start.7 = (f16[16,16,128]{2,1,0:T(8,128)(2,1)S(1)}, f16[16,16,128]{2,1,0:T(8,128)(2,1)S(1)}, u32[]{:S(2)}, u32[]{:S(2)}) collective-permute-start(f16[16,16,128]{2,1,0:T(8,128)(2,1)S(1)} %get-tuple-element.36), channel_id=1, source_target_pairs={{0,8},{2,10},{4,12},{6,14},{8,0},{10,2},{12,4},{14,6},{16,24},{18,... | collective-permute-start | bytes 196616 | tf_op jit(solution)/shard_map/ppermute | solution.py:45
  22.4 1.2 %collective-permute-start.8 = (f16[16,16,128]{2,1,0:T(8,128)(2,1)S(1)}, f16[16,16,128]{2,1,0:T(8,128)(2,1)S(1)}, u32[]{:S(2)}, u32[]{:S(2)}) collective-permute-start(f16[16,16,128]{2,1,0:T(8,128)(2,1)S(1)} %get-tuple-element.37), channel_id=1, source_target_pairs={{0,16},{2,18},{4,20},{6,22},{8,24},{10,26},{12,28},{14,30},{16,0},... | collective-permute-start | bytes 196616 | tf_op jit(solution)/shard_map/ppermute | solution.py:45
  23.7 0.0 collective-permute-done.5
  23.7 1.8 %collective-permute-start.6 = (f16[14,16,128]{2,1,0:T(8,128)(2,1)S(1)}, f16[14,16,128]{2,1,0:T(8,128)(2,1)S(1)}, u32[]{:S(2)}, u32[]{:S(2)}) collective-permute-start(f16[14,16,128]{2,1,0:T(8,128)(2,1)S(1)} %multiply_convert_fusion.7), channel_id=1, source_target_pairs={{0,16},{2,18},{4,20},{6,22},{8,24},{10,26},{12,28},{14,30},{16,0},... | collective-permute-start | bytes 172040 | tf_op jit(solution)/shard_map/ppermute | solution.py:45
  25.5 4.7 %collective-permute-done.8 = f16[16,16,128]{2,1,0:T(8,128)(2,1)S(1)} collective-permute-done((f16[16,16,128]{2,1,0:T(8,128)(2,1)S(1)}, f16[16,16,128]{2,1,0:T(8,128)(2,1)S(1)}, u32[]{:S(2)}, u32[]{:S(2)}) %collective-permute-start.8) | collective-permute-done | bytes 65568 | tf_op jit(solution)/shard_map/ppermute | solution.py:45
  30.2 0.0 collective-permute-done.9
  30.2 0.0 collective-permute-done.7
  30.2 0.6 %collective-permute-done.6 = f16[14,16,128]{2,1,0:T(8,128)(2,1)S(1)} collective-permute-done((f16[14,16,128]{2,1,0:T(8,128)(2,1)S(1)}, f16[14,16,128]{2,1,0:T(8,128)(2,1)S(1)}, u32[]{:S(2)}, u32[]{:S(2)}) %collective-permute-start.6) | collective-permute-done | bytes 57376 | tf_op jit(solution)/shard_map/ppermute | solution.py:45
  30.9 0.0 copy-done.1
  30.9 0.4 adam.1
  31.3 0.1 multiply_convert_fusion
  31.4 11.5 %all_to_all.5 = f16[8,16,16,128]{3,2,1,0:T(8,128)(2,1)S(1)} all-to-all(f16[8,16,16,128]{3,2,1,0:T(8,128)(2,1)S(1)} %multiply_convert_fusion), channel_id=1, replica_groups={{0,2,4,6,8,10,12,14},{16,18,20,22,24,26,28,30},{1,3,5,7,9,11,13,15},{17..., dimensions={0} | all-to-all | bytes 1048576 | tf_op jit(solution)/shard_map/all_to_all | solution.py:51
  42.9 0.1 convert_multiply_fusion.message
  43.0 0.9 %final.1 = (bf16[14,128,128]{2,1,0:T(8,128)(2,1)}, f32[256,128]{1,0:T(8,128)}, f32[256,128]{1,0:T(8,128)}) custom-call(f32[8,16,16,128]{3,2,1,0:T(8,128)S(1)} %convert_multiply_fusion.message, f32[256,128]{1,0:T(8,128)S(1)} %get-tuple-element.42.first_old, f32[256,128]{1,0:T(8,128)S(1)} %get-tuple-element.43.second_old), custom_call_target="tpu_custom_call" | custom-call | tf_op jit(solution)/shard_map/final/pallas_call | solution.py:368
  (16 shorter events, 0.4 us)
Async XLA Ops:
  0.6 3.9 %collective-permute-start = (bf16[128,4096]{1,0:T(8,128)(2,1)}, bf16[128,4096]{1,0:T(8,128)(2,1)S(1)}, u32[]{:S(2)}, u32[]{:S(2)}) collective-permute-start(bf16[128,4096]{1,0:T(8,128)(2,1)} %refs_1_.1), channel_id=1, source_target_pairs={{0,1},{1,0},{2,3},{3,2},{4,5},{5,4},{6,7},{7,6},{8,9},{9,8},{10,11... | collective-permute-start | bytes 3145736 | tf_op jit(solution)/shard_map/ppermute | solution.py:45
  1.2 4.0 %collective-permute-start.1 = (bf16[128,4096]{1,0:T(8,128)(2,1)}, bf16[128,4096]{1,0:T(8,128)(2,1)S(1)}, u32[]{:S(2)}, u32[]{:S(2)}) collective-permute-start(bf16[128,4096]{1,0:T(8,128)(2,1)} %refs_2_.1), channel_id=1, source_target_pairs={{0,1},{1,0},{2,3},{3,2},{4,5},{5,4},{6,7},{7,6},{8,9},{9,8},{10,11... | collective-permute-start | bytes 3145736 | tf_op jit(solution)/shard_map/ppermute | solution.py:45
  1.2 3.9 %copy-start = (s32[14,3]{0,1:T(4,128)S(1)}, s32[14,3]{0,1:T(4,128)}, u32[]{:S(2)}) copy-start(s32[14,3]{0,1:T(4,128)} %param.18) | copy-start | bytes 508
  5.8 25.1 %copy-start.1 = (s32[14]{0:T(128)S(1)}, s32[14]{0:T(128)}, u32[]{:S(2)}) copy-start(s32[14]{0:T(128)} %param.19) | copy-start | bytes 172
  5.9 8.4 %collective-permute-start.4 = (f16[2,18,16,128]{3,2,1,0:T(8,128)(2,1)S(1)}, f16[2,18,16,128]{3,2,1,0:T(8,128)(2,1)S(1)}, u32[]{:S(2)}, u32[]{:S(2)}) collective-permute-start(f16[2,18,16,128]{3,2,1,0:T(8,128)(2,1)S(1)} %multiply_convert_fusion.1), channel_id=1, source_target_pairs={{0,6},{2,4},{4,2},{6,0},{8,14},{10,12},{12,10},{14,8},{16,22},{18,... | collective-permute-start | bytes 442376 | tf_op jit(solution)/shard_map/ppermute | solution.py:45
  9.8 7.3 %collective-permute-start.3 = (f16[2,18,16,128]{3,2,1,0:T(8,128)(2,1)S(1)}, f16[2,18,16,128]{3,2,1,0:T(8,128)(2,1)S(1)}, u32[]{:S(2)}, u32[]{:S(2)}) collective-permute-start(f16[2,18,16,128]{3,2,1,0:T(8,128)(2,1)S(1)} %multiply_convert_fusion.2), channel_id=1, source_target_pairs={{0,4},{2,6},{4,0},{6,2},{8,12},{10,14},{12,8},{14,10},{16,20},{18,... | collective-permute-start | bytes 442376 | tf_op jit(solution)/shard_map/ppermute | solution.py:45
  10.4 7.0 %collective-permute-start.2 = (f16[2,18,16,128]{3,2,1,0:T(8,128)(2,1)S(1)}, f16[2,18,16,128]{3,2,1,0:T(8,128)(2,1)S(1)}, u32[]{:S(2)}, u32[]{:S(2)}) collective-permute-start(f16[2,18,16,128]{3,2,1,0:T(8,128)(2,1)S(1)} %multiply_convert_fusion.3), channel_id=1, source_target_pairs={{0,2},{2,0},{4,6},{6,4},{8,10},{10,8},{12,14},{14,12},{16,18},{18,... | collective-permute-start | bytes 442376 | tf_op jit(solution)/shard_map/ppermute | solution.py:45
  17.5 6.1 %collective-permute-start.5 = (f16[14,16,128]{2,1,0:T(8,128)(2,1)S(1)}, f16[14,16,128]{2,1,0:T(8,128)(2,1)S(1)}, u32[]{:S(2)}, u32[]{:S(2)}) collective-permute-start(f16[14,16,128]{2,1,0:T(8,128)(2,1)S(1)} %multiply_convert_fusion.8), channel_id=1, source_target_pairs={{0,8},{2,10},{4,12},{6,14},{8,0},{10,2},{12,4},{14,6},{16,24},{18,... | collective-permute-start | bytes 172040 | tf_op jit(solution)/shard_map/ppermute | solution.py:45
  19.2 11.0 %collective-permute-start.9 = (f16[16,16,128]{2,1,0:T(8,128)(2,1)S(1)}, f16[16,16,128]{2,1,0:T(8,128)(2,1)S(1)}, u32[]{:S(2)}, u32[]{:S(2)}) collective-permute-start(f16[16,16,128]{2,1,0:T(8,128)(2,1)S(1)} %get-tuple-element.36), channel_id=1, source_target_pairs={{0,24},{2,26},{4,28},{6,30},{8,16},{10,18},{12,20},{14,22},{16,8},... | collective-permute-start | bytes 196616 | tf_op jit(solution)/shard_map/ppermute | solution.py:45
  21.7 8.5 %collective-permute-start.7 = (f16[16,16,128]{2,1,0:T(8,128)(2,1)S(1)}, f16[16,16,128]{2,1,0:T(8,128)(2,1)S(1)}, u32[]{:S(2)}, u32[]{:S(2)}) collective-permute-start(f16[16,16,128]{2,1,0:T(8,128)(2,1)S(1)} %get-tuple-element.36), channel_id=1, source_target_pairs={{0,8},{2,10},{4,12},{6,14},{8,0},{10,2},{12,4},{14,6},{16,24},{18,... | collective-permute-start | bytes 196616 | tf_op jit(solution)/shard_map/ppermute | solution.py:45
  22.4 7.8 %collective-permute-start.8 = (f16[16,16,128]{2,1,0:T(8,128)(2,1)S(1)}, f16[16,16,128]{2,1,0:T(8,128)(2,1)S(1)}, u32[]{:S(2)}, u32[]{:S(2)}) collective-permute-start(f16[16,16,128]{2,1,0:T(8,128)(2,1)S(1)} %get-tuple-element.37), channel_id=1, source_target_pairs={{0,16},{2,18},{4,20},{6,22},{8,24},{10,26},{12,28},{14,30},{16,0},... | collective-permute-start | bytes 196616 | tf_op jit(solution)/shard_map/ppermute | solution.py:45
  23.7 7.1 %collective-permute-start.6 = (f16[14,16,128]{2,1,0:T(8,128)(2,1)S(1)}, f16[14,16,128]{2,1,0:T(8,128)(2,1)S(1)}, u32[]{:S(2)}, u32[]{:S(2)}) collective-permute-start(f16[14,16,128]{2,1,0:T(8,128)(2,1)S(1)} %multiply_convert_fusion.7), channel_id=1, source_target_pairs={{0,16},{2,18},{4,20},{6,22},{8,24},{10,26},{12,28},{14,30},{16,0},... | collective-permute-start | bytes 172040 | tf_op jit(solution)/shard_map/ppermute | solution.py:45

commit v7 on v6

--- a/solution.py
+++ b/solution.py
@@ -343,8 +343,9 @@
     sent = narrow(sent)
     near16, far16 = lax.optimization_barrier((narrow(near), narrow(far), sent))[:2]
     beside = widen(partner(sent, "dp", PLANE))
-    distant = [partner(far16 if p % HALVES else near16, "dp", p * PLANE) for p in range(1, planes)]
     summed = narrow(kept + beside)
+    late16 = lax.optimization_barrier((far16, summed))[0]
+    distant = [partner(late16 if p == 1 else far16 if p % HALVES else near16, "dp", p * PLANE) for p in range(1, planes)]
     sums = [partner(summed, "dp", r * INNER) for r in range(1, outer)]
     sums, distant = lax.optimization_barrier((sums, distant))
     states = [near, *map(widen, distant)]

time: 44.2 us -> 43.8 us (level)
  waiting for transfers between devices: 12.8 us -> 11.2 us
  starting transfers between devices: 13 us -> 14.3 us
    ppermute x10, waiting for transfers between devices: 12.8 us -> 11.2 us  [partner(): return lax.ppermute(array, axis, [(i, i ^ distance) for i in range(count)])]
    ppermute x10, starting transfers between devices: 13 us -> 14.3 us  [partner(): return lax.ppermute(array, axis, [(i, i ^ distance) for i in range(count)])]
  transfers between devices with their start and end apart: 10 -> 10, of which waited for: 6 -> 7; matrix products, arithmetic and copies ran while one was open for 1% -> 1% of each run, Pallas kernels for 7% -> 7%
where the time goes in v7:
time: 43.8 us; the launch traced here: 43.6 us
  starting transfers between devices  14.3 us (33%)
  blocking collectives  11.4 us (26%)
  waiting for transfers between devices  11.2 us (26%)
  Pallas kernels  5.15 us (12%)
  between operations  0.8 us (2%)
  other arithmetic  0.6 us (1%)
    ppermute x10, starting transfers between devices, partner(): return lax.ppermute(array, axis, [(i, i ^ distance) for i in range(count)])  14.3 us
    all_to_all x1, blocking collectives, exchange(): lax.all_to_all(array, 'dp', 0, 0, tiled=True, axis_index_groups=groups)  11.4 us
    ppermute x10, waiting for transfers between devices, partner(): return lax.ppermute(array, axis, [(i, i ^ distance) for i in range(count)])  11.2 us
    pallas_call x1, Pallas kernels, body(): pl.pallas_call(prepare_kernel, out_shape=(kept_whole, kept_whole, kept_ol...  3.17 us
    pallas_call x1, Pallas kernels, body(): pl.pallas_call(final_kernel, out_shape=(jax.ShapeDtypeStruct((tiles, TB,...  0.91 us
  transfers between devices with their start and end apart: 10, of which 7 were waited for; matrix products, arithmetic and copies ran while one was open for 1% of the time, Pallas kernels for 7%

profile of v7, /device:TPU:0, one launch (start us, length us, event | category | flops | bytes accessed | tf_op | source)
XLA Modules:
  0.0 43.6 jit_solution(17587990652221012436)
XLA Ops:
  0.6 0.5 %collective-permute-start = (bf16[128,4096]{1,0:T(8,128)(2,1)}, bf16[128,4096]{1,0:T(8,128)(2,1)S(1)}, u32[]{:S(2)}, u32[]{:S(2)}) collective-permute-start(bf16[128,4096]{1,0:T(8,128)(2,1)} %refs_1_.1), channel_id=1, source_target_pairs={{0,1},{1,0},{2,3},{3,2},{4,5},{5,4},{6,7},{7,6},{8,9},{9,8},{10,11... | collective-permute-start | bytes 3145736 | tf_op jit(solution)/shard_map/ppermute | solution.py:45
  1.2 0.1 collective-permute-start.1
  1.2 0.0 copy-start
  1.2 3.2 %prepare.1 = (bf16[14,128,128]{2,1,0:T(8,128)(2,1)S(1)}, bf16[14,128,128]{2,1,0:T(8,128)(2,1)S(1)}, f32[256,128]{1,0:T(8,128)S(1)}, f32[256,128]{1,0:T(8,128)S(1)}, f32[8,4,16,128]{3,2,1,0:T(8,128)S(1)}) custom-call(s32[3,14]{1,0:T(4,128)} %bitcast.26, bf16[128,4096]{1,0:T(8,128)(2,1)} %refs_1_.1, bf16[128,4096]{1,0:T(8,128)(2,1)} %refs_2_.1, ...), custom_call_target="tpu_custom_call" | custom-call | tf_op jit(solution)/shard_map/prepare/pallas_call | solution.py:284
  4.5 0.0 collective-permute-done.refs_4_
  4.5 0.7 %collective-permute-done.1.refs_5_ = bf16[128,4096]{1,0:T(8,128)(2,1)S(1)} collective-permute-done((bf16[128,4096]{1,0:T(8,128)(2,1)}, bf16[128,4096]{1,0:T(8,128)(2,1)S(1)}, u32[]{:S(2)}, u32[]{:S(2)}) %collective-permute-start.1) | collective-permute-done | bytes 1048608 | tf_op jit(solution)/shard_map/ppermute | solution.py:45
  5.1 0.0 copy-done
  5.2 0.6 %partials.1 = (f32[2,14,16,128]{3,2,1,0:T(8,128)S(1)}, f32[2,18,16,128]{3,2,1,0:T(8,128)S(1)}, f32[2,18,16,128]{3,2,1,0:T(8,128)S(1)}, f32[2,18,16,128]{3,2,1,0:T(8,128)S(1)}) custom-call(s32[3,14]{1,0:T(4,128)S(1)} %bitcast.27, bf16[14,128,128]{2,1,0:T(8,128)(2,1)S(1)} %get-tuple-element.27.refs_1_, bf16[14,128,128]{2,1,0:T(8,128)(2,1)S(1)} %get-tuple-element.28.refs_2_, ...), custom_call_target="tpu_custom_call" | custom-call | tf_op jit(solution)/shard_map/partials/pallas_call | solution.py:315
  5.8 0.0 copy-start.1
  5.9 3.9 %collective-permute-start.4 = (f16[2,18,16,128]{3,2,1,0:T(8,128)(2,1)S(1)}, f16[2,18,16,128]{3,2,1,0:T(8,128)(2,1)S(1)}, u32[]{:S(2)}, u32[]{:S(2)}) collective-permute-start(f16[2,18,16,128]{3,2,1,0:T(8,128)(2,1)S(1)} %multiply_convert_fusion.1), channel_id=1, source_target_pairs={{0,6},{2,4},{4,2},{6,0},{8,14},{10,12},{12,10},{14,8},{16,22},{18,... | collective-permute-start | bytes 442376 | tf_op jit(solution)/shard_map/ppermute | solution.py:45
  9.8 0.6 %collective-permute-start.3 = (f16[2,18,16,128]{3,2,1,0:T(8,128)(2,1)S(1)}, f16[2,18,16,128]{3,2,1,0:T(8,128)(2,1)S(1)}, u32[]{:S(2)}, u32[]{:S(2)}) collective-permute-start(f16[2,18,16,128]{3,2,1,0:T(8,128)(2,1)S(1)} %multiply_convert_fusion.2), channel_id=1, source_target_pairs={{0,4},{2,6},{4,0},{6,2},{8,12},{10,14},{12,8},{14,10},{16,20},{18,... | collective-permute-start | bytes 442376 | tf_op jit(solution)/shard_map/ppermute | solution.py:45
  10.4 0.1 collective-permute-start.2
  10.5 3.8 %collective-permute-done.4 = f16[2,18,16,128]{3,2,1,0:T(8,128)(2,1)S(1)} collective-permute-done((f16[2,18,16,128]{3,2,1,0:T(8,128)(2,1)S(1)}, f16[2,18,16,128]{3,2,1,0:T(8,128)(2,1)S(1)}, u32[]{:S(2)}, u32[]{:S(2)}) %collective-permute-start.4) | collective-permute-done | bytes 147488 | tf_op jit(solution)/shard_map/ppermute | solution.py:45
  14.3 2.8 %collective-permute-done.3 = f16[2,18,16,128]{3,2,1,0:T(8,128)(2,1)S(1)} collective-permute-done((f16[2,18,16,128]{3,2,1,0:T(8,128)(2,1)S(1)}, f16[2,18,16,128]{3,2,1,0:T(8,128)(2,1)S(1)}, u32[]{:S(2)}, u32[]{:S(2)}) %collective-permute-start.3) | collective-permute-done | bytes 147488 | tf_op jit(solution)/shard_map/ppermute | solution.py:45
  17.1 0.3 collective-permute-done.2
  17.4 0.1 plane.1
  17.5 1.6 %collective-permute-start.5 = (f16[14,16,128]{2,1,0:T(8,128)(2,1)S(1)}, f16[14,16,128]{2,1,0:T(8,128)(2,1)S(1)}, u32[]{:S(2)}, u32[]{:S(2)}) collective-permute-start(f16[14,16,128]{2,1,0:T(8,128)(2,1)S(1)} %multiply_convert_fusion.8), channel_id=1, source_target_pairs={{0,8},{2,10},{4,12},{6,14},{8,0},{10,2},{12,4},{14,6},{16,24},{18,... | collective-permute-start | bytes 172040 | tf_op jit(solution)/shard_map/ppermute | solution.py:45
  19.2 2.7 %collective-permute-start.8 = (f16[16,16,128]{2,1,0:T(8,128)(2,1)S(1)}, f16[16,16,128]{2,1,0:T(8,128)(2,1)S(1)}, u32[]{:S(2)}, u32[]{:S(2)}) collective-permute-start(f16[16,16,128]{2,1,0:T(8,128)(2,1)S(1)} %get-tuple-element.39), channel_id=1, source_target_pairs={{0,16},{2,18},{4,20},{6,22},{8,24},{10,26},{12,28},{14,30},{16,0},... | collective-permute-start | bytes 196616 | tf_op jit(solution)/shard_map/ppermute | solution.py:45
  21.9 0.2 collective-permute-start.9
  22.1 0.0 collective-permute-done.5
  22.1 2.6 %collective-permute-start.6 = (f16[14,16,128]{2,1,0:T(8,128)(2,1)S(1)}, f16[14,16,128]{2,1,0:T(8,128)(2,1)S(1)}, u32[]{:S(2)}, u32[]{:S(2)}) collective-permute-start(f16[14,16,128]{2,1,0:T(8,128)(2,1)S(1)} %multiply_convert_fusion.7), channel_id=1, source_target_pairs={{0,16},{2,18},{4,20},{6,22},{8,24},{10,26},{12,28},{14,30},{16,0},... | collective-permute-start | bytes 172040 | tf_op jit(solution)/shard_map/ppermute | solution.py:45
  24.8 2.0 %collective-permute-start.7 = (f16[16,16,128]{2,1,0:T(8,128)(2,1)S(1)}, f16[16,16,128]{2,1,0:T(8,128)(2,1)S(1)}, u32[]{:S(2)}, u32[]{:S(2)}) collective-permute-start(f16[16,16,128]{2,1,0:T(8,128)(2,1)S(1)} %get-tuple-element.38), channel_id=1, source_target_pairs={{0,8},{2,10},{4,12},{6,14},{8,0},{10,2},{12,4},{14,6},{16,24},{18,... | collective-permute-start | bytes 196616 | tf_op jit(solution)/shard_map/ppermute | solution.py:45
  26.8 0.4 %collective-permute-done.8 = f16[16,16,128]{2,1,0:T(8,128)(2,1)S(1)} collective-permute-done((f16[16,16,128]{2,1,0:T(8,128)(2,1)S(1)}, f16[16,16,128]{2,1,0:T(8,128)(2,1)S(1)}, u32[]{:S(2)}, u32[]{:S(2)}) %collective-permute-start.8) | collective-permute-done | bytes 65568 | tf_op jit(solution)/shard_map/ppermute | solution.py:45
  27.2 1.2 %collective-permute-done.9 = f16[16,16,128]{2,1,0:T(8,128)(2,1)S(1)} collective-permute-done((f16[16,16,128]{2,1,0:T(8,128)(2,1)S(1)}, f16[16,16,128]{2,1,0:T(8,128)(2,1)S(1)}, u32[]{:S(2)}, u32[]{:S(2)}) %collective-permute-start.9) | collective-permute-done | bytes 65568 | tf_op jit(solution)/shard_map/ppermute | solution.py:45
  28.4 2.1 %collective-permute-done.6 = f16[14,16,128]{2,1,0:T(8,128)(2,1)S(1)} collective-permute-done((f16[14,16,128]{2,1,0:T(8,128)(2,1)S(1)}, f16[14,16,128]{2,1,0:T(8,128)(2,1)S(1)}, u32[]{:S(2)}, u32[]{:S(2)}) %collective-permute-start.6) | collective-permute-done | bytes 57376 | tf_op jit(solution)/shard_map/ppermute | solution.py:45
  30.5 0.0 collective-permute-done.7
  30.6 0.0 copy-done.1
  30.6 0.4 adam.1
  31.0 0.1 multiply_convert_fusion
  31.1 11.4 %all_to_all.5 = f16[8,16,16,128]{3,2,1,0:T(8,128)(2,1)S(1)} all-to-all(f16[8,16,16,128]{3,2,1,0:T(8,128)(2,1)S(1)} %multiply_convert_fusion), channel_id=1, replica_groups={{0,2,4,6,8,10,12,14},{16,18,20,22,24,26,28,30},{1,3,5,7,9,11,13,15},{17..., dimensions={0} | all-to-all | bytes 1048576 | tf_op jit(solution)/shard_map/all_to_all | solution.py:51
  42.5 0.1 convert_multiply_fusion.message
  42.6 0.9 %final.1 = (bf16[14,128,128]{2,1,0:T(8,128)(2,1)}, f32[256,128]{1,0:T(8,128)}, f32[256,128]{1,0:T(8,128)}) custom-call(f32[8,16,16,128]{3,2,1,0:T(8,128)S(1)} %convert_multiply_fusion.message, f32[256,128]{1,0:T(8,128)S(1)} %get-tuple-element.44.first_old, f32[256,128]{1,0:T(8,128)S(1)} %get-tuple-element.45.second_old), custom_call_target="tpu_custom_call" | custom-call | tf_op jit(solution)/shard_map/final/pallas_call | solution.py:369
  (16 shorter events, 0.4 us)
Async XLA Ops:
  0.6 3.9 %collective-permute-start = (bf16[128,4096]{1,0:T(8,128)(2,1)}, bf16[128,4096]{1,0:T(8,128)(2,1)S(1)}, u32[]{:S(2)}, u32[]{:S(2)}) collective-permute-start(bf16[128,4096]{1,0:T(8,128)(2,1)} %refs_1_.1), channel_id=1, source_target_pairs={{0,1},{1,0},{2,3},{3,2},{4,5},{5,4},{6,7},{7,6},{8,9},{9,8},{10,11... | collective-permute-start | bytes 3145736 | tf_op jit(solution)/shard_map/ppermute | solution.py:45
  1.2 4.0 %collective-permute-start.1 = (bf16[128,4096]{1,0:T(8,128)(2,1)}, bf16[128,4096]{1,0:T(8,128)(2,1)S(1)}, u32[]{:S(2)}, u32[]{:S(2)}) collective-permute-start(bf16[128,4096]{1,0:T(8,128)(2,1)} %refs_2_.1), channel_id=1, source_target_pairs={{0,1},{1,0},{2,3},{3,2},{4,5},{5,4},{6,7},{7,6},{8,9},{9,8},{10,11... | collective-permute-start | bytes 3145736 | tf_op jit(solution)/shard_map/ppermute | solution.py:45
  1.2 3.9 %copy-start = (s32[14,3]{0,1:T(4,128)S(1)}, s32[14,3]{0,1:T(4,128)}, u32[]{:S(2)}) copy-start(s32[14,3]{0,1:T(4,128)} %param.18) | copy-start | bytes 508
  5.8 24.8 %copy-start.1 = (s32[14]{0:T(128)S(1)}, s32[14]{0:T(128)}, u32[]{:S(2)}) copy-start(s32[14]{0:T(128)} %param.19) | copy-start | bytes 172
  5.9 8.4 %collective-permute-start.4 = (f16[2,18,16,128]{3,2,1,0:T(8,128)(2,1)S(1)}, f16[2,18,16,128]{3,2,1,0:T(8,128)(2,1)S(1)}, u32[]{:S(2)}, u32[]{:S(2)}) collective-permute-start(f16[2,18,16,128]{3,2,1,0:T(8,128)(2,1)S(1)} %multiply_convert_fusion.1), channel_id=1, source_target_pairs={{0,6},{2,4},{4,2},{6,0},{8,14},{10,12},{12,10},{14,8},{16,22},{18,... | collective-permute-start | bytes 442376 | tf_op jit(solution)/shard_map/ppermute | solution.py:45
  9.8 7.3 %collective-permute-start.3 = (f16[2,18,16,128]{3,2,1,0:T(8,128)(2,1)S(1)}, f16[2,18,16,128]{3,2,1,0:T(8,128)(2,1)S(1)}, u32[]{:S(2)}, u32[]{:S(2)}) collective-permute-start(f16[2,18,16,128]{3,2,1,0:T(8,128)(2,1)S(1)} %multiply_convert_fusion.2), channel_id=1, source_target_pairs={{0,4},{2,6},{4,0},{6,2},{8,12},{10,14},{12,8},{14,10},{16,20},{18,... | collective-permute-start | bytes 442376 | tf_op jit(solution)/shard_map/ppermute | solution.py:45
  10.4 7.0 %collective-permute-start.2 = (f16[2,18,16,128]{3,2,1,0:T(8,128)(2,1)S(1)}, f16[2,18,16,128]{3,2,1,0:T(8,128)(2,1)S(1)}, u32[]{:S(2)}, u32[]{:S(2)}) collective-permute-start(f16[2,18,16,128]{3,2,1,0:T(8,128)(2,1)S(1)} %multiply_convert_fusion.3), channel_id=1, source_target_pairs={{0,2},{2,0},{4,6},{6,4},{8,10},{10,8},{12,14},{14,12},{16,18},{18,... | collective-permute-start | bytes 442376 | tf_op jit(solution)/shard_map/ppermute | solution.py:45
  17.5 4.6 %collective-permute-start.5 = (f16[14,16,128]{2,1,0:T(8,128)(2,1)S(1)}, f16[14,16,128]{2,1,0:T(8,128)(2,1)S(1)}, u32[]{:S(2)}, u32[]{:S(2)}) collective-permute-start(f16[14,16,128]{2,1,0:T(8,128)(2,1)S(1)} %multiply_convert_fusion.8), channel_id=1, source_target_pairs={{0,8},{2,10},{4,12},{6,14},{8,0},{10,2},{12,4},{14,6},{16,24},{18,... | collective-permute-start | bytes 172040 | tf_op jit(solution)/shard_map/ppermute | solution.py:45
  19.2 8.0 %collective-permute-start.8 = (f16[16,16,128]{2,1,0:T(8,128)(2,1)S(1)}, f16[16,16,128]{2,1,0:T(8,128)(2,1)S(1)}, u32[]{:S(2)}, u32[]{:S(2)}) collective-permute-start(f16[16,16,128]{2,1,0:T(8,128)(2,1)S(1)} %get-tuple-element.39), channel_id=1, source_target_pairs={{0,16},{2,18},{4,20},{6,22},{8,24},{10,26},{12,28},{14,30},{16,0},... | collective-permute-start | bytes 196616 | tf_op jit(solution)/shard_map/ppermute | solution.py:45
  21.9 6.5 %collective-permute-start.9 = (f16[16,16,128]{2,1,0:T(8,128)(2,1)S(1)}, f16[16,16,128]{2,1,0:T(8,128)(2,1)S(1)}, u32[]{:S(2)}, u32[]{:S(2)}) collective-permute-start(f16[16,16,128]{2,1,0:T(8,128)(2,1)S(1)} %get-tuple-element.38), channel_id=1, source_target_pairs={{0,24},{2,26},{4,28},{6,30},{8,16},{10,18},{12,20},{14,22},{16,8},... | collective-permute-start | bytes 196616 | tf_op jit(solution)/shard_map/ppermute | solution.py:45
  22.1 8.4 %collective-permute-start.6 = (f16[14,16,128]{2,1,0:T(8,128)(2,1)S(1)}, f16[14,16,128]{2,1,0:T(8,128)(2,1)S(1)}, u32[]{:S(2)}, u32[]{:S(2)}) collective-permute-start(f16[14,16,128]{2,1,0:T(8,128)(2,1)S(1)} %multiply_convert_fusion.7), channel_id=1, source_target_pairs={{0,16},{2,18},{4,20},{6,22},{8,24},{10,26},{12,28},{14,30},{16,0},... | collective-permute-start | bytes 172040 | tf_op jit(solution)/shard_map/ppermute | solution.py:45
  24.8 5.8 %collective-permute-start.7 = (f16[16,16,128]{2,1,0:T(8,128)(2,1)S(1)}, f16[16,16,128]{2,1,0:T(8,128)(2,1)S(1)}, u32[]{:S(2)}, u32[]{:S(2)}) collective-permute-start(f16[16,16,128]{2,1,0:T(8,128)(2,1)S(1)} %get-tuple-element.38), channel_id=1, source_target_pairs={{0,8},{2,10},{4,12},{6,14},{8,0},{10,2},{12,4},{14,6},{16,24},{18,... | collective-permute-start | bytes 196616 | tf_op jit(solution)/shard_map/ppermute | solution.py:45
